TPU v7x, 32 devices: a whole 2x2x4 slice. The times are simulated.
32 devices in a mesh: region: 2 (over x), tm: 8 (over z, y), tile: 2 (over core).
Axes of the slice: x: 2, y: 2, z: 4, core: 2. Of those that a mesh axis runs over, the one named last changes fastest.
Arguments:
- coords: float32 [3, 65536], P(None, ('region', 'tm', 'tile')), parts along dimension 1, may hold values from 0 to 16, as said below
- anomalies: float32 [65536, 128], P(('region', 'tm', 'tile')), parts along dimension 0, may hold values from -6 to 6
- noise_var: float32 [65536], P(('region', 'tm', 'tile')), parts along dimension 0, may hold values from 0.3 to 3
Outputs:
- weights: float32 [65536, 128], P(('region', 'tm', 'tile')), parts along dimension 0
- residual: float32 [65536, 128], P(('region', 'tm', 'tile')), parts along dimension 0
There are 2 independent parts, one for each index of `region`. A program takes and returns all parts, laid end to end along the dimension named above; each array names one. Nothing has to cross between parts.
Inputs may be any that keep to these rules, and one draw needn't show every extreme that they name: `coords`: row 0 holds times in units of the kernel's time support, rising along the observations; observations k * 4096 to (k + 1) * 4096 - 1 have times in [k, k + 1). Rows 1 and 2 are positions in units of the spatial support.
All inputs are finite; a program needn't handle non-finite values.
Results may differ from a plain program's by a relative error of at most 0.0003.
Values sent between devices are 32-bit elements; how exact they have to be, the bound alone decides.
No kernel may reach another device: no remote copies, remote signals or barrier semaphores. Data moves between devices by JAX's collectives and lax.ppermute only.
A program may use at most 64 MiB of HBM per device.

v0:
```python
import functools

import jax
import jax.numpy as jnp
from jax import lax
from jax.experimental import pallas as pl
from jax.experimental.pallas import tpu as pltpu
from jax.sharding import PartitionSpec as P

LANES = 128
ROWS = 224
SLOTS = 72
UNROLL = 4
CHUNKS = 2
FAR = 1.0e6
F32 = jnp.float32
BF16 = jnp.bfloat16
MIB = 1 << 20


def vmem_spec():
    return pl.BlockSpec(memory_space=pltpu.VMEM)


def smem_spec():
    return pl.BlockSpec(memory_space=pltpu.SMEM)


def split2(value):
    high = value.astype(BF16)
    low = (value - high.astype(F32)).astype(BF16)
    return high, low


def list_length(points):
    return 2 * (points // LANES) * -(-points // ROWS) + UNROLL


def sort_kernel(points, coords, noise, values, *refs):
    out_values, (lanes, rows, ranks, xcol, facts, sorted_facts, sorted_values, rank_row, rank_smem, sem) = (
        refs[:CHUNKS],
        refs[CHUNKS:],
    )
    groups = points // LANES
    for g in range(groups):
        here = slice(g * LANES, (g + 1) * LANES)
        xcol[here, :] = jnp.transpose(jnp.broadcast_to(coords[1:2, here], (LANES, LANES)))

    xrow = [jnp.broadcast_to(coords[1:2, g * LANES : (g + 1) * LANES], (8, LANES)) for g in range(groups)]
    lane = lax.broadcasted_iota(jnp.int32, (8, LANES), 1)
    sub = lax.broadcasted_iota(jnp.int32, (8, LANES), 0)
    counts = tuple(jnp.zeros((8, LANES), F32) for _ in range(groups))
    for jg in range(groups):

        def count(step, carry):
            at = pl.multiple_of(jg * LANES + step * 8, 8)
            mine = xcol[pl.ds(at, 8), :]
            out = []
            for ig in range(groups):
                if ig == jg:
                    before = jnp.logical_or(
                        mine < xrow[ig],
                        jnp.logical_and(mine == xrow[ig], sub + step * 8 < lane),
                    )
                elif ig > jg:
                    before = mine <= xrow[ig]
                else:
                    before = mine < xrow[ig]
                out.append(carry[ig] + jnp.where(before, 1.0, 0.0))
            return tuple(out)

        counts = lax.fori_loop(0, LANES // 8, count, counts, unroll=2)
    for g in range(groups):
        rank_row[0:1, g * LANES : (g + 1) * LANES] = jnp.sum(counts[g], axis=0, keepdims=True).astype(jnp.int32)
    ranks[...] = rank_row[...]
    copy = pltpu.make_async_copy(rank_row, rank_smem, sem)
    copy.start()
    blank = jnp.zeros((LANES - 4, LANES), F32)
    for g in range(groups):
        here = slice(g * LANES, (g + 1) * LANES)
        facts[here, :] = jnp.transpose(jnp.concatenate([coords[:, here], noise[:, here], blank], axis=0))
    copy.wait()
    size = points // CHUNKS

    def scatter(step, carry):
        at = pl.multiple_of(step * 8, 8)
        block = values[pl.ds(at, 8), :]
        fact = facts[pl.ds(at, 8), :]
        for k in range(8):
            to = rank_smem[0, at + k]
            sorted_facts[pl.ds(to, 1), :] = fact[k : k + 1, :]
            sorted_values[pl.ds(to, 1), :] = block[k : k + 1, :]
        return carry

    lax.fori_loop(0, points // 8, scatter, 0, unroll=4)
    for c in range(CHUNKS):
        out_values[c][...] = sorted_values[c * size : (c + 1) * size, :]
    for g in range(groups):
        here = slice(g * LANES, (g + 1) * LANES)
        got = sorted_facts[here, :]
        lanes[0:4, here] = jnp.transpose(got)[0:4, :]
        for k in range(4):
            scale = 4.0 if k < 3 else 1.0
            rows[k, here, :] = jnp.broadcast_to(got[:, k : k + 1] * scale, (LANES, LANES))
    for k in range(4):
        rows[k, points:, :] = jnp.full((ROWS, LANES), FAR if k < 3 else 0.0, F32)
    lanes[4:5, :] = jnp.full((1, points), jnp.min(coords[0:1, :]), F32)
    lanes[5:6, :] = jnp.full((1, points), jnp.max(coords[0:1, :]), F32)
    lanes[6:8, :] = jnp.ones((2, points), F32)


def sort_points(coords, noise, values):
    points, width = values.shape
    out = pl.pallas_call(
        functools.partial(sort_kernel, points),
        out_shape=tuple(jax.ShapeDtypeStruct((points // CHUNKS, width), F32) for _ in range(CHUNKS))
        + (
            jax.ShapeDtypeStruct((8, points), F32),
            pltpu.VMEM((4, points + ROWS, LANES), F32),
            jax.ShapeDtypeStruct((1, points), jnp.int32),
        ),
        in_specs=[vmem_spec()] * 3,
        out_specs=[vmem_spec()] * (CHUNKS + 3),
        scratch_shapes=[
            pltpu.VMEM((points, LANES), F32),
            pltpu.VMEM((points, LANES), F32),
            pltpu.VMEM((points, LANES), F32),
            pltpu.VMEM((points, LANES), F32),
            pltpu.VMEM((1, points), jnp.int32),
            pltpu.SMEM((1, points), jnp.int32),
            pltpu.SemaphoreType.DMA,
        ],
        compiler_params=pltpu.CompilerParams(vmem_limit_bytes=16 * MIB),
        name="sort_points",
    )(coords, noise, values)
    return out[:CHUNKS], *out[CHUNKS:]


def tile_values(rows, cols, at, count):
    span = pl.ds(at, count)
    dtime = jnp.abs(rows[0, span, :] - cols[0])
    dx = rows[1, span, :] - cols[1]
    dy = rows[2, span, :] - cols[2]
    square = jnp.maximum(dx * dx + dy * dy, 1e-30)
    dist = square * lax.rsqrt(square)
    near = jnp.maximum(4.0 - dtime, 0.0) * jnp.maximum(4.0 - dist, 0.0)
    near = near * near
    return near * near * ((dtime + 1.0) * (dist + 1.0))


def fill_tile(tile, rows, facts, at):
    cols = [jnp.broadcast_to(facts[k : k + 1, :] * 4.0, (16, LANES)) for k in range(3)]
    for part in range(ROWS // 16):
        start = pl.multiple_of(at + part * 16, 16)
        high, low = split2(tile_values(rows, cols, start, 16))
        tile[part * 16 : (part + 1) * 16, 0:LANES] = high
        tile[part * 16 : (part + 1) * 16, LANES:] = low


def find_ranges(points, own, lanes, table, base):
    windows = points // LANES
    x = jnp.concatenate([lanes[1:2, g * LANES : (g + 1) * LANES] for g in range(windows)], axis=0)
    low = jnp.broadcast_to(x[:, 0:1], (windows, LANES))
    high = jnp.broadcast_to(x[:, LANES - 1 : LANES], (windows, LANES))
    begin = jnp.zeros((windows, LANES), F32)
    beyond = jnp.zeros((windows, LANES), F32)
    for g in range(windows):
        row = jnp.broadcast_to(own[1:2, g * LANES : (g + 1) * LANES], (windows, LANES))
        begin = begin + jnp.where(low - row >= 1.0, 1.0, 0.0)
        beyond = beyond + jnp.where(row - high >= 1.0, 1.0, 0.0)
    begin = jnp.sum(begin, axis=1, keepdims=True)
    end = points - jnp.sum(beyond, axis=1, keepdims=True)
    first = begin.astype(jnp.int32) // 16 * 16
    length = end - first.astype(F32)
    blocks = jnp.zeros((windows, 1), F32)
    for k in range(-(-points // ROWS)):
        blocks = blocks + jnp.where(length > float(k * ROWS), 1.0, 0.0)
    apart = jnp.maximum(lanes[4:5, 0:1] - own[5:6, 0:1], own[4:5, 0:1] - lanes[5:6, 0:1])
    apart = jnp.where(lanes[6:7, 0:1] > 0.5, apart, 2.0)
    blocks = jnp.where(jnp.logical_and(end > begin, jnp.broadcast_to(apart, (windows, 1)) < 1.0), blocks, 0.0)
    table[base : base + windows, 0:LANES] = jnp.broadcast_to(first, (windows, LANES))
    table[base : base + windows, LANES:] = jnp.broadcast_to(blocks.astype(jnp.int32), (windows, LANES))


def eval_kernel(points, own, lanes_a, lanes_b, rows, cache, work, facts, table, table_smem, sem):
    windows = points // LANES
    for half, lanes in enumerate((lanes_a, lanes_b)):
        find_ranges(points, own, lanes, table, half * windows)
    copy = pltpu.make_async_copy(table, table_smem, sem)
    copy.start()
    for half, lanes in enumerate((lanes_a, lanes_b)):
        for g in range(windows):
            facts[half * windows + g] = lanes[:, g * LANES : (g + 1) * LANES]
    copy.wait()

    def window(w, slot):
        first = table_smem[w, 0]
        blocks = table_smem[w, LANES]

        def block(b, carry):
            work[0, slot + b] = first + b * ROWS
            work[1, slot + b] = w
            return carry

        lax.fori_loop(0, blocks, block, 0)
        return slot + blocks

    total = lax.fori_loop(0, 2 * windows, window, 0)
    for k in range(UNROLL):
        work[0, total + k] = points
        work[1, total + k] = 0
    work[2, 0] = total

    def slot(s, carry):
        fill_tile(cache.at[s], rows, facts[work[1, s]], pl.multiple_of(work[0, s], 16))
        return carry

    lax.fori_loop(0, jnp.minimum(total, SLOTS), slot, 0)


def eval_pair(own, lanes, rows):
    points = own.shape[1]
    windows = points // LANES
    return pl.pallas_call(
        functools.partial(eval_kernel, points),
        out_shape=(
            pltpu.VMEM((SLOTS, ROWS, 2 * LANES), BF16),
            jax.ShapeDtypeStruct((3, list_length(points)), jnp.int32),
        ),
        in_specs=[vmem_spec()] * 4,
        out_specs=(vmem_spec(), smem_spec()),
        scratch_shapes=[
            pltpu.VMEM((2 * windows, 8, LANES), F32),
            pltpu.VMEM((2 * windows, 2 * LANES), jnp.int32),
            pltpu.SMEM((2 * windows, 2 * LANES), jnp.int32),
            pltpu.SemaphoreType.DMA,
        ],
        compiler_params=pltpu.CompilerParams(vmem_limit_bytes=4 * MIB),
        cost_estimate=pl.CostEstimate(flops=6_000_000_000, bytes_accessed=200_000, transcendentals=0),
        name="eval_pair",
    )(own, *lanes, rows)


def product_kernel(points, start, extra, work, lanes_a, lanes_b, rows, cache, *refs):
    values, refs = refs[: 2 * CHUNKS], refs[2 * CHUNKS :]
    before, refs = refs[: 0 if start else CHUNKS], refs[0 if start else CHUNKS :]
    inputs, refs = refs[: extra[1]], refs[extra[1] :]
    out, refs = refs[:CHUNKS], refs[CHUNKS:]
    sums, refs = refs[: extra[2]], refs[extra[2] :]
    acc, pairs, tile = refs
    windows = points // LANES
    size = points // CHUNKS
    per_chunk = size // LANES
    total = work[2, 0]
    acc[...] = jnp.zeros_like(acc)

    @pl.when(total > 0)
    def _():
        for piece in range(2 * CHUNKS):

            def split(w, carry):
                high, low = split2(values[piece][pl.ds(pl.multiple_of(w * LANES, LANES), LANES), :])
                both = jnp.concatenate([high, low], axis=1)
                pairs[piece * per_chunk + w, 0:LANES, :] = both
                pairs[piece * per_chunk + w, LANES:, :] = both
                return carry

            lax.fori_loop(0, per_chunk, split, 0)

        def slots(step, carry):
            for k in range(UNROLL):
                s = step * UNROLL + k
                at = pl.multiple_of(work[0, s], 16)
                acc[pl.ds(at, ROWS), :] += jnp.dot(
                    cache[s], pairs[work[1, s]], preferred_element_type=F32
                )
            return carry

        kept = jnp.minimum(total, SLOTS)
        lax.fori_loop(0, (kept + UNROLL - 1) // UNROLL, slots, 0)

        def again(s, carry):
            at = pl.multiple_of(work[0, s], 16)
            w = work[1, s]
            offset = pl.multiple_of(lax.rem(w, windows) * LANES, LANES)
            in_first = w < windows
            facts = jnp.where(in_first, lanes_a[:, pl.ds(offset, LANES)], lanes_b[:, pl.ds(offset, LANES)])
            fill_tile(tile, rows, facts, at)
            acc[pl.ds(at, ROWS), :] += jnp.dot(tile[...], pairs[w], preferred_element_type=F32)
            return carry

        lax.fori_loop(SLOTS, total, again, 0)

    marks = [jnp.zeros((8, LANES), F32)] * 2
    for c in range(CHUNKS):
        here = slice(c * size, (c + 1) * size)
        image = (acc[here, 0:LANES] + acc[here, LANES:]) * (2.0**-16)
        if start:
            image = image + rows[3, here, :] * values[c][...]
        else:
            image = image + before[c][...]
        out[c][...] = image
        if extra[0] is not None:
            marks = extra[0](c, image, inputs, marks)
    if extra[2]:
        sums[0][...] = jnp.zeros((8, LANES), F32)
        for k in range(2):
            sums[0][k : k + 1, :] = jnp.sum(marks[k], axis=0, keepdims=True)


def fold(value):
    return jnp.sum(value.reshape(value.shape[0] // 8, 8, LANES), axis=0)


def first_marks(c, image, inputs, marks):
    given = inputs[c][...]
    return [marks[0] + fold(given * given), marks[1] + fold(given * image)]


def second_marks(c, image, inputs, marks):
    given, once, scalars = inputs[c][...], inputs[CHUNKS + c][...], inputs[2 * CHUNKS]
    alpha, more = scalars[0:1, :], 1.0 + scalars[1:2, :]
    direction = more * given - alpha * once
    turned = more * once - alpha * image
    return [marks[0] + fold(direction * turned), marks[1]]


def product_pair(work, lanes, rows, cache, values, before, marks=None, inputs=()):
    points = lanes[0].shape[1]
    windows = points // LANES
    start = before is None
    before = () if start else before
    operands = (*lanes, rows, cache, *values[0], *values[1], *before, *inputs)
    has_sums = marks is not None
    out = pl.pallas_call(
        functools.partial(product_kernel, points, start, (marks, len(inputs), int(has_sums))),
        out_shape=[jax.ShapeDtypeStruct((points // CHUNKS, LANES), F32)] * CHUNKS
        + [jax.ShapeDtypeStruct((8, LANES), F32)] * has_sums,
        in_specs=[smem_spec()] + [vmem_spec()] * len(operands),
        out_specs=[vmem_spec()] * (CHUNKS + has_sums),
        scratch_shapes=[
            pltpu.VMEM((points + ROWS, 2 * LANES), F32),
            pltpu.VMEM((2 * windows, 2 * LANES, 2 * LANES), BF16),
            pltpu.VMEM((ROWS, 2 * LANES), BF16),
        ],
        compiler_params=pltpu.CompilerParams(vmem_limit_bytes=18 * MIB),
        cost_estimate=pl.CostEstimate(flops=4_000_000_000, bytes_accessed=4_000_000, transcendentals=0),
        name="product_pair",
    )(work, *operands)
    return (tuple(out[:CHUNKS]), out[CHUNKS]) if has_sums else tuple(out)


def unsort_kernel(points, ranks, *refs):
    source, (out, stage) = refs[:CHUNKS], refs[CHUNKS:]
    size = points // CHUNKS
    for c in range(CHUNKS):
        stage[c * size : (c + 1) * size, :] = source[c][...]

    def gather(step, carry):
        at = pl.multiple_of(step * 8, 8)
        out[pl.ds(at, 8), :] = jnp.concatenate(
            [stage[pl.ds(ranks[0, at + k], 1), :] for k in range(8)], axis=0
        )
        return carry

    lax.fori_loop(0, points // 8, gather, 0, unroll=4)


def unsort(ranks, source):
    points = ranks.shape[1]
    return pl.pallas_call(
        functools.partial(unsort_kernel, points),
        out_shape=jax.ShapeDtypeStruct((points, LANES), F32),
        in_specs=[smem_spec()] + [vmem_spec()] * CHUNKS,
        out_specs=vmem_spec(),
        scratch_shapes=[pltpu.VMEM((points, LANES), F32)],
        compiler_params=pltpu.CompilerParams(vmem_limit_bytes=8 * MIB),
        cost_estimate=pl.CostEstimate(flops=3_000_000_000, bytes_accessed=2_000_000, transcendentals=0),
        name="unsort",
    )(ranks, *source)


def pair_swap(block):
    count = lax.axis_size("tm")
    return lax.ppermute(block, "tm", [(i, i ^ 1) for i in range(count)])


def pair_shift(block):
    count = lax.axis_size("tm")
    route = []
    for i in range(count):
        source = i - 2 if i % 2 == 0 else i + 2
        if 0 <= source < count:
            route.append((source, i))
    return lax.ppermute(block, "tm", route)


def core_swap(block):
    count = lax.axis_size("tile")
    return lax.ppermute(block, "tile", [(i, i ^ 1) for i in range(count)])


def gather_pairs(chunks):
    near = tuple(pair_swap(c) for c in chunks)
    partner = tuple(core_swap(c) for c in chunks)
    far = tuple(pair_shift(c) for c in near)
    near_partner = tuple(core_swap(c) for c in near)
    far_partner = tuple(core_swap(c) for c in far)
    return (chunks, partner), (near, near_partner), (far, far_partner)


def gather_small(block):
    tms, tiles = lax.axis_size("tm"), lax.axis_size("tile")

    def fetch(offset, flip):
        route = []
        for t in range(tms):
            source = offset(t)
            if 0 <= source < tms:
                for c in range(tiles):
                    route.append((source * tiles + (c ^ flip), t * tiles + c))
        return lax.ppermute(block, ("tm", "tile"), route)

    near = lambda t: t ^ 1
    far = lambda t: t - 1 if t % 2 == 0 else t + 1
    return (block, fetch(lambda t: t, 1)), (fetch(near, 0), fetch(near, 1)), (fetch(far, 0), fetch(far, 1))


def total(value):
    count = lax.axis_size("tm")
    value = value + core_swap(value)
    step = 1
    while step < count:
        value = value + lax.ppermute(value, "tm", [(i, i ^ step) for i in range(count)])
        step *= 2
    return value


def local(coords, anomalies, noise_var):
    given, lanes, rows, ranks = sort_points(coords, noise_var[None, :], anomalies)
    lane_pairs = gather_small(lanes)
    value_pairs = gather_pairs(given)
    evals = [eval_pair(lanes, pair, rows) for pair in lane_pairs]

    def apply(values, marks, inputs):
        image = None
        for k in range(3):
            last = dict(marks=marks, inputs=inputs) if k == 2 else {}
            image = product_pair(evals[k][1], lane_pairs[k], rows, evals[k][0], values[k], image, **last)
        return image

    once, sums = apply(value_pairs, first_marks, given)
    once_pairs = gather_pairs(once)
    image0 = unsort(ranks, once)
    sums = total(sums)
    rr0 = sums[0:1]
    alpha0 = rr0 / sums[1:2]
    squares = sum(jnp.sum(jnp.square(g - alpha0 * o), axis=0, keepdims=True) for g, o in zip(given, once))
    rr1 = total(jnp.broadcast_to(squares, (8, LANES)))[0:1]
    beta = rr1 / rr0
    scalars = jnp.concatenate([alpha0, beta, jnp.zeros((6, LANES), F32)], axis=0)
    twice, curve = apply(once_pairs, second_marks, (*given, *once, scalars))
    image1 = unsort(ranks, twice)
    alpha1 = rr1 / total(curve)[0:1]
    weights = (alpha0 + alpha1 * (1.0 + beta)) * anomalies - (alpha1 * alpha0) * image0
    turned = (1.0 + beta) * image0 - alpha0 * image1
    return weights, (anomalies - alpha0 * image0) - alpha1 * turned


def solution(mesh):
    placed = (
        P(None, ("region", "tm", "tile")),
        P(("region", "tm", "tile"), None),
        P(("region", "tm", "tile")),
    )
    return jax.shard_map(
        local,
        mesh=mesh,
        in_specs=placed,
        out_specs=(P(("region", "tm", "tile"), None), P(("region", "tm", "tile"), None)),
        check_vma=False,
    )
```

profile of v0, /device:TPU:0, one launch (start us, length us, event | category | flops | bytes accessed | tf_op | source)
XLA Modules:
  0.0 186.9 jit_solution(7145657437434477271)
XLA Ops:
  3.3 8.2 %sort_points.1 = (f32[1024,128]{1,0:T(8,128)S(1)}, f32[1024,128]{1,0:T(8,128)S(1)}, f32[8,2048]{1,0:T(8,128)S(1)}, f32[4,2272,128]{2,1,0:T(8,128)S(1)}, s32[1,2048]{1,0:T(1,128)S(1)}) custom-call(f32[3,2048]{1,0:T(4,128)S(1)} %copy-done.4, f32[1,2048]{1,0:T(1,128)S(1)} %bitcast.12, f32[2048,128]{1,0:T(8,128)S(1)} %copy-done.2), custom_call_target="tpu_custom_call" | custom-call | tf_op jit(solution)/shard_map/sort_points/pallas_call | solution.py:114
  12.0 2.6 %collective-permute-start.8 = (f32[8,2048]{1,0:T(8,128)S(1)}, f32[8,2048]{1,0:T(8,128)S(1)}, u32[]{:S(2)}, u32[]{:S(2)}) collective-permute-start(f32[8,2048]{1,0:T(8,128)S(1)} %get-tuple-element.27.own.lanes_a), channel_id=1, source_target_pairs={{2,0},{3,1},{0,2},{1,3},{6,4},{7,5},{4,6},{5,7},{10,8},{11,9},{8,1... | collective-permute-start | bytes 196616 | tf_op jit(solution)/shard_map/ppermute | solution.py:422
  17.4 9.8 %eval_pair.5 = (bf16[72,224,256]{2,1,0:T(8,128)(2,1)S(1)}, s32[3,324]{1,0:T(4,128)S(1)}) custom-call(f32[8,2048]{1,0:T(8,128)S(1)} %get-tuple-element.27.own.lanes_a, f32[8,2048]{1,0:T(8,128)S(1)} %get-tuple-element.27.own.lanes_a, f32[8,2048]{1,0:T(8,128)S(1)} %collective-permute-done.12.lanes_b, f32[4,2272,128]{2,1,0:T(8,128)S(1)} %get-tuple-element.28.rows), custom_call_target="tpu_custom_call" | custom-call | flops 6000000000 | bytes 200000 | tf_op jit(solution)/shard_map/eval_pair/pallas_call | solution.py:224
  27.9 5.6 %collective-permute-start.4 = (f32[1024,128]{1,0:T(8,128)S(1)}, f32[1024,128]{1,0:T(8,128)S(1)}, u32[]{:S(2)}, u32[]{:S(2)}) collective-permute-start(f32[1024,128]{1,0:T(8,128)S(1)} %get-tuple-element.32.refs_1_.refs_7_), channel_id=1, source_target_pairs={{0,2},{2,0},{4,6},{6,4},{8,10},{10,8},{12,14},{14,12},{1,3},{3,1},... | collective-permute-start | bytes 1572872 | tf_op jit(solution)/shard_map/ppermute | solution.py:385
  33.5 6.2 %eval_pair.4 = (bf16[72,224,256]{2,1,0:T(8,128)(2,1)S(1)}, s32[3,324]{1,0:T(4,128)S(1)}) custom-call(f32[8,2048]{1,0:T(8,128)S(1)} %get-tuple-element.27.own.lanes_a, f32[8,2048]{1,0:T(8,128)S(1)} %collective-permute-done.8.lanes_a, f32[8,2048]{1,0:T(8,128)S(1)} %collective-permute-done.9.lanes_b, f32[4,2272,128]{2,1,0:T(8,128)S(1)} %get-tuple-element.28.rows), custom_call_target="tpu_custom_call" | custom-call | flops 6000000000 | bytes 200000 | tf_op jit(solution)/shard_map/eval_pair/pallas_call | solution.py:224
  39.7 3.3 %collective-permute-start.14 = (f32[1024,128]{1,0:T(8,128)S(1)}, f32[1024,128]{1,0:T(8,128)S(1)}, u32[]{:S(2)}, u32[]{:S(2)}) collective-permute-start(f32[1024,128]{1,0:T(8,128)S(1)} %get-tuple-element.32.refs_1_.refs_7_), channel_id=1, source_target_pairs={{0,1},{1,0},{2,3},{3,2},{4,5},{5,4},{6,7},{7,6},{8,9},{9,8},{10,11... | collective-permute-start | bytes 1572872 | tf_op jit(solution)/shard_map/ppermute | solution.py:400
  43.1 4.1 %collective-permute-start.3 = (f32[1024,128]{1,0:T(8,128)S(1)}, f32[1024,128]{1,0:T(8,128)S(1)}, u32[]{:S(2)}, u32[]{:S(2)}) collective-permute-start(f32[1024,128]{1,0:T(8,128)S(1)} %collective-permute-done.2.refs_0_), channel_id=1, source_target_pairs={{6,2},{0,4},{10,6},{4,8},{14,10},{8,12},{7,3},{1,5},{11,7},{5,9},{... | collective-permute-start | bytes 1572872 | tf_op jit(solution)/shard_map/ppermute | solution.py:395
  47.5 3.5 %collective-permute-start.5 = (f32[1024,128]{1,0:T(8,128)S(1)}, f32[1024,128]{1,0:T(8,128)S(1)}, u32[]{:S(2)}, u32[]{:S(2)}) collective-permute-start(f32[1024,128]{1,0:T(8,128)S(1)} %collective-permute-done.4.refs_1_), channel_id=1, source_target_pairs={{6,2},{0,4},{10,6},{4,8},{14,10},{8,12},{7,3},{1,5},{11,7},{5,9},{... | collective-permute-start | bytes 1572872 | tf_op jit(solution)/shard_map/ppermute | solution.py:395
  51.0 2.6 %eval_pair.3 = (bf16[72,224,256]{2,1,0:T(8,128)(2,1)S(1)}, s32[3,324]{1,0:T(4,128)S(1)}) custom-call(f32[8,2048]{1,0:T(8,128)S(1)} %get-tuple-element.27.own.lanes_a, f32[8,2048]{1,0:T(8,128)S(1)} %collective-permute-done.lanes_a, f32[8,2048]{1,0:T(8,128)S(1)} %collective-permute-done.1.lanes_b, f32[4,2272,128]{2,1,0:T(8,128)S(1)} %get-tuple-element.28.rows), custom_call_target="tpu_custom_call" | custom-call | flops 6000000000 | bytes 200000 | tf_op jit(solution)/shard_map/eval_pair/pallas_call | solution.py:224
  53.6 3.2 %copy-done = bf16[72,224,256]{2,1,0:T(8,128)(2,1)} copy-done((bf16[72,224,256]{2,1,0:T(8,128)(2,1)}, bf16[72,224,256]{2,1,0:T(8,128)(2,1)S(1)}, u32[]{:S(2)}) %copy-start) | copy-done | bytes 8257560
  56.8 2.6 %collective-permute-done.3.refs_0_ = f32[1024,128]{1,0:T(8,128)S(1)} collective-permute-done((f32[1024,128]{1,0:T(8,128)S(1)}, f32[1024,128]{1,0:T(8,128)S(1)}, u32[]{:S(2)}, u32[]{:S(2)}) %collective-permute-start.3) | collective-permute-done | bytes 524320 | tf_op jit(solution)/shard_map/ppermute | solution.py:395
  59.4 10.8 %collective-permute-done.5.refs_1_ = f32[1024,128]{1,0:T(8,128)S(1)} collective-permute-done((f32[1024,128]{1,0:T(8,128)S(1)}, f32[1024,128]{1,0:T(8,128)S(1)}, u32[]{:S(2)}, u32[]{:S(2)}) %collective-permute-start.5) | collective-permute-done | bytes 524320 | tf_op jit(solution)/shard_map/ppermute | solution.py:395
  70.2 6.3 %product_pair.6 = (f32[1024,128]{1,0:T(8,128)S(1)}, f32[1024,128]{1,0:T(8,128)S(1)}) custom-call(s32[3,324]{1,0:T(4,128)S(1)} %get-tuple-element.35.work, f32[8,2048]{1,0:T(8,128)S(1)} %get-tuple-element.27.own.lanes_a, f32[8,2048]{1,0:T(8,128)S(1)} %collective-permute-done.12.lanes_b, f32[4,2272,128]{2,1,0:T(8,128)S(1)} %get-tuple-element.28.rows, ...), custom_call_target="tpu_custom_call" | custom-call | flops 4000000000 | bytes 4000000 | tf_op jit(solution)/shard_map/product_pair/pallas_call | solution.py:335
  76.6 3.9 %product_pair.7 = (f32[1024,128]{1,0:T(8,128)S(1)}, f32[1024,128]{1,0:T(8,128)S(1)}) custom-call(s32[3,324]{1,0:T(4,128)S(1)} %get-tuple-element.33.work, f32[8,2048]{1,0:T(8,128)S(1)} %collective-permute-done.8.lanes_a, f32[8,2048]{1,0:T(8,128)S(1)} %collective-permute-done.9.lanes_b, f32[4,2272,128]{2,1,0:T(8,128)S(1)} %get-tuple-element.28.rows, ...), custom_call_target="tpu_custom_call" | custom-call | flops 4000000000 | bytes 4000000 | tf_op jit(solution)/shard_map/product_pair/pallas_call | solution.py:335
  80.5 3.3 %copy-done.1 = bf16[72,224,256]{2,1,0:T(8,128)(2,1)S(1)} copy-done((bf16[72,224,256]{2,1,0:T(8,128)(2,1)S(1)}, bf16[72,224,256]{2,1,0:T(8,128)(2,1)}, u32[]{:S(2)}) %copy-start.1) | copy-done | bytes 8257560
  84.9 3.0 %collective-permute-start.15 = (f32[8,128]{1,0:T(8,128)S(1)}, f32[8,128]{1,0:T(8,128)S(1)}, u32[]{:S(2)}, u32[]{:S(2)}) collective-permute-start(f32[8,128]{1,0:T(8,128)S(1)} %get-tuple-element.41), channel_id=1, source_target_pairs={{0,1},{1,0},{2,3},{3,2},{4,5},{5,4},{6,7},{7,6},{8,9},{9,8},{10,11... | collective-permute-start | bytes 12296 | tf_op jit(solution)/shard_map/ppermute | solution.py:400
  88.8 4.6 %collective-permute-start.16 = (f32[8,128]{1,0:T(8,128)S(1)}, f32[8,128]{1,0:T(8,128)S(1)}, u32[]{:S(2)}, u32[]{:S(2)}) collective-permute-start(f32[8,128]{1,0:T(8,128)S(1)} %add.51), channel_id=1, source_target_pairs={{0,2},{2,0},{4,6},{6,4},{8,10},{10,8},{12,14},{14,12},{1,3},{3,1},... | collective-permute-start | bytes 12296 | tf_op jit(solution)/shard_map/ppermute | solution.py:434
  95.0 2.8 %collective-permute-start.17 = (f32[8,128]{1,0:T(8,128)S(1)}, f32[8,128]{1,0:T(8,128)S(1)}, u32[]{:S(2)}, u32[]{:S(2)}) collective-permute-start(f32[8,128]{1,0:T(8,128)S(1)} %add.52), channel_id=1, source_target_pairs={{0,4},{2,6},{4,0},{6,2},{8,12},{10,14},{12,8},{14,10},{1,5},{3,7},... | collective-permute-start | bytes 12296 | tf_op jit(solution)/shard_map/ppermute | solution.py:434
  99.4 3.0 %collective-permute-start.18 = (f32[8,128]{1,0:T(8,128)S(1)}, f32[8,128]{1,0:T(8,128)S(1)}, u32[]{:S(2)}, u32[]{:S(2)}) collective-permute-start(f32[8,128]{1,0:T(8,128)S(1)} %add.53), channel_id=1, source_target_pairs={{0,8},{2,10},{4,12},{6,14},{8,0},{10,2},{12,4},{14,6},{1,9},{3,11}... | collective-permute-start | bytes 12296 | tf_op jit(solution)/shard_map/ppermute | solution.py:434
  106.8 18.5 %collective-permute-done.20 = f32[8,128]{1,0:T(8,128)S(1)} collective-permute-done((f32[8,128]{1,0:T(8,128)S(1)}, f32[8,128]{1,0:T(8,128)S(1)}, u32[]{:S(2)}, u32[]{:S(2)}) %collective-permute-start.20) | collective-permute-done | bytes 4128 | tf_op jit(solution)/shard_map/ppermute | solution.py:434
  126.8 2.2 %collective-permute-done.21 = f32[8,128]{1,0:T(8,128)S(1)} collective-permute-done((f32[8,128]{1,0:T(8,128)S(1)}, f32[8,128]{1,0:T(8,128)S(1)}, u32[]{:S(2)}, u32[]{:S(2)}) %collective-permute-start.21) | collective-permute-done | bytes 4128 | tf_op jit(solution)/shard_map/ppermute | solution.py:434
  129.2 3.6 %collective-permute-start.24 = (f32[1024,128]{1,0:T(8,128)S(1)}, f32[1024,128]{1,0:T(8,128)S(1)}, u32[]{:S(2)}, u32[]{:S(2)}) collective-permute-start(f32[1024,128]{1,0:T(8,128)S(1)} %collective-permute-done.23.refs_0_), channel_id=1, source_target_pairs={{6,2},{0,4},{10,6},{4,8},{14,10},{8,12},{7,3},{1,5},{11,7},{5,9},{... | collective-permute-start | bytes 1572872 | tf_op jit(solution)/shard_map/ppermute | solution.py:395
  132.8 3.5 %collective-permute-start.26 = (f32[1024,128]{1,0:T(8,128)S(1)}, f32[1024,128]{1,0:T(8,128)S(1)}, u32[]{:S(2)}, u32[]{:S(2)}) collective-permute-start(f32[1024,128]{1,0:T(8,128)S(1)} %collective-permute-done.25.refs_1_), channel_id=1, source_target_pairs={{6,2},{0,4},{10,6},{4,8},{14,10},{8,12},{7,3},{1,5},{11,7},{5,9},{... | collective-permute-start | bytes 1572872 | tf_op jit(solution)/shard_map/ppermute | solution.py:395
  137.0 8.1 %collective-permute-done.24.refs_0_ = f32[1024,128]{1,0:T(8,128)S(1)} collective-permute-done((f32[1024,128]{1,0:T(8,128)S(1)}, f32[1024,128]{1,0:T(8,128)S(1)}, u32[]{:S(2)}, u32[]{:S(2)}) %collective-permute-start.24) | collective-permute-done | bytes 524320 | tf_op jit(solution)/shard_map/ppermute | solution.py:395
  145.1 7.4 %collective-permute-done.26.refs_1_ = f32[1024,128]{1,0:T(8,128)S(1)} collective-permute-done((f32[1024,128]{1,0:T(8,128)S(1)}, f32[1024,128]{1,0:T(8,128)S(1)}, u32[]{:S(2)}, u32[]{:S(2)}) %collective-permute-start.26) | collective-permute-done | bytes 524320 | tf_op jit(solution)/shard_map/ppermute | solution.py:395
  152.5 6.3 %product_pair.9 = (f32[1024,128]{1,0:T(8,128)S(1)}, f32[1024,128]{1,0:T(8,128)S(1)}) custom-call(s32[3,324]{1,0:T(4,128)S(1)} %get-tuple-element.35.work, f32[8,2048]{1,0:T(8,128)S(1)} %get-tuple-element.27.own.lanes_a, f32[8,2048]{1,0:T(8,128)S(1)} %collective-permute-done.12.lanes_b, f32[4,2272,128]{2,1,0:T(8,128)S(1)} %get-tuple-element.28.rows, ...), custom_call_target="tpu_custom_call" | custom-call | flops 4000000000 | bytes 4000000 | tf_op jit(solution)/shard_map/product_pair/pallas_call | solution.py:335
  158.9 4.0 %product_pair.10 = (f32[1024,128]{1,0:T(8,128)S(1)}, f32[1024,128]{1,0:T(8,128)S(1)}) custom-call(s32[3,324]{1,0:T(4,128)S(1)} %get-tuple-element.33.work, f32[8,2048]{1,0:T(8,128)S(1)} %collective-permute-done.8.lanes_a, f32[8,2048]{1,0:T(8,128)S(1)} %collective-permute-done.9.lanes_b, f32[4,2272,128]{2,1,0:T(8,128)S(1)} %get-tuple-element.28.rows, ...), custom_call_target="tpu_custom_call" | custom-call | flops 4000000000 | bytes 4000000 | tf_op jit(solution)/shard_map/product_pair/pallas_call | solution.py:335
  164.1 3.0 %collective-permute-start.33 = (f32[8,128]{1,0:T(8,128)S(1)}, f32[8,128]{1,0:T(8,128)S(1)}, u32[]{:S(2)}, u32[]{:S(2)}) collective-permute-start(f32[8,128]{1,0:T(8,128)S(1)} %get-tuple-element.48), channel_id=1, source_target_pairs={{0,1},{1,0},{2,3},{3,2},{4,5},{5,4},{6,7},{7,6},{8,9},{9,8},{10,11... | collective-permute-start | bytes 12296 | tf_op jit(solution)/shard_map/ppermute | solution.py:400
  167.9 6.0 %collective-permute-start.34 = (f32[8,128]{1,0:T(8,128)S(1)}, f32[8,128]{1,0:T(8,128)S(1)}, u32[]{:S(2)}, u32[]{:S(2)}) collective-permute-start(f32[8,128]{1,0:T(8,128)S(1)} %add.60), channel_id=1, source_target_pairs={{0,2},{2,0},{4,6},{6,4},{8,10},{10,8},{12,14},{14,12},{1,3},{3,1},... | collective-permute-start | bytes 12296 | tf_op jit(solution)/shard_map/ppermute | solution.py:434
  177.0 2.7 %unsort.2 = f32[2048,128]{1,0:T(8,128)S(1)} custom-call(s32[1,2048]{1,0:T(1,128)S(1)} %get-tuple-element.49.ranks, f32[1024,128]{1,0:T(8,128)S(1)} %get-tuple-element.42.refs_0_.refs_8_, f32[1024,128]{1,0:T(8,128)S(1)} %get-tuple-element.43.refs_1_.refs_9_), custom_call_target="tpu_custom_call" | custom-call | flops 3000000000 | bytes 2000000 | tf_op jit(solution)/shard_map/unsort/pallas_call | solution.py:371
  179.7 2.8 %collective-permute-start.36 = (f32[8,128]{1,0:T(8,128)S(1)}, f32[8,128]{1,0:T(8,128)S(1)}, u32[]{:S(2)}, u32[]{:S(2)}) collective-permute-start(f32[8,128]{1,0:T(8,128)S(1)} %add.62), channel_id=1, source_target_pairs={{0,8},{2,10},{4,12},{6,14},{8,0},{10,2},{12,4},{14,6},{1,9},{3,11}... | collective-permute-start | bytes 12296 | tf_op jit(solution)/shard_map/ppermute | solution.py:434
  182.5 2.7 %unsort.3 = f32[2048,128]{1,0:T(8,128)S(1)} custom-call(s32[1,2048]{1,0:T(1,128)S(1)} %get-tuple-element.49.ranks, f32[1024,128]{1,0:T(8,128)S(1)} %get-tuple-element.50.refs_0_, f32[1024,128]{1,0:T(8,128)S(1)} %get-tuple-element.51.refs_1_), custom_call_target="tpu_custom_call" | custom-call | flops 3000000000 | bytes 2000000 | tf_op jit(solution)/shard_map/unsort/pallas_call | solution.py:371
  (95 shorter events, 25.7 us)
Async XLA Ops:
  11.5 5.3 %collective-permute-start.12 = (f32[8,2048]{1,0:T(8,128)S(1)}, f32[8,2048]{1,0:T(8,128)S(1)}, u32[]{:S(2)}, u32[]{:S(2)}) collective-permute-start(f32[8,2048]{1,0:T(8,128)S(1)} %get-tuple-element.27.own.lanes_a), channel_id=1, source_target_pairs={{1,0},{0,1},{3,2},{2,3},{5,4},{4,5},{7,6},{6,7},{9,8},{8,9},{11,10... | collective-permute-start | bytes 196616 | tf_op jit(solution)/shard_map/ppermute | solution.py:422
  12.0 15.2 %collective-permute-start.8 = (f32[8,2048]{1,0:T(8,128)S(1)}, f32[8,2048]{1,0:T(8,128)S(1)}, u32[]{:S(2)}, u32[]{:S(2)}) collective-permute-start(f32[8,2048]{1,0:T(8,128)S(1)} %get-tuple-element.27.own.lanes_a), channel_id=1, source_target_pairs={{2,0},{3,1},{0,2},{1,3},{6,4},{7,5},{4,6},{5,7},{10,8},{11,9},{8,1... | collective-permute-start | bytes 196616 | tf_op jit(solution)/shard_map/ppermute | solution.py:422
  14.6 13.3 %collective-permute-start.9 = (f32[8,2048]{1,0:T(8,128)S(1)}, f32[8,2048]{1,0:T(8,128)S(1)}, u32[]{:S(2)}, u32[]{:S(2)}) collective-permute-start(f32[8,2048]{1,0:T(8,128)S(1)} %get-tuple-element.27.own.lanes_a), channel_id=1, source_target_pairs={{3,0},{2,1},{1,2},{0,3},{7,4},{6,5},{5,6},{4,7},{11,8},{10,9},{9,1... | collective-permute-start | bytes 196616 | tf_op jit(solution)/shard_map/ppermute | solution.py:422
  14.7 32.8 %collective-permute-start.13 = (f32[1024,128]{1,0:T(8,128)S(1)}, f32[1024,128]{1,0:T(8,128)S(1)}, u32[]{:S(2)}, u32[]{:S(2)}) collective-permute-start(f32[1024,128]{1,0:T(8,128)S(1)} %get-tuple-element.31.refs_0_.refs_6_), channel_id=1, source_target_pairs={{0,1},{1,0},{2,3},{3,2},{4,5},{5,4},{6,7},{7,6},{8,9},{9,8},{10,11... | collective-permute-start | bytes 1572872 | tf_op jit(solution)/shard_map/ppermute | solution.py:400
  14.8 28.2 %collective-permute-start.2 = (f32[1024,128]{1,0:T(8,128)S(1)}, f32[1024,128]{1,0:T(8,128)S(1)}, u32[]{:S(2)}, u32[]{:S(2)}) collective-permute-start(f32[1024,128]{1,0:T(8,128)S(1)} %get-tuple-element.31.refs_0_.refs_6_), channel_id=1, source_target_pairs={{0,2},{2,0},{4,6},{6,4},{8,10},{10,8},{12,14},{14,12},{1,3},{3,1},... | collective-permute-start | bytes 1572872 | tf_op jit(solution)/shard_map/ppermute | solution.py:385
  16.7 23.0 %collective-permute-start = (f32[8,2048]{1,0:T(8,128)S(1)}, f32[8,2048]{1,0:T(8,128)S(1)}, u32[]{:S(2)}, u32[]{:S(2)}) collective-permute-start(f32[8,2048]{1,0:T(8,128)S(1)} %get-tuple-element.27.own.lanes_a), channel_id=1, source_target_pairs={{4,2},{5,3},{2,4},{3,5},{8,6},{9,7},{6,8},{7,9},{12,10},{13,11},{1... | collective-permute-start | bytes 196616 | tf_op jit(solution)/shard_map/ppermute | solution.py:422
  27.2 15.9 %collective-permute-start.1 = (f32[8,2048]{1,0:T(8,128)S(1)}, f32[8,2048]{1,0:T(8,128)S(1)}, u32[]{:S(2)}, u32[]{:S(2)}) collective-permute-start(f32[8,2048]{1,0:T(8,128)S(1)} %get-tuple-element.27.own.lanes_a), channel_id=1, source_target_pairs={{5,2},{4,3},{3,4},{2,5},{9,6},{8,7},{7,8},{6,9},{13,10},{12,11},{1... | collective-permute-start | bytes 196616 | tf_op jit(solution)/shard_map/ppermute | solution.py:422
  27.9 19.3 %collective-permute-start.4 = (f32[1024,128]{1,0:T(8,128)S(1)}, f32[1024,128]{1,0:T(8,128)S(1)}, u32[]{:S(2)}, u32[]{:S(2)}) collective-permute-start(f32[1024,128]{1,0:T(8,128)S(1)} %get-tuple-element.32.refs_1_.refs_7_), channel_id=1, source_target_pairs={{0,2},{2,0},{4,6},{6,4},{8,10},{10,8},{12,14},{14,12},{1,3},{3,1},... | collective-permute-start | bytes 1572872 | tf_op jit(solution)/shard_map/ppermute | solution.py:385
  39.7 30.5 %collective-permute-start.14 = (f32[1024,128]{1,0:T(8,128)S(1)}, f32[1024,128]{1,0:T(8,128)S(1)}, u32[]{:S(2)}, u32[]{:S(2)}) collective-permute-start(f32[1024,128]{1,0:T(8,128)S(1)} %get-tuple-element.32.refs_1_.refs_7_), channel_id=1, source_target_pairs={{0,1},{1,0},{2,3},{3,2},{4,5},{5,4},{6,7},{7,6},{8,9},{9,8},{10,11... | collective-permute-start | bytes 1572872 | tf_op jit(solution)/shard_map/ppermute | solution.py:400
  43.0 33.5 %collective-permute-start.10 = (f32[1024,128]{1,0:T(8,128)S(1)}, f32[1024,128]{1,0:T(8,128)S(1)}, u32[]{:S(2)}, u32[]{:S(2)}) collective-permute-start(f32[1024,128]{1,0:T(8,128)S(1)} %collective-permute-done.2.refs_0_), channel_id=1, source_target_pairs={{0,1},{1,0},{2,3},{3,2},{4,5},{5,4},{6,7},{7,6},{8,9},{9,8},{10,11... | collective-permute-start | bytes 1572872 | tf_op jit(solution)/shard_map/ppermute | solution.py:400
  43.1 16.3 %collective-permute-start.3 = (f32[1024,128]{1,0:T(8,128)S(1)}, f32[1024,128]{1,0:T(8,128)S(1)}, u32[]{:S(2)}, u32[]{:S(2)}) collective-permute-start(f32[1024,128]{1,0:T(8,128)S(1)} %collective-permute-done.2.refs_0_), channel_id=1, source_target_pairs={{6,2},{0,4},{10,6},{4,8},{14,10},{8,12},{7,3},{1,5},{11,7},{5,9},{... | collective-permute-start | bytes 1572872 | tf_op jit(solution)/shard_map/ppermute | solution.py:395
  47.2 29.3 %collective-permute-start.11 = (f32[1024,128]{1,0:T(8,128)S(1)}, f32[1024,128]{1,0:T(8,128)S(1)}, u32[]{:S(2)}, u32[]{:S(2)}) collective-permute-start(f32[1024,128]{1,0:T(8,128)S(1)} %collective-permute-done.4.refs_1_), channel_id=1, source_target_pairs={{0,1},{1,0},{2,3},{3,2},{4,5},{5,4},{6,7},{7,6},{8,9},{9,8},{10,11... | collective-permute-start | bytes 1572872 | tf_op jit(solution)/shard_map/ppermute | solution.py:400
  47.5 22.7 %collective-permute-start.5 = (f32[1024,128]{1,0:T(8,128)S(1)}, f32[1024,128]{1,0:T(8,128)S(1)}, u32[]{:S(2)}, u32[]{:S(2)}) collective-permute-start(f32[1024,128]{1,0:T(8,128)S(1)} %collective-permute-done.4.refs_1_), channel_id=1, source_target_pairs={{6,2},{0,4},{10,6},{4,8},{14,10},{8,12},{7,3},{1,5},{11,7},{5,9},{... | collective-permute-start | bytes 1572872 | tf_op jit(solution)/shard_map/ppermute | solution.py:395
  59.4 21.1 %collective-permute-start.6 = (f32[1024,128]{1,0:T(8,128)S(1)}, f32[1024,128]{1,0:T(8,128)S(1)}, u32[]{:S(2)}, u32[]{:S(2)}) collective-permute-start(f32[1024,128]{1,0:T(8,128)S(1)} %collective-permute-done.3.refs_0_), channel_id=1, source_target_pairs={{0,1},{1,0},{2,3},{3,2},{4,5},{5,4},{6,7},{7,6},{8,9},{9,8},{10,11... | collective-permute-start | bytes 1572872 | tf_op jit(solution)/shard_map/ppermute | solution.py:400
  70.2 10.3 %collective-permute-start.7 = (f32[1024,128]{1,0:T(8,128)S(1)}, f32[1024,128]{1,0:T(8,128)S(1)}, u32[]{:S(2)}, u32[]{:S(2)}) collective-permute-start(f32[1024,128]{1,0:T(8,128)S(1)} %collective-permute-done.5.refs_1_), channel_id=1, source_target_pairs={{0,1},{1,0},{2,3},{3,2},{4,5},{5,4},{6,7},{7,6},{8,9},{9,8},{10,11... | collective-permute-start | bytes 1572872 | tf_op jit(solution)/shard_map/ppermute | solution.py:400
  88.8 6.2 %collective-permute-start.16 = (f32[8,128]{1,0:T(8,128)S(1)}, f32[8,128]{1,0:T(8,128)S(1)}, u32[]{:S(2)}, u32[]{:S(2)}) collective-permute-start(f32[8,128]{1,0:T(8,128)S(1)} %add.51), channel_id=1, source_target_pairs={{0,2},{2,0},{4,6},{6,4},{8,10},{10,8},{12,14},{14,12},{1,3},{3,1},... | collective-permute-start | bytes 12296 | tf_op jit(solution)/shard_map/ppermute | solution.py:434
  95.0 4.4 %collective-permute-start.17 = (f32[8,128]{1,0:T(8,128)S(1)}, f32[8,128]{1,0:T(8,128)S(1)}, u32[]{:S(2)}, u32[]{:S(2)}) collective-permute-start(f32[8,128]{1,0:T(8,128)S(1)} %add.52), channel_id=1, source_target_pairs={{0,4},{2,6},{4,0},{6,2},{8,12},{10,14},{12,8},{14,10},{1,5},{3,7},... | collective-permute-start | bytes 12296 | tf_op jit(solution)/shard_map/ppermute | solution.py:434
  99.4 5.1 %collective-permute-start.18 = (f32[8,128]{1,0:T(8,128)S(1)}, f32[8,128]{1,0:T(8,128)S(1)}, u32[]{:S(2)}, u32[]{:S(2)}) collective-permute-start(f32[8,128]{1,0:T(8,128)S(1)} %add.53), channel_id=1, source_target_pairs={{0,8},{2,10},{4,12},{6,14},{8,0},{10,2},{12,4},{14,6},{1,9},{3,11}... | collective-permute-start | bytes 12296 | tf_op jit(solution)/shard_map/ppermute | solution.py:434
  102.4 26.8 %collective-permute-start.23 = (f32[1024,128]{1,0:T(8,128)S(1)}, f32[1024,128]{1,0:T(8,128)S(1)}, u32[]{:S(2)}, u32[]{:S(2)}) collective-permute-start(f32[1024,128]{1,0:T(8,128)S(1)} %get-tuple-element.42.refs_0_.refs_8_), channel_id=1, source_target_pairs={{0,2},{2,0},{4,6},{6,4},{8,10},{10,8},{12,14},{14,12},{1,3},{3,1},... | collective-permute-start | bytes 1572872 | tf_op jit(solution)/shard_map/ppermute | solution.py:385
  103.4 29.4 %collective-permute-start.25 = (f32[1024,128]{1,0:T(8,128)S(1)}, f32[1024,128]{1,0:T(8,128)S(1)}, u32[]{:S(2)}, u32[]{:S(2)}) collective-permute-start(f32[1024,128]{1,0:T(8,128)S(1)} %get-tuple-element.43.refs_1_.refs_9_), channel_id=1, source_target_pairs={{0,2},{2,0},{4,6},{6,4},{8,10},{10,8},{12,14},{14,12},{1,3},{3,1},... | collective-permute-start | bytes 1572872 | tf_op jit(solution)/shard_map/ppermute | solution.py:385
  105.9 19.5 %collective-permute-start.20 = (f32[8,128]{1,0:T(8,128)S(1)}, f32[8,128]{1,0:T(8,128)S(1)}, u32[]{:S(2)}, u32[]{:S(2)}) collective-permute-start(f32[8,128]{1,0:T(8,128)S(1)} %broadcast_add_fusion), channel_id=1, source_target_pairs={{0,2},{2,0},{4,6},{6,4},{8,10},{10,8},{12,14},{14,12},{1,3},{3,1},... | collective-permute-start | bytes 12296 | tf_op jit(solution)/shard_map/ppermute | solution.py:434
  106.8 29.6 %collective-permute-start.31 = (f32[1024,128]{1,0:T(8,128)S(1)}, f32[1024,128]{1,0:T(8,128)S(1)}, u32[]{:S(2)}, u32[]{:S(2)}) collective-permute-start(f32[1024,128]{1,0:T(8,128)S(1)} %get-tuple-element.42.refs_0_.refs_8_), channel_id=1, source_target_pairs={{0,1},{1,0},{2,3},{3,2},{4,5},{5,4},{6,7},{7,6},{8,9},{9,8},{10,11... | collective-permute-start | bytes 1572872 | tf_op jit(solution)/shard_map/ppermute | solution.py:400
  126.8 25.7 %collective-permute-start.32 = (f32[1024,128]{1,0:T(8,128)S(1)}, f32[1024,128]{1,0:T(8,128)S(1)}, u32[]{:S(2)}, u32[]{:S(2)}) collective-permute-start(f32[1024,128]{1,0:T(8,128)S(1)} %get-tuple-element.43.refs_1_.refs_9_), channel_id=1, source_target_pairs={{0,1},{1,0},{2,3},{3,2},{4,5},{5,4},{6,7},{7,6},{8,9},{9,8},{10,11... | collective-permute-start | bytes 1572872 | tf_op jit(solution)/shard_map/ppermute | solution.py:400
  128.9 7.4 %collective-permute-start.22 = (f32[8,128]{1,0:T(8,128)S(1)}, f32[8,128]{1,0:T(8,128)S(1)}, u32[]{:S(2)}, u32[]{:S(2)}) collective-permute-start(f32[8,128]{1,0:T(8,128)S(1)} %add.58), channel_id=1, source_target_pairs={{0,8},{2,10},{4,12},{6,14},{8,0},{10,2},{12,4},{14,6},{1,9},{3,11}... | collective-permute-start | bytes 12296 | tf_op jit(solution)/shard_map/ppermute | solution.py:434
  129.2 15.9 %collective-permute-start.24 = (f32[1024,128]{1,0:T(8,128)S(1)}, f32[1024,128]{1,0:T(8,128)S(1)}, u32[]{:S(2)}, u32[]{:S(2)}) collective-permute-start(f32[1024,128]{1,0:T(8,128)S(1)} %collective-permute-done.23.refs_0_), channel_id=1, source_target_pairs={{6,2},{0,4},{10,6},{4,8},{14,10},{8,12},{7,3},{1,5},{11,7},{5,9},{... | collective-permute-start | bytes 1572872 | tf_op jit(solution)/shard_map/ppermute | solution.py:395
  132.8 19.7 %collective-permute-start.26 = (f32[1024,128]{1,0:T(8,128)S(1)}, f32[1024,128]{1,0:T(8,128)S(1)}, u32[]{:S(2)}, u32[]{:S(2)}) collective-permute-start(f32[1024,128]{1,0:T(8,128)S(1)} %collective-permute-done.25.refs_1_), channel_id=1, source_target_pairs={{6,2},{0,4},{10,6},{4,8},{14,10},{8,12},{7,3},{1,5},{11,7},{5,9},{... | collective-permute-start | bytes 1572872 | tf_op jit(solution)/shard_map/ppermute | solution.py:395
  136.4 22.5 %collective-permute-start.29 = (f32[1024,128]{1,0:T(8,128)S(1)}, f32[1024,128]{1,0:T(8,128)S(1)}, u32[]{:S(2)}, u32[]{:S(2)}) collective-permute-start(f32[1024,128]{1,0:T(8,128)S(1)} %collective-permute-done.23.refs_0_), channel_id=1, source_target_pairs={{0,1},{1,0},{2,3},{3,2},{4,5},{5,4},{6,7},{7,6},{8,9},{9,8},{10,11... | collective-permute-start | bytes 1572872 | tf_op jit(solution)/shard_map/ppermute | solution.py:400
  136.4 22.4 %collective-permute-start.30 = (f32[1024,128]{1,0:T(8,128)S(1)}, f32[1024,128]{1,0:T(8,128)S(1)}, u32[]{:S(2)}, u32[]{:S(2)}) collective-permute-start(f32[1024,128]{1,0:T(8,128)S(1)} %collective-permute-done.25.refs_1_), channel_id=1, source_target_pairs={{0,1},{1,0},{2,3},{3,2},{4,5},{5,4},{6,7},{7,6},{8,9},{9,8},{10,11... | collective-permute-start | bytes 1572872 | tf_op jit(solution)/shard_map/ppermute | solution.py:400
  145.1 17.7 %collective-permute-start.27 = (f32[1024,128]{1,0:T(8,128)S(1)}, f32[1024,128]{1,0:T(8,128)S(1)}, u32[]{:S(2)}, u32[]{:S(2)}) collective-permute-start(f32[1024,128]{1,0:T(8,128)S(1)} %collective-permute-done.24.refs_0_), channel_id=1, source_target_pairs={{0,1},{1,0},{2,3},{3,2},{4,5},{5,4},{6,7},{7,6},{8,9},{9,8},{10,11... | collective-permute-start | bytes 1572872 | tf_op jit(solution)/shard_map/ppermute | solution.py:400
  152.5 10.4 %collective-permute-start.28 = (f32[1024,128]{1,0:T(8,128)S(1)}, f32[1024,128]{1,0:T(8,128)S(1)}, u32[]{:S(2)}, u32[]{:S(2)}) collective-permute-start(f32[1024,128]{1,0:T(8,128)S(1)} %collective-permute-done.26.refs_1_), channel_id=1, source_target_pairs={{0,1},{1,0},{2,3},{3,2},{4,5},{5,4},{6,7},{7,6},{8,9},{9,8},{10,11... | collective-permute-start | bytes 1572872 | tf_op jit(solution)/shard_map/ppermute | solution.py:400
  167.9 7.5 %collective-permute-start.34 = (f32[8,128]{1,0:T(8,128)S(1)}, f32[8,128]{1,0:T(8,128)S(1)}, u32[]{:S(2)}, u32[]{:S(2)}) collective-permute-start(f32[8,128]{1,0:T(8,128)S(1)} %add.60), channel_id=1, source_target_pairs={{0,2},{2,0},{4,6},{6,4},{8,10},{10,8},{12,14},{14,12},{1,3},{3,1},... | collective-permute-start | bytes 12296 | tf_op jit(solution)/shard_map/ppermute | solution.py:434
  179.7 5.5 %collective-permute-start.36 = (f32[8,128]{1,0:T(8,128)S(1)}, f32[8,128]{1,0:T(8,128)S(1)}, u32[]{:S(2)}, u32[]{:S(2)}) collective-permute-start(f32[8,128]{1,0:T(8,128)S(1)} %add.62), channel_id=1, source_target_pairs={{0,8},{2,10},{4,12},{6,14},{8,0},{10,2},{12,4},{14,6},{1,9},{3,11}... | collective-permute-start | bytes 12296 | tf_op jit(solution)/shard_map/ppermute | solution.py:434
  (13 other events, 39.6 us)
where the time goes:
time: 187 us
  starting transfers between devices  62.4 us (33%)
  waiting for transfers between devices  57.1 us (31%)
  Pallas kernels  55.1 us (29%)
  local copies, waits for them, and re-layouts  9.34 us (5%)
  other arithmetic  1.98 us (1%)
    ppermute x4, waiting for transfers between devices, pair_shift(): return lax.ppermute(block, 'tm', route)  28.9 us
    ppermute x9, waiting for transfers between devices, total(): lax.ppermute(value, 'tm', [(i, i ^ step) for i in range(count)])  25.4 us
    ppermute x9, starting transfers between devices, total(): lax.ppermute(value, 'tm', [(i, i ^ step) for i in range(count)])  23.3 us
    pallas_call x6, Pallas kernels, product_pair(): pl.pallas_call(functools.partial(product_kernel, points, start, (marks, l...  22.8 us
    pallas_call x3, Pallas kernels, eval_pair(): pl.pallas_call(functools.partial(eval_kernel, points), out_shape=(pltpu.V...  18.6 us
    ppermute x4, starting transfers between devices, pair_shift(): return lax.ppermute(block, 'tm', route)  14.6 us
    ppermute x15, starting transfers between devices, core_swap(): return lax.ppermute(block, 'tile', [(i, i ^ 1) for i in range(count)])  10.4 us
    ppermute x4, starting transfers between devices, pair_swap(): return lax.ppermute(block, 'tm', [(i, i ^ 1) for i in range(count)])  9.56 us
  transfers between devices with their start and end apart: 37, of which 12 were waited for; matrix products, arithmetic and copies ran while one was open for 0% of the time, Pallas kernels for 24%

commit v1 on v0

v1 whole, which is shorter than its diff:
```python
import functools

import jax
import jax.numpy as jnp
from jax import lax
from jax.experimental import pallas as pl
from jax.experimental.pallas import tpu as pltpu
from jax.sharding import PartitionSpec as P

LANES = 128
ROWS = 224
SLOTS = 72
UNROLL = 8
EVAL_UNROLL = 2
PIECES = 2
FAR = 1.0e6
F32 = jnp.float32
BF16 = jnp.bfloat16
MIB = 1 << 20


def vmem_spec():
    return pl.BlockSpec(memory_space=pltpu.VMEM)


def smem_spec():
    return pl.BlockSpec(memory_space=pltpu.SMEM)


def split2(value):
    high = value.astype(BF16)
    low = (value - high.astype(F32)).astype(BF16)
    return high, low


def list_length(points):
    return 2 * (points // LANES) * -(-points // ROWS) + UNROLL


def header_rows(points):
    return -(-(3 * (points // LANES) + 3) // 8) * 8


def piece_sizes(points):
    large = points // LANES * 5 // 8 * LANES
    return [large, points - large]


def spans(chunks, top):
    found, start = [], 0
    for c, chunk in enumerate(chunks):
        skip = top if c == 0 else 0
        found.append((chunk, start, skip, chunk.shape[0] - skip))
        start += chunk.shape[0] - skip
    return found


def group_rows(chunks, top, start):
    for chunk, begin, skip, size in spans(chunks, top):
        if begin <= start < begin + size:
            return chunk, slice(start - begin + skip, start - begin + skip + LANES)
    raise ValueError(start)


def read_rows(chunks, top, start):
    chunk, here = group_rows(chunks, top, start)
    return chunk[here, :]


def sort_kernel(points, coords_hbm, noise_hbm, values_hbm, *refs):
    out_values, refs = refs[: PIECES + 1], refs[PIECES + 1 :]
    rows, ranks, coords, noise, values, xcol, facts, sorted_facts, sorted_values, rank_row, rank_smem, sems = refs
    fetches = [
        pltpu.make_async_copy(source, target, sems.at[k])
        for k, (source, target) in enumerate(((coords_hbm, coords), (noise_hbm, noise), (values_hbm, values)))
    ]
    for fetch in fetches:
        fetch.start()
    fetches[0].wait()
    groups = points // LANES
    for g in range(groups):
        here = slice(g * LANES, (g + 1) * LANES)
        xcol[here, :] = jnp.transpose(jnp.broadcast_to(coords[1:2, here], (LANES, LANES)))

    xrow = [jnp.broadcast_to(coords[1:2, g * LANES : (g + 1) * LANES], (8, LANES)) for g in range(groups)]
    lane = lax.broadcasted_iota(jnp.int32, (8, LANES), 1)
    sub = lax.broadcasted_iota(jnp.int32, (8, LANES), 0)
    counts = tuple(jnp.zeros((8, LANES), F32) for _ in range(groups))
    for jg in range(groups):

        def count(step, carry):
            at = pl.multiple_of(jg * LANES + step * 8, 8)
            mine = xcol[pl.ds(at, 8), :]
            out = []
            for ig in range(groups):
                if ig == jg:
                    before = jnp.logical_or(
                        mine < xrow[ig],
                        jnp.logical_and(mine == xrow[ig], sub + step * 8 < lane),
                    )
                elif ig > jg:
                    before = mine <= xrow[ig]
                else:
                    before = mine < xrow[ig]
                out.append(carry[ig] + jnp.where(before, 1.0, 0.0))
            return tuple(out)

        counts = lax.fori_loop(0, LANES // 8, count, counts, unroll=2)
    for g in range(groups):
        rank_row[0:1, g * LANES : (g + 1) * LANES] = jnp.sum(counts[g], axis=0, keepdims=True).astype(jnp.int32)
    ranks[...] = rank_row[...]
    copy = pltpu.make_async_copy(rank_row, rank_smem, sems.at[3])
    copy.start()
    fetches[1].wait()
    blank = jnp.zeros((LANES - 4, LANES), F32)
    for g in range(groups):
        here = slice(g * LANES, (g + 1) * LANES)
        facts[here, :] = jnp.transpose(jnp.concatenate([coords[:, here], noise[:, here], blank], axis=0))
    copy.wait()
    fetches[2].wait()

    def scatter(step, carry):
        at = pl.multiple_of(step * 8, 8)
        block = values[pl.ds(at, 8), :]
        fact = facts[pl.ds(at, 8), :]
        for k in range(8):
            to = rank_smem[0, at + k]
            sorted_facts[pl.ds(to, 1), :] = fact[k : k + 1, :]
            sorted_values[pl.ds(to, 1), :] = block[k : k + 1, :]
        return carry

    lax.fori_loop(0, points // 8, scatter, 0, unroll=4)
    header = header_rows(points)
    whole = out_values[PIECES]
    whole[header:, :] = sorted_values[...]
    for chunk, start, skip, size in spans(out_values[:PIECES], header):
        chunk[skip:, :] = sorted_values[start : start + size, :]
    head = out_values[0]
    for g in range(groups):
        here = slice(g * LANES, (g + 1) * LANES)
        got = sorted_facts[here, :]
        flat = jnp.transpose(got)
        for k in range(4):
            if k < 3:
                head[k * groups + g : k * groups + g + 1, :] = flat[k : k + 1, :]
            scale = 4.0 if k < 3 else 1.0
            rows[k, here, :] = jnp.broadcast_to(got[:, k : k + 1] * scale, (LANES, LANES))
    for k in range(4):
        rows[k, points:, :] = jnp.full((ROWS, LANES), FAR if k < 3 else 0.0, F32)
    end = 3 * groups
    head[end : end + 1, :] = jnp.full((1, LANES), jnp.min(coords[0:1, :]), F32)
    head[end + 1 : end + 2, :] = jnp.full((1, LANES), jnp.max(coords[0:1, :]), F32)
    head[end + 2 : header, :] = jnp.ones((header - end - 2, LANES), F32)
    whole[0:header, :] = head[0:header, :]


def sort_points(coords, noise, values):
    points, width = values.shape
    header = header_rows(points)
    out = pl.pallas_call(
        functools.partial(sort_kernel, points),
        out_shape=tuple(
            jax.ShapeDtypeStruct((size + (header if c in (0, PIECES) else 0), width), F32)
            for c, size in enumerate([*piece_sizes(points), points])
        )
        + (
            pltpu.VMEM((4, points + ROWS, LANES), F32),
            jax.ShapeDtypeStruct((1, points), jnp.int32),
        ),
        in_specs=[pl.BlockSpec(memory_space=pltpu.HBM)] * 3,
        out_specs=[vmem_spec()] * (PIECES + 3),
        scratch_shapes=[
            pltpu.VMEM((3, points), F32),
            pltpu.VMEM((1, points), F32),
            pltpu.VMEM((points, width), F32),
            pltpu.VMEM((points, LANES), F32),
            pltpu.VMEM((points, LANES), F32),
            pltpu.VMEM((points, LANES), F32),
            pltpu.VMEM((points, LANES), F32),
            pltpu.VMEM((1, points), jnp.int32),
            pltpu.SMEM((1, points), jnp.int32),
            pltpu.SemaphoreType.DMA((4,)),
        ],
        compiler_params=pltpu.CompilerParams(vmem_limit_bytes=14 * MIB),
        name="sort_points",
    )(coords, noise, values)
    return out[:PIECES], *out[PIECES:]


def tile_values(rows, cols, at, count):
    span = pl.ds(at, count)
    dtime = jnp.abs(rows[0, span, :] - cols[0])
    dx = rows[1, span, :] - cols[1]
    dy = rows[2, span, :] - cols[2]
    square = jnp.maximum(dx * dx + dy * dy, 1e-30)
    dist = square * lax.rsqrt(square)
    near = jnp.maximum(4.0 - dtime, 0.0) * jnp.maximum(4.0 - dist, 0.0)
    near = near * near
    return near * near * ((dtime + 1.0) * (dist + 1.0))


def fill_tile(tile, rows, facts, w, step, at):
    cols = [jnp.broadcast_to(facts[pl.ds(k * step + w, 1), :], (16, LANES)) for k in range(3)]
    for part in range(ROWS // 16):
        start = pl.multiple_of(at + part * 16, 16)
        high, low = split2(tile_values(rows, cols, start, 16))
        tile[part * 16 : (part + 1) * 16, 0:LANES] = high
        tile[part * 16 : (part + 1) * 16, LANES:] = low


def gather_facts(windows, facts, heads):
    for half, head in enumerate(heads):
        for k in range(3):
            base = (2 * k + half) * windows
            facts[base : base + windows, :] = head[k * windows : (k + 1) * windows, :] * 4.0


def find_ranges(points, own, other, table, base):
    windows = points // LANES
    end_row = 3 * windows
    x = other[windows : 2 * windows, :]
    low = jnp.broadcast_to(x[:, 0:1], (windows, LANES))
    high = jnp.broadcast_to(x[:, LANES - 1 : LANES], (windows, LANES))
    begin = jnp.zeros((windows, LANES), F32)
    beyond = jnp.zeros((windows, LANES), F32)
    for g in range(windows):
        row = jnp.broadcast_to(own[windows + g : windows + g + 1, :], (windows, LANES))
        begin = begin + jnp.where(low - row >= 1.0, 1.0, 0.0)
        beyond = beyond + jnp.where(row - high >= 1.0, 1.0, 0.0)
    begin = jnp.sum(begin, axis=1, keepdims=True)
    end = points - jnp.sum(beyond, axis=1, keepdims=True)
    first = begin.astype(jnp.int32) // 16 * 16
    length = end - first.astype(F32)
    blocks = jnp.zeros((windows, 1), F32)
    for k in range(-(-points // ROWS)):
        blocks = blocks + jnp.where(length > float(k * ROWS), 1.0, 0.0)
    early, late, mark = end_row, end_row + 1, end_row + 2
    apart = jnp.maximum(
        other[early : early + 1, 0:1] - own[late : late + 1, 0:1],
        own[early : early + 1, 0:1] - other[late : late + 1, 0:1],
    )
    apart = jnp.where(other[mark : mark + 1, 0:1] > 0.5, apart, 2.0)
    blocks = jnp.where(jnp.logical_and(end > begin, jnp.broadcast_to(apart, (windows, 1)) < 1.0), blocks, 0.0)
    table[base : base + windows, 0:LANES] = jnp.broadcast_to(first, (windows, LANES))
    table[base : base + windows, LANES:] = jnp.broadcast_to(blocks.astype(jnp.int32), (windows, LANES))


def eval_kernel(points, own, head_a, head_b, rows, cache, work, facts, table, table_smem, sem):
    windows = points // LANES
    for half, head in enumerate((head_a, head_b)):
        find_ranges(points, own, head, table, half * windows)
    copy = pltpu.make_async_copy(table, table_smem, sem)
    copy.start()
    gather_facts(windows, facts, (head_a, head_b))
    copy.wait()

    def window(w, slot):
        first = table_smem[w, 0]
        blocks = table_smem[w, LANES]

        def block(b, carry):
            work[0, slot + b] = first + b * ROWS
            work[1, slot + b] = w
            return carry

        lax.fori_loop(0, blocks, block, 0)
        return slot + blocks

    total = lax.fori_loop(0, 2 * windows, window, 0)
    for k in range(UNROLL):
        work[0, total + k] = points
        work[1, total + k] = 0
    work[2, 0] = total

    def slots(step, carry):
        for k in range(EVAL_UNROLL):
            s = step * EVAL_UNROLL + k
            fill_tile(cache.at[s], rows, facts, work[1, s], 2 * windows, pl.multiple_of(work[0, s], 16))
        return carry

    kept = jnp.minimum(total, SLOTS)
    lax.fori_loop(0, (kept + EVAL_UNROLL - 1) // EVAL_UNROLL, slots, 0)


def eval_pair(points, own, heads, rows):
    windows = points // LANES
    return pl.pallas_call(
        functools.partial(eval_kernel, points),
        out_shape=(
            pltpu.VMEM((SLOTS, ROWS, 2 * LANES), BF16),
            jax.ShapeDtypeStruct((3, list_length(points)), jnp.int32),
            jax.ShapeDtypeStruct((6 * windows, LANES), F32),
        ),
        in_specs=[vmem_spec()] * 4,
        out_specs=(vmem_spec(), smem_spec(), vmem_spec()),
        scratch_shapes=[
            pltpu.VMEM((2 * windows, 2 * LANES), jnp.int32),
            pltpu.SMEM((2 * windows, 2 * LANES), jnp.int32),
            pltpu.SemaphoreType.DMA,
        ],
        compiler_params=pltpu.CompilerParams(vmem_limit_bytes=4 * MIB),
        cost_estimate=pl.CostEstimate(flops=1_000_000, bytes_accessed=100_000, transcendentals=0),
        name="eval_pair",
    )(own, *heads, rows)


def product_kernel(points, headed, counts, marker, work, facts, rows, cache, *refs):
    groups = []
    for count in counts:
        groups.append(refs[:count])
        refs = refs[count:]
    first, second, before, given, once, out, sums = groups
    values = (first, second)
    acc, pairs, tile = refs
    windows = points // LANES
    header = header_rows(points)
    top = header if headed else 0
    total = work[2, 0]
    acc[...] = jnp.zeros_like(acc)

    @pl.when(total > 0)
    def _():
        for half in range(2):
            for chunk, start, skip, size in spans(values[half], top):
                base = half * windows + start // LANES

                def split(w, carry):
                    high, low = split2(chunk[pl.ds(pl.multiple_of(skip + w * LANES, 8), LANES), :])
                    both = jnp.concatenate([high, low], axis=1)
                    pairs[base + w, 0:LANES, :] = both
                    pairs[base + w, LANES:, :] = both
                    return carry

                lax.fori_loop(0, size // LANES, split, 0)

        def slots(step, carry):
            for k in range(UNROLL):
                s = step * UNROLL + k
                at = pl.multiple_of(work[0, s], 16)
                acc[pl.ds(at, ROWS), :] += jnp.dot(
                    cache[s], pairs[work[1, s]], preferred_element_type=F32
                )
            return carry

        kept = jnp.minimum(total, SLOTS)
        lax.fori_loop(0, (kept + UNROLL - 1) // UNROLL, slots, 0)

        @pl.when(total > SLOTS)
        def _():
            def again(s, carry):
                at = pl.multiple_of(work[0, s], 16)
                w = work[1, s]
                fill_tile(tile, rows, facts, w, 2 * windows, at)
                acc[pl.ds(at, ROWS), :] += jnp.dot(tile[...], pairs[w], preferred_element_type=F32)
                return carry

            lax.fori_loop(SLOTS, total, again, 0)

    marks = [jnp.zeros((8, LANES), F32)] * 5
    for start in range(0, points, LANES):
        here = slice(start, start + LANES)
        image = (acc[here, 0:LANES] + acc[here, LANES:]) * (2.0**-16)
        if before:
            image = image + read_rows(before, 0, start)
        else:
            image = image + rows[3, here, :] * read_rows(first, top, start)
        if len(out) > 1:
            target, place = group_rows(out[:-1], 0, start)
            target[place, :] = image
        out[-1][here, :] = image
        if marker is not None:
            marks = marker(marks, image, read_rows(given, header, start), read_rows(once, 0, start))
    if marker is not None:
        sums[0][...] = jnp.zeros((8, LANES), F32)
        for k in range(5):
            sums[0][k : k + 1, :] = jnp.sum(marks[k], axis=0, keepdims=True)


def fold(value):
    return jnp.sum(value.reshape(value.shape[0] // 8, 8, LANES), axis=0)


def inner_sums(marks, image, given, once):
    terms = (given * given, given * once, once * once, given * image, once * image)
    return [mark + fold(term) for mark, term in zip(marks, terms)]


def product_pair(points, evaluated, rows, values, headed, before=(), sent=False, marker=None, given=(), once=()):
    cache, work, facts = evaluated
    windows = points // LANES
    groups = (*values, before, given, once)
    operands = (facts, rows, cache, *(x for group in groups for x in group))
    sizes = [*(piece_sizes(points) if sent else []), points]
    sums = int(marker is not None)
    counts = [len(group) for group in groups] + [len(sizes), sums]
    out = pl.pallas_call(
        functools.partial(product_kernel, points, headed, counts, marker),
        out_shape=[jax.ShapeDtypeStruct((size, LANES), F32) for size in sizes]
        + [jax.ShapeDtypeStruct((8, LANES), F32)] * sums,
        in_specs=[smem_spec()] + [vmem_spec()] * len(operands),
        out_specs=[vmem_spec()] * (len(sizes) + sums),
        scratch_shapes=[
            pltpu.VMEM((points + ROWS, 2 * LANES), F32),
            pltpu.VMEM((2 * windows, 2 * LANES, 2 * LANES), BF16),
            pltpu.VMEM((ROWS, 2 * LANES), BF16),
        ],
        compiler_params=pltpu.CompilerParams(vmem_limit_bytes=15 * MIB),
        cost_estimate=pl.CostEstimate(flops=1_000_000, bytes_accessed=100_000, transcendentals=0),
        name="product_pair",
    )(work, *operands)
    return tuple(out)


def unsort_kernel(points, ranks, source, out):
    def gather(step, carry):
        at = pl.multiple_of(step * 8, 8)
        out[pl.ds(at, 8), :] = jnp.concatenate(
            [source[pl.ds(ranks[0, at + k], 1), :] for k in range(8)], axis=0
        )
        return carry

    lax.fori_loop(0, points // 8, gather, 0, unroll=4)


def unsort(ranks, source):
    points = ranks.shape[1]
    return pl.pallas_call(
        functools.partial(unsort_kernel, points),
        out_shape=jax.ShapeDtypeStruct((points, LANES), F32),
        in_specs=[smem_spec(), vmem_spec()],
        out_specs=vmem_spec(),
        compiler_params=pltpu.CompilerParams(vmem_limit_bytes=8 * MIB),
        cost_estimate=pl.CostEstimate(flops=1_000_000, bytes_accessed=100_000, transcendentals=0),
        name="unsort",
    )(ranks, source)


def pair_swap(block):
    count = lax.axis_size("tm")
    return lax.ppermute(block, "tm", [(i, i ^ 1) for i in range(count)])


def pair_shift(block, turn=0):
    count = lax.axis_size("tm")
    route = []
    for i in range(count):
        source = i - 2 if i % 2 == turn else i + 2
        if 0 <= source < count:
            route.append((source, i))
    return lax.ppermute(block, "tm", route)


def core_swap(block):
    count = lax.axis_size("tile")
    return lax.ppermute(block, "tile", [(i, i ^ 1) for i in range(count)])


def after(value, *earlier):
    return lax.optimization_barrier((value, *earlier))[0]


def stride_sum(value, step):
    count = lax.axis_size("tm")
    return value + lax.ppermute(value, "tm", [(i, i ^ step) for i in range(count)])


def far_strides():
    step, steps = 2, []
    while step < lax.axis_size("tm"):
        steps.append(step)
        step *= 2
    return steps


def total(value):
    for step in [1] + far_strides():
        value = stride_sum(value, step)
    return value + core_swap(value)


def local(coords, anomalies, noise_var):
    points = anomalies.shape[0]
    operands = [pltpu.with_memory_space_constraint(x, pltpu.HBM) for x in (coords, noise_var[None, :], anomalies)]
    given, whole, rows, ranks = sort_points(*operands)

    near = [pair_swap(c) for c in given]
    turned = pair_shift(given[1], 1)
    mates = core_swap(whole)
    own_eval = eval_pair(points, given[0], (given[0], mates), rows)
    image = product_pair(points, own_eval, rows, (given, (after(mates, own_eval[1]),)), True)
    near[0] = after(near[0], image[0], turned)
    far = [pair_shift(near[0])]
    near_mates = [core_swap(near[0])]
    near_eval = eval_pair(points, given[0], (near[0], near_mates[0]), rows)
    near[1] = after(near[1], near_eval[1])
    far.append(pair_swap(after(turned, near[1])))
    near_mates.append(core_swap(near[1]))
    image = product_pair(points, near_eval, rows, (near, near_mates), True, image)
    far[0] = after(far[0], image[0])
    far_mates = [core_swap(far[0])]
    far_eval = eval_pair(points, given[0], (far[0], far_mates[0]), rows)
    far[1] = after(far[1], far_eval[1])
    far_mates.append(core_swap(far[1]))
    *once, whole = product_pair(points, far_eval, rows, (far, far_mates), True, image, True)

    near = [pair_swap(c) for c in once]
    turned = pair_shift(once[1], 1)
    mates = core_swap(whole)
    image0 = unsort(ranks, after(whole, mates))
    image = product_pair(points, own_eval, rows, (once, (after(mates, image0),)), False)
    near[0] = after(near[0], image[0], turned)
    far = [pair_shift(near[0])]
    near_mates = [core_swap(near[0])]
    far.append(pair_swap(after(turned, near[1], near[0])))
    near_mates.append(core_swap(near[1]))
    image = product_pair(points, near_eval, rows, (near, near_mates), False, image)
    far_mates = [core_swap(c) for c in far]
    twice, sums = product_pair(points, far_eval, rows, (far, far_mates), False, image, False, inner_sums, given, once)
    image1 = unsort(ranks, twice)

    sums = total(sums)
    rr0, curve0, once_once, given_twice, once_twice = [sums[k : k + 1] for k in range(5)]
    alpha0 = rr0 / curve0
    rr1 = rr0 - 2.0 * alpha0 * curve0 + alpha0 * alpha0 * once_once
    beta = rr1 / rr0
    more = 1.0 + beta
    curve1 = more * more * curve0 - more * alpha0 * (given_twice + once_once) + alpha0 * alpha0 * once_twice
    alpha1 = rr1 / curve1
    residual = anomalies - alpha0 * image0
    weights = alpha0 * anomalies + alpha1 * (residual + beta * anomalies)
    again = (image0 - alpha0 * image1) + beta * image0
    return weights, residual - alpha1 * again


def solution(mesh):
    placed = (
        P(None, ("region", "tm", "tile")),
        P(("region", "tm", "tile"), None),
        P(("region", "tm", "tile")),
    )
    return jax.shard_map(
        local,
        mesh=mesh,
        in_specs=placed,
        out_specs=(P(("region", "tm", "tile"), None), P(("region", "tm", "tile"), None)),
        check_vma=False,
    )
```

time: 187 us -> 136 us (0.73)
  starting transfers between devices: 62.4 us -> 37.7 us
  waiting for transfers between devices: 57.1 us -> 43.7 us
  local copies, waits for them, and re-layouts: 9.34 us -> 0.01 us
  Pallas kernels: 55.1 us -> 51.2 us
    ppermute x4 -> x6, waiting for transfers between devices: 0.01 us -> 24.9 us  [pair_swap(): return lax.ppermute(block, 'tm', [(i, i ^ 1) for i in range(count)])]
    ppermute x4, waiting for transfers between devices: 28.9 us -> 8.15 us  [pair_shift(): return lax.ppermute(block, 'tm', route)]
    ppermute x14 -> x3, waiting for transfers between devices: 25.4 us -> 5.84 us  [stride_sum(): lax.ppermute(value, 'tm', [(i, i ^ step) for i in range(count)])]
    ppermute x14 -> x3, starting transfers between devices: 27.8 us -> 10.3 us  [stride_sum(): lax.ppermute(value, 'tm', [(i, i ^ step) for i in range(count)])]
    unnamed x16 -> x2, local copies, waits for them, and re-layouts: 9.26 us -> 0.01 us
    ppermute x15 -> x11, starting transfers between devices: 10.4 us -> 5.46 us  [core_swap(): return lax.ppermute(block, 'tile', [(i, i ^ 1) for i in range(count)])]
    pallas_call x6, Pallas kernels: 22.8 us -> 19.4 us  [product_pair(): pl.pallas_call(functools.partial(product_kernel, points, headed, counts,...]
    ppermute x4, starting transfers between devices: 14.6 us -> 11.8 us  [pair_shift(): return lax.ppermute(block, 'tm', route)]
  transfers between devices with their start and end apart: 37 -> 24, of which waited for: 12 -> 15; matrix products, arithmetic and copies ran while one was open for 0% -> 0% of each run, Pallas kernels for 24% -> 30%
where the time goes in v1:
time: 136 us; the launch traced here: 135 us
  Pallas kernels  51.2 us (38%)
  waiting for transfers between devices  43.7 us (32%)
  starting transfers between devices  37.7 us (28%)
  other arithmetic  1.82 us (1%)
    ppermute x6, waiting for transfers between devices, pair_swap(): return lax.ppermute(block, 'tm', [(i, i ^ 1) for i in range(count)])  24.9 us
    pallas_call x6, Pallas kernels, product_pair(): pl.pallas_call(functools.partial(product_kernel, points, headed, counts,...  19.4 us
    pallas_call x3, Pallas kernels, eval_pair(): pl.pallas_call(functools.partial(eval_kernel, points), out_shape=(pltpu.V...  17.7 us
    ppermute x4, starting transfers between devices, pair_shift(): return lax.ppermute(block, 'tm', route)  11.8 us
    ppermute x3, starting transfers between devices, stride_sum(): lax.ppermute(value, 'tm', [(i, i ^ step) for i in range(count)])  10.3 us
    ppermute x6, starting transfers between devices, pair_swap(): return lax.ppermute(block, 'tm', [(i, i ^ 1) for i in range(count)])  10.2 us
    pallas_call x1, Pallas kernels, sort_points(): pl.pallas_call(functools.partial(sort_kernel, points), out_shape=tuple((j...  8.76 us
    ppermute x4, waiting for transfers between devices, pair_shift(): return lax.ppermute(block, 'tm', route)  8.15 us
  transfers between devices with their start and end apart: 24, of which 15 were waited for; matrix products, arithmetic and copies ran while one was open for 0% of the time, Pallas kernels for 30%

profile of v1, /device:TPU:0, one launch (start us, length us, event | category | flops | bytes accessed | tf_op | source)
XLA Modules:
  0.0 135.3 jit_solution(3914188137296744704)
XLA Ops:
  0.6 8.8 %sort_points.1 = (f32[1336,128]{1,0:T(8,128)S(1)}, f32[768,128]{1,0:T(8,128)S(1)}, f32[2104,128]{1,0:T(8,128)S(1)}, f32[4,2272,128]{2,1,0:T(8,128)S(1)}, s32[1,2048]{1,0:T(1,128)S(1)}) custom-call(f32[3,2048]{1,0:T(4,128)} %coords_hbm.1, f32[1,2048]{1,0:T(1,128)} %bitcast.5, f32[2048,128]{1,0:T(8,128)} %values_hbm.1), custom_call_target="tpu_custom_call" | custom-call | tf_op jit(solution)/shard_map/sort_points/pallas_call | solution.py:160
  9.9 2.6 %collective-permute-start = (f32[1336,128]{1,0:T(8,128)S(1)}, f32[1336,128]{1,0:T(8,128)S(1)}, u32[]{:S(2)}, u32[]{:S(2)}) collective-permute-start(f32[1336,128]{1,0:T(8,128)S(1)} %get-tuple-element.31.own.head_a.refs_0_.refs_5_), channel_id=1, source_target_pairs={{0,2},{2,0},{4,6},{6,4},{8,10},{10,8},{12,14},{14,12},{1,3},{3,1},... | collective-permute-start | bytes 2052104 | tf_op jit(solution)/shard_map/ppermute | solution.py:440
  13.8 9.2 %eval_pair.3 = (bf16[72,224,256]{2,1,0:T(8,128)(2,1)S(1)}, s32[3,328]{1,0:T(4,128)S(1)}, f32[96,128]{1,0:T(8,128)S(1)}) custom-call(f32[1336,128]{1,0:T(8,128)S(1)} %get-tuple-element.31.own.head_a.refs_0_.refs_5_, f32[1336,128]{1,0:T(8,128)S(1)} %get-tuple-element.31.own.head_a.refs_0_.refs_5_, f32[2104,128]{1,0:T(8,128)S(1)} %collective-permute-done.1.head_b.refs_2_, ...), custom_call_target="tpu_custom_call" | custom-call | flops 1000000 | bytes 100000 | tf_op jit(solution)/shard_map/eval_pair/pallas_call | solution.py:287
  23.0 5.3 %product_pair.6.refs_4_ = f32[2048,128]{1,0:T(8,128)S(1)} custom-call(s32[3,328]{1,0:T(4,128)S(1)} %get-tuple-element.34.work, f32[96,128]{1,0:T(8,128)S(1)} %get-tuple-element.35.facts, f32[4,2272,128]{2,1,0:T(8,128)S(1)} %get-tuple-element.33.rows, bf16[72,224,256]{2,1,0:T(8,128)(2,1)S(1)} %get-tuple-element.36.cache, ...), custom_call_target="tpu_custom_call" | custom-call | flops 1000000 | bytes 100000 | tf_op jit(solution)/shard_map/product_pair/pallas_call | solution.py:396
  28.5 2.6 %collective-permute-start.5 = (f32[768,128]{1,0:T(8,128)S(1)}, f32[768,128]{1,0:T(8,128)S(1)}, u32[]{:S(2)}, u32[]{:S(2)}) collective-permute-start(f32[768,128]{1,0:T(8,128)S(1)} %get-tuple-element.37.refs_1_.refs_6_), channel_id=1, source_target_pairs={{0,2},{2,0},{4,6},{6,4},{8,10},{10,8},{12,14},{14,12},{1,3},{3,1},... | collective-permute-start | bytes 1179656 | tf_op jit(solution)/shard_map/ppermute | solution.py:440
  31.2 3.5 %collective-permute-start.3 = (f32[1336,128]{1,0:T(8,128)S(1)}, f32[1336,128]{1,0:T(8,128)S(1)}, u32[]{:S(2)}, u32[]{:S(2)}) collective-permute-start(f32[1336,128]{1,0:T(8,128)S(1)} %collective-permute-done.head_a.refs_0_), channel_id=1, source_target_pairs={{6,2},{0,4},{10,6},{4,8},{14,10},{8,12},{7,3},{1,5},{11,7},{5,9},{... | collective-permute-start | bytes 2052104 | tf_op jit(solution)/shard_map/ppermute | solution.py:450
  34.7 5.9 %eval_pair.4 = (bf16[72,224,256]{2,1,0:T(8,128)(2,1)S(1)}, s32[3,328]{1,0:T(4,128)S(1)}, f32[96,128]{1,0:T(8,128)S(1)}) custom-call(f32[1336,128]{1,0:T(8,128)S(1)} %get-tuple-element.31.own.head_a.refs_0_.refs_5_, f32[1336,128]{1,0:T(8,128)S(1)} %collective-permute-done.head_a.refs_0_, f32[1336,128]{1,0:T(8,128)S(1)} %collective-permute-done.4.head_b.refs_2_, ...), custom_call_target="tpu_custom_call" | custom-call | flops 1000000 | bytes 100000 | tf_op jit(solution)/shard_map/eval_pair/pallas_call | solution.py:287
  40.9 3.0 %collective-permute-start.6 = (f32[768,128]{1,0:T(8,128)S(1)}, f32[768,128]{1,0:T(8,128)S(1)}, u32[]{:S(2)}, u32[]{:S(2)}) collective-permute-start(f32[768,128]{1,0:T(8,128)S(1)} %collective-permute-done.5.refs_1_), channel_id=1, source_target_pairs={{0,1},{1,0},{2,3},{3,2},{4,5},{5,4},{6,7},{7,6},{8,9},{9,8},{10,11... | collective-permute-start | bytes 1179656 | tf_op jit(solution)/shard_map/ppermute | solution.py:455
  43.8 1.3 collective-permute-done.6.refs_3_
  45.2 3.3 %product_pair.7.refs_4_ = f32[2048,128]{1,0:T(8,128)S(1)} custom-call(s32[3,328]{1,0:T(4,128)S(1)} %get-tuple-element.40.work, f32[96,128]{1,0:T(8,128)S(1)} %get-tuple-element.41.facts, f32[4,2272,128]{2,1,0:T(8,128)S(1)} %get-tuple-element.33.rows, bf16[72,224,256]{2,1,0:T(8,128)(2,1)S(1)} %get-tuple-element.42.cache, ...), custom_call_target="tpu_custom_call" | custom-call | flops 1000000 | bytes 100000 | tf_op jit(solution)/shard_map/product_pair/pallas_call | solution.py:396
  50.8 1.7 %collective-permute-done.7.head_b.refs_2_ = f32[1336,128]{1,0:T(8,128)S(1)} collective-permute-done((f32[1336,128]{1,0:T(8,128)S(1)}, f32[1336,128]{1,0:T(8,128)S(1)}, u32[]{:S(2)}, u32[]{:S(2)}) %collective-permute-start.7) | collective-permute-done | bytes 684064 | tf_op jit(solution)/shard_map/ppermute | solution.py:455
  52.5 2.6 %eval_pair.5 = (bf16[72,224,256]{2,1,0:T(8,128)(2,1)S(1)}, s32[3,328]{1,0:T(4,128)S(1)}, f32[96,128]{1,0:T(8,128)S(1)}) custom-call(f32[1336,128]{1,0:T(8,128)S(1)} %get-tuple-element.31.own.head_a.refs_0_.refs_5_, f32[1336,128]{1,0:T(8,128)S(1)} %collective-permute-done.3.head_a.refs_0_, f32[1336,128]{1,0:T(8,128)S(1)} %collective-permute-done.7.head_b.refs_2_, ...), custom_call_target="tpu_custom_call" | custom-call | flops 1000000 | bytes 100000 | tf_op jit(solution)/shard_map/eval_pair/pallas_call | solution.py:287
  55.1 6.7 %collective-permute-done.8.refs_1_ = f32[768,128]{1,0:T(8,128)S(1)} collective-permute-done((f32[768,128]{1,0:T(8,128)S(1)}, f32[768,128]{1,0:T(8,128)S(1)}, u32[]{:S(2)}, u32[]{:S(2)}) %collective-permute-start.8) | collective-permute-done | bytes 393248 | tf_op jit(solution)/shard_map/ppermute | solution.py:440
  61.8 1.7 %collective-permute-done.9.refs_3_ = f32[768,128]{1,0:T(8,128)S(1)} collective-permute-done((f32[768,128]{1,0:T(8,128)S(1)}, f32[768,128]{1,0:T(8,128)S(1)}, u32[]{:S(2)}, u32[]{:S(2)}) %collective-permute-start.9) | collective-permute-done | bytes 393248 | tf_op jit(solution)/shard_map/ppermute | solution.py:455
  64.7 4.6 %collective-permute-start.10 = (f32[1280,128]{1,0:T(8,128)S(1)}, f32[1280,128]{1,0:T(8,128)S(1)}, u32[]{:S(2)}, u32[]{:S(2)}) collective-permute-start(f32[1280,128]{1,0:T(8,128)S(1)} %get-tuple-element.50.refs_0_.refs_7_), channel_id=1, source_target_pairs={{0,2},{2,0},{4,6},{6,4},{8,10},{10,8},{12,14},{14,12},{1,3},{3,1},... | collective-permute-start | bytes 1966088 | tf_op jit(solution)/shard_map/ppermute | solution.py:440
  70.6 2.7 %unsort.2 = f32[2048,128]{1,0:T(8,128)S(1)} custom-call(s32[1,2048]{1,0:T(1,128)S(1)} %get-tuple-element.53.ranks, f32[2048,128]{1,0:T(8,128)S(1)} %get-tuple-element.54.source), custom_call_target="tpu_custom_call" | custom-call | flops 1000000 | bytes 100000 | tf_op jit(solution)/shard_map/unsort/pallas_call | solution.py:427
  73.3 5.3 %product_pair.9.refs_4_ = f32[2048,128]{1,0:T(8,128)S(1)} custom-call(s32[3,328]{1,0:T(4,128)S(1)} %get-tuple-element.34.work, f32[96,128]{1,0:T(8,128)S(1)} %get-tuple-element.35.facts, f32[4,2272,128]{2,1,0:T(8,128)S(1)} %get-tuple-element.33.rows, bf16[72,224,256]{2,1,0:T(8,128)(2,1)S(1)} %get-tuple-element.36.cache, ...), custom_call_target="tpu_custom_call" | custom-call | flops 1000000 | bytes 100000 | tf_op jit(solution)/shard_map/product_pair/pallas_call | solution.py:396
  78.5 4.1 %collective-permute-done.12 = f32[768,128]{1,0:T(8,128)S(1)} collective-permute-done((f32[768,128]{1,0:T(8,128)S(1)}, f32[768,128]{1,0:T(8,128)S(1)}, u32[]{:S(2)}, u32[]{:S(2)}) %collective-permute-start.12) | collective-permute-done | bytes 393248 | tf_op jit(solution)/shard_map/ppermute | solution.py:450
  82.6 1.7 %collective-permute-done.10.refs_0_ = f32[1280,128]{1,0:T(8,128)S(1)} collective-permute-done((f32[1280,128]{1,0:T(8,128)S(1)}, f32[1280,128]{1,0:T(8,128)S(1)}, u32[]{:S(2)}, u32[]{:S(2)}) %collective-permute-start.10) | collective-permute-done | bytes 655392 | tf_op jit(solution)/shard_map/ppermute | solution.py:440
  84.3 5.7 %collective-permute-start.13 = (f32[1280,128]{1,0:T(8,128)S(1)}, f32[1280,128]{1,0:T(8,128)S(1)}, u32[]{:S(2)}, u32[]{:S(2)}) collective-permute-start(f32[1280,128]{1,0:T(8,128)S(1)} %collective-permute-done.10.refs_0_), channel_id=1, source_target_pairs={{6,2},{0,4},{10,6},{4,8},{14,10},{8,12},{7,3},{1,5},{11,7},{5,9},{... | collective-permute-start | bytes 1966088 | tf_op jit(solution)/shard_map/ppermute | solution.py:450
  90.1 10.4 %collective-permute-done.14.refs_1_ = f32[768,128]{1,0:T(8,128)S(1)} collective-permute-done((f32[768,128]{1,0:T(8,128)S(1)}, f32[768,128]{1,0:T(8,128)S(1)}, u32[]{:S(2)}, u32[]{:S(2)}) %collective-permute-start.14) | collective-permute-done | bytes 393248 | tf_op jit(solution)/shard_map/ppermute | solution.py:440
  100.8 3.0 %collective-permute-done.13.refs_0_ = f32[1280,128]{1,0:T(8,128)S(1)} collective-permute-done((f32[1280,128]{1,0:T(8,128)S(1)}, f32[1280,128]{1,0:T(8,128)S(1)}, u32[]{:S(2)}, u32[]{:S(2)}) %collective-permute-start.13) | collective-permute-done | bytes 655392 | tf_op jit(solution)/shard_map/ppermute | solution.py:450
  104.3 5.7 %collective-permute-done.15.refs_1_ = f32[768,128]{1,0:T(8,128)S(1)} collective-permute-done((f32[768,128]{1,0:T(8,128)S(1)}, f32[768,128]{1,0:T(8,128)S(1)}, u32[]{:S(2)}, u32[]{:S(2)}) %collective-permute-start.15) | collective-permute-done | bytes 393248 | tf_op jit(solution)/shard_map/ppermute | solution.py:440
  110.0 3.3 %product_pair.10.refs_4_ = f32[2048,128]{1,0:T(8,128)S(1)} custom-call(s32[3,328]{1,0:T(4,128)S(1)} %get-tuple-element.40.work, f32[96,128]{1,0:T(8,128)S(1)} %get-tuple-element.41.facts, f32[4,2272,128]{2,1,0:T(8,128)S(1)} %get-tuple-element.33.rows, bf16[72,224,256]{2,1,0:T(8,128)(2,1)S(1)} %get-tuple-element.42.cache, ...), custom_call_target="tpu_custom_call" | custom-call | flops 1000000 | bytes 100000 | tf_op jit(solution)/shard_map/product_pair/pallas_call | solution.py:396
  114.7 4.8 %collective-permute-start.20 = (f32[8,128]{1,0:T(8,128)S(1)}, f32[8,128]{1,0:T(8,128)S(1)}, u32[]{:S(2)}, u32[]{:S(2)}) collective-permute-start(f32[8,128]{1,0:T(8,128)S(1)} %get-tuple-element.58), channel_id=1, source_target_pairs={{0,2},{2,0},{4,6},{6,4},{8,10},{10,8},{12,14},{14,12},{1,3},{3,1},... | collective-permute-start | bytes 12296 | tf_op jit(solution)/shard_map/ppermute | solution.py:464
  119.5 1.6 %collective-permute-done.20 = f32[8,128]{1,0:T(8,128)S(1)} collective-permute-done((f32[8,128]{1,0:T(8,128)S(1)}, f32[8,128]{1,0:T(8,128)S(1)}, u32[]{:S(2)}, u32[]{:S(2)}) %collective-permute-start.20) | collective-permute-done | bytes 4128 | tf_op jit(solution)/shard_map/ppermute | solution.py:464
  121.1 3.6 %collective-permute-start.21 = (f32[8,128]{1,0:T(8,128)S(1)}, f32[8,128]{1,0:T(8,128)S(1)}, u32[]{:S(2)}, u32[]{:S(2)}) collective-permute-start(f32[8,128]{1,0:T(8,128)S(1)} %add.36), channel_id=1, source_target_pairs={{0,4},{2,6},{4,0},{6,2},{8,12},{10,14},{12,8},{14,10},{1,5},{3,7},... | collective-permute-start | bytes 12296 | tf_op jit(solution)/shard_map/ppermute | solution.py:464
  124.7 1.6 %collective-permute-done.21 = f32[8,128]{1,0:T(8,128)S(1)} collective-permute-done((f32[8,128]{1,0:T(8,128)S(1)}, f32[8,128]{1,0:T(8,128)S(1)}, u32[]{:S(2)}, u32[]{:S(2)}) %collective-permute-start.21) | collective-permute-done | bytes 4128 | tf_op jit(solution)/shard_map/ppermute | solution.py:464
  126.3 1.8 %collective-permute-start.22 = (f32[8,128]{1,0:T(8,128)S(1)}, f32[8,128]{1,0:T(8,128)S(1)}, u32[]{:S(2)}, u32[]{:S(2)}) collective-permute-start(f32[8,128]{1,0:T(8,128)S(1)} %add.37), channel_id=1, source_target_pairs={{0,8},{2,10},{4,12},{6,14},{8,0},{10,2},{12,4},{14,6},{1,9},{3,11}... | collective-permute-start | bytes 12296 | tf_op jit(solution)/shard_map/ppermute | solution.py:464
  128.1 2.7 %collective-permute-done.22 = f32[8,128]{1,0:T(8,128)S(1)} collective-permute-done((f32[8,128]{1,0:T(8,128)S(1)}, f32[8,128]{1,0:T(8,128)S(1)}, u32[]{:S(2)}, u32[]{:S(2)}) %collective-permute-start.22) | collective-permute-done | bytes 4128 | tf_op jit(solution)/shard_map/ppermute | solution.py:464
  130.8 2.7 %unsort.3 = f32[2048,128]{1,0:T(8,128)S(1)} custom-call(s32[1,2048]{1,0:T(1,128)S(1)} %get-tuple-element.53.ranks, f32[2048,128]{1,0:T(8,128)S(1)} %get-tuple-element.59.source), custom_call_target="tpu_custom_call" | custom-call | flops 1000000 | bytes 100000 | tf_op jit(solution)/shard_map/unsort/pallas_call | solution.py:427
  133.5 1.8 %multiply_subtract_fusion = (f32[2048,128]{1,0:T(8,128)}, f32[2048,128]{1,0:T(8,128)}) fusion(f32[2048,128]{1,0:T(8,128)S(1)} %unsort.2, f32[2048,128]{1,0:T(8,128)S(1)} %unsort.3, f32[2048,128]{1,0:T(8,128)S(1)} %copy-done, f32[128]{0:T(128)S(1)} %bitcast.7, f32[128]{0:T(128)S(1)} %get-tuple-element.60, f32[128]{0:T(128)S(1)} %bitcast.6), kind=kLoop, calls=%fused_computation | loop fusion | flops 3407872 | bytes 5244416 | tf_op jit(solution)/shard_map/sub | solution.py:532
  (37 shorter events, 9.3 us)
Async XLA Ops:
  9.4 4.4 %collective-permute-start.1 = (f32[2104,128]{1,0:T(8,128)S(1)}, f32[2104,128]{1,0:T(8,128)S(1)}, u32[]{:S(2)}, u32[]{:S(2)}) collective-permute-start(f32[2104,128]{1,0:T(8,128)S(1)} %get-tuple-element.32), channel_id=1, source_target_pairs={{0,1},{1,0},{2,3},{3,2},{4,5},{5,4},{6,7},{7,6},{8,9},{9,8},{10,11... | collective-permute-start | bytes 3231752 | tf_op jit(solution)/shard_map/ppermute | solution.py:455
  9.9 18.5 %collective-permute-start = (f32[1336,128]{1,0:T(8,128)S(1)}, f32[1336,128]{1,0:T(8,128)S(1)}, u32[]{:S(2)}, u32[]{:S(2)}) collective-permute-start(f32[1336,128]{1,0:T(8,128)S(1)} %get-tuple-element.31.own.head_a.refs_0_.refs_5_), channel_id=1, source_target_pairs={{0,2},{2,0},{4,6},{6,4},{8,10},{10,8},{12,14},{14,12},{1,3},{3,1},... | collective-permute-start | bytes 2052104 | tf_op jit(solution)/shard_map/ppermute | solution.py:440
  12.5 15.8 %collective-permute-start.2 = (f32[768,128]{1,0:T(8,128)S(1)}, f32[768,128]{1,0:T(8,128)S(1)}, u32[]{:S(2)}, u32[]{:S(2)}) collective-permute-start(f32[768,128]{1,0:T(8,128)S(1)} %get-tuple-element.37.refs_1_.refs_6_), channel_id=1, source_target_pairs={{4,0},{8,4},{2,6},{12,8},{6,10},{10,14},{5,1},{9,5},{3,7},{13,9},{... | collective-permute-start | bytes 1179656 | tf_op jit(solution)/shard_map/ppermute | solution.py:450
  28.5 6.2 %collective-permute-start.4 = (f32[1336,128]{1,0:T(8,128)S(1)}, f32[1336,128]{1,0:T(8,128)S(1)}, u32[]{:S(2)}, u32[]{:S(2)}) collective-permute-start(f32[1336,128]{1,0:T(8,128)S(1)} %collective-permute-done.head_a.refs_0_), channel_id=1, source_target_pairs={{0,1},{1,0},{2,3},{3,2},{4,5},{5,4},{6,7},{7,6},{8,9},{9,8},{10,11... | collective-permute-start | bytes 2052104 | tf_op jit(solution)/shard_map/ppermute | solution.py:455
  28.5 12.3 %collective-permute-start.5 = (f32[768,128]{1,0:T(8,128)S(1)}, f32[768,128]{1,0:T(8,128)S(1)}, u32[]{:S(2)}, u32[]{:S(2)}) collective-permute-start(f32[768,128]{1,0:T(8,128)S(1)} %get-tuple-element.37.refs_1_.refs_6_), channel_id=1, source_target_pairs={{0,2},{2,0},{4,6},{6,4},{8,10},{10,8},{12,14},{14,12},{1,3},{3,1},... | collective-permute-start | bytes 1179656 | tf_op jit(solution)/shard_map/ppermute | solution.py:440
  31.2 18.4 %collective-permute-start.3 = (f32[1336,128]{1,0:T(8,128)S(1)}, f32[1336,128]{1,0:T(8,128)S(1)}, u32[]{:S(2)}, u32[]{:S(2)}) collective-permute-start(f32[1336,128]{1,0:T(8,128)S(1)} %collective-permute-done.head_a.refs_0_), channel_id=1, source_target_pairs={{6,2},{0,4},{10,6},{4,8},{14,10},{8,12},{7,3},{1,5},{11,7},{5,9},{... | collective-permute-start | bytes 2052104 | tf_op jit(solution)/shard_map/ppermute | solution.py:450
  40.9 4.3 %collective-permute-start.6 = (f32[768,128]{1,0:T(8,128)S(1)}, f32[768,128]{1,0:T(8,128)S(1)}, u32[]{:S(2)}, u32[]{:S(2)}) collective-permute-start(f32[768,128]{1,0:T(8,128)S(1)} %collective-permute-done.5.refs_1_), channel_id=1, source_target_pairs={{0,1},{1,0},{2,3},{3,2},{4,5},{5,4},{6,7},{7,6},{8,9},{9,8},{10,11... | collective-permute-start | bytes 1179656 | tf_op jit(solution)/shard_map/ppermute | solution.py:455
  49.5 3.0 %collective-permute-start.7 = (f32[1336,128]{1,0:T(8,128)S(1)}, f32[1336,128]{1,0:T(8,128)S(1)}, u32[]{:S(2)}, u32[]{:S(2)}) collective-permute-start(f32[1336,128]{1,0:T(8,128)S(1)} %collective-permute-done.3.head_a.refs_0_), channel_id=1, source_target_pairs={{0,1},{1,0},{2,3},{3,2},{4,5},{5,4},{6,7},{7,6},{8,9},{9,8},{10,11... | collective-permute-start | bytes 2052104 | tf_op jit(solution)/shard_map/ppermute | solution.py:455
  50.7 11.1 %collective-permute-start.8 = (f32[768,128]{1,0:T(8,128)S(1)}, f32[768,128]{1,0:T(8,128)S(1)}, u32[]{:S(2)}, u32[]{:S(2)}) collective-permute-start(f32[768,128]{1,0:T(8,128)S(1)} %collective-permute-done.2), channel_id=1, source_target_pairs={{0,2},{2,0},{4,6},{6,4},{8,10},{10,8},{12,14},{14,12},{1,3},{3,1},... | collective-permute-start | bytes 1179656 | tf_op jit(solution)/shard_map/ppermute | solution.py:440
  61.8 1.7 %collective-permute-start.9 = (f32[768,128]{1,0:T(8,128)S(1)}, f32[768,128]{1,0:T(8,128)S(1)}, u32[]{:S(2)}, u32[]{:S(2)}) collective-permute-start(f32[768,128]{1,0:T(8,128)S(1)} %collective-permute-done.8.refs_1_), channel_id=1, source_target_pairs={{0,1},{1,0},{2,3},{3,2},{4,5},{5,4},{6,7},{7,6},{8,9},{9,8},{10,11... | collective-permute-start | bytes 1179656 | tf_op jit(solution)/shard_map/ppermute | solution.py:455
  64.5 6.1 %collective-permute-start.11 = (f32[2048,128]{1,0:T(8,128)S(1)}, f32[2048,128]{1,0:T(8,128)S(1)}, u32[]{:S(2)}, u32[]{:S(2)}) collective-permute-start(f32[2048,128]{1,0:T(8,128)S(1)} %get-tuple-element.54.source), channel_id=1, source_target_pairs={{0,1},{1,0},{2,3},{3,2},{4,5},{5,4},{6,7},{7,6},{8,9},{9,8},{10,11... | collective-permute-start | bytes 3145736 | tf_op jit(solution)/shard_map/ppermute | solution.py:455
  64.7 19.6 %collective-permute-start.10 = (f32[1280,128]{1,0:T(8,128)S(1)}, f32[1280,128]{1,0:T(8,128)S(1)}, u32[]{:S(2)}, u32[]{:S(2)}) collective-permute-start(f32[1280,128]{1,0:T(8,128)S(1)} %get-tuple-element.50.refs_0_.refs_7_), channel_id=1, source_target_pairs={{0,2},{2,0},{4,6},{6,4},{8,10},{10,8},{12,14},{14,12},{1,3},{3,1},... | collective-permute-start | bytes 1966088 | tf_op jit(solution)/shard_map/ppermute | solution.py:440
  69.3 13.3 %collective-permute-start.12 = (f32[768,128]{1,0:T(8,128)S(1)}, f32[768,128]{1,0:T(8,128)S(1)}, u32[]{:S(2)}, u32[]{:S(2)}) collective-permute-start(f32[768,128]{1,0:T(8,128)S(1)} %get-tuple-element.51.refs_1_.refs_8_), channel_id=1, source_target_pairs={{4,0},{8,4},{2,6},{12,8},{6,10},{10,14},{5,1},{9,5},{3,7},{13,9},{... | collective-permute-start | bytes 1179656 | tf_op jit(solution)/shard_map/ppermute | solution.py:450
  84.3 19.5 %collective-permute-start.13 = (f32[1280,128]{1,0:T(8,128)S(1)}, f32[1280,128]{1,0:T(8,128)S(1)}, u32[]{:S(2)}, u32[]{:S(2)}) collective-permute-start(f32[1280,128]{1,0:T(8,128)S(1)} %collective-permute-done.10.refs_0_), channel_id=1, source_target_pairs={{6,2},{0,4},{10,6},{4,8},{14,10},{8,12},{7,3},{1,5},{11,7},{5,9},{... | collective-permute-start | bytes 1966088 | tf_op jit(solution)/shard_map/ppermute | solution.py:450
  90.0 10.5 %collective-permute-start.14 = (f32[768,128]{1,0:T(8,128)S(1)}, f32[768,128]{1,0:T(8,128)S(1)}, u32[]{:S(2)}, u32[]{:S(2)}) collective-permute-start(f32[768,128]{1,0:T(8,128)S(1)} %get-tuple-element.51.refs_1_.refs_8_), channel_id=1, source_target_pairs={{0,2},{2,0},{4,6},{6,4},{8,10},{10,8},{12,14},{14,12},{1,3},{3,1},... | collective-permute-start | bytes 1179656 | tf_op jit(solution)/shard_map/ppermute | solution.py:440
  100.5 9.5 %collective-permute-start.15 = (f32[768,128]{1,0:T(8,128)S(1)}, f32[768,128]{1,0:T(8,128)S(1)}, u32[]{:S(2)}, u32[]{:S(2)}) collective-permute-start(f32[768,128]{1,0:T(8,128)S(1)} %collective-permute-done.12), channel_id=1, source_target_pairs={{0,2},{2,0},{4,6},{6,4},{8,10},{10,8},{12,14},{14,12},{1,3},{3,1},... | collective-permute-start | bytes 1179656 | tf_op jit(solution)/shard_map/ppermute | solution.py:440
  100.8 9.2 %collective-permute-start.18 = (f32[1280,128]{1,0:T(8,128)S(1)}, f32[1280,128]{1,0:T(8,128)S(1)}, u32[]{:S(2)}, u32[]{:S(2)}) collective-permute-start(f32[1280,128]{1,0:T(8,128)S(1)} %collective-permute-done.10.refs_0_), channel_id=1, source_target_pairs={{0,1},{1,0},{2,3},{3,2},{4,5},{5,4},{6,7},{7,6},{8,9},{9,8},{10,11... | collective-permute-start | bytes 1966088 | tf_op jit(solution)/shard_map/ppermute | solution.py:455
  103.8 9.6 %collective-permute-start.16 = (f32[1280,128]{1,0:T(8,128)S(1)}, f32[1280,128]{1,0:T(8,128)S(1)}, u32[]{:S(2)}, u32[]{:S(2)}) collective-permute-start(f32[1280,128]{1,0:T(8,128)S(1)} %collective-permute-done.13.refs_0_), channel_id=1, source_target_pairs={{0,1},{1,0},{2,3},{3,2},{4,5},{5,4},{6,7},{7,6},{8,9},{9,8},{10,11... | collective-permute-start | bytes 1966088 | tf_op jit(solution)/shard_map/ppermute | solution.py:455
  103.8 6.2 %collective-permute-start.19 = (f32[768,128]{1,0:T(8,128)S(1)}, f32[768,128]{1,0:T(8,128)S(1)}, u32[]{:S(2)}, u32[]{:S(2)}) collective-permute-start(f32[768,128]{1,0:T(8,128)S(1)} %collective-permute-done.14.refs_1_), channel_id=1, source_target_pairs={{0,1},{1,0},{2,3},{3,2},{4,5},{5,4},{6,7},{7,6},{8,9},{9,8},{10,11... | collective-permute-start | bytes 1179656 | tf_op jit(solution)/shard_map/ppermute | solution.py:455
  110.0 3.4 %collective-permute-start.17 = (f32[768,128]{1,0:T(8,128)S(1)}, f32[768,128]{1,0:T(8,128)S(1)}, u32[]{:S(2)}, u32[]{:S(2)}) collective-permute-start(f32[768,128]{1,0:T(8,128)S(1)} %collective-permute-done.15.refs_1_), channel_id=1, source_target_pairs={{0,1},{1,0},{2,3},{3,2},{4,5},{5,4},{6,7},{7,6},{8,9},{9,8},{10,11... | collective-permute-start | bytes 1179656 | tf_op jit(solution)/shard_map/ppermute | solution.py:455
  113.3 20.2 %copy-start = (f32[2048,128]{1,0:T(8,128)S(1)}, f32[2048,128]{1,0:T(8,128)}, u32[]{:S(2)}) copy-start(f32[2048,128]{1,0:T(8,128)} %values_hbm.1) | copy-start | bytes 3145732
  114.7 6.4 %collective-permute-start.20 = (f32[8,128]{1,0:T(8,128)S(1)}, f32[8,128]{1,0:T(8,128)S(1)}, u32[]{:S(2)}, u32[]{:S(2)}) collective-permute-start(f32[8,128]{1,0:T(8,128)S(1)} %get-tuple-element.58), channel_id=1, source_target_pairs={{0,2},{2,0},{4,6},{6,4},{8,10},{10,8},{12,14},{14,12},{1,3},{3,1},... | collective-permute-start | bytes 12296 | tf_op jit(solution)/shard_map/ppermute | solution.py:464
  121.1 5.2 %collective-permute-start.21 = (f32[8,128]{1,0:T(8,128)S(1)}, f32[8,128]{1,0:T(8,128)S(1)}, u32[]{:S(2)}, u32[]{:S(2)}) collective-permute-start(f32[8,128]{1,0:T(8,128)S(1)} %add.36), channel_id=1, source_target_pairs={{0,4},{2,6},{4,0},{6,2},{8,12},{10,14},{12,8},{14,10},{1,5},{3,7},... | collective-permute-start | bytes 12296 | tf_op jit(solution)/shard_map/ppermute | solution.py:464
  126.3 4.5 %collective-permute-start.22 = (f32[8,128]{1,0:T(8,128)S(1)}, f32[8,128]{1,0:T(8,128)S(1)}, u32[]{:S(2)}, u32[]{:S(2)}) collective-permute-start(f32[8,128]{1,0:T(8,128)S(1)} %add.37), channel_id=1, source_target_pairs={{0,8},{2,10},{4,12},{6,14},{8,0},{10,2},{12,4},{14,6},{1,9},{3,11}... | collective-permute-start | bytes 12296 | tf_op jit(solution)/shard_map/ppermute | solution.py:464
  130.8 2.7 %collective-permute-start.23 = (f32[8,128]{1,0:T(8,128)S(1)}, f32[8,128]{1,0:T(8,128)S(1)}, u32[]{:S(2)}, u32[]{:S(2)}) collective-permute-start(f32[8,128]{1,0:T(8,128)S(1)} %add.38), channel_id=1, source_target_pairs={{0,1},{1,0},{2,3},{3,2},{4,5},{5,4},{6,7},{7,6},{8,9},{9,8},{10,11... | collective-permute-start | bytes 12296 | tf_op jit(solution)/shard_map/ppermute | solution.py:455

commit v2 on v1

--- a/solution.py
+++ b/solution.py
@@ -9,10 +9,13 @@
 
 LANES = 128
 ROWS = 224
-SLOTS = 72
+OWN_SLOTS = 72
+SLOTS = 40
 UNROLL = 8
 EVAL_UNROLL = 2
 PIECES = 2
+FIRST_SHARE = 9
+LATER_SHARE = 9
 FAR = 1.0e6
 F32 = jnp.float32
 BF16 = jnp.bfloat16
@@ -33,16 +36,16 @@
     return high, low
 
 
-def list_length(points):
-    return 2 * (points // LANES) * -(-points // ROWS) + UNROLL
+def list_length(points, halves):
+    return halves * (points // LANES) * -(-points // ROWS) + UNROLL
 
 
 def header_rows(points):
     return -(-(3 * (points // LANES) + 3) // 8) * 8
 
 
-def piece_sizes(points):
-    large = points // LANES * 5 // 8 * LANES
+def piece_sizes(points, share):
+    large = points // LANES * share // 16 * LANES
     return [large, points - large]
 
 
@@ -161,7 +164,7 @@
         functools.partial(sort_kernel, points),
         out_shape=tuple(
             jax.ShapeDtypeStruct((size + (header if c in (0, PIECES) else 0), width), F32)
-            for c, size in enumerate([*piece_sizes(points), points])
+            for c, size in enumerate([*piece_sizes(points, FIRST_SHARE), points])
         )
         + (
             pltpu.VMEM((4, points + ROWS, LANES), F32),
@@ -211,13 +214,13 @@
 def gather_facts(windows, facts, heads):
     for half, head in enumerate(heads):
         for k in range(3):
-            base = (2 * k + half) * windows
+            base = (len(heads) * k + half) * windows
             facts[base : base + windows, :] = head[k * windows : (k + 1) * windows, :] * 4.0
 
 
-def find_ranges(points, own, other, table, base):
+def find_ranges(points, own, other):
     windows = points // LANES
-    end_row = 3 * windows
+    early, late, mark = 3 * windows, 3 * windows + 1, 3 * windows + 2
     x = other[windows : 2 * windows, :]
     low = jnp.broadcast_to(x[:, 0:1], (windows, LANES))
     high = jnp.broadcast_to(x[:, LANES - 1 : LANES], (windows, LANES))
@@ -234,128 +237,112 @@
     blocks = jnp.zeros((windows, 1), F32)
     for k in range(-(-points // ROWS)):
         blocks = blocks + jnp.where(length > float(k * ROWS), 1.0, 0.0)
-    early, late, mark = end_row, end_row + 1, end_row + 2
     apart = jnp.maximum(
         other[early : early + 1, 0:1] - own[late : late + 1, 0:1],
         own[early : early + 1, 0:1] - other[late : late + 1, 0:1],
     )
     apart = jnp.where(other[mark : mark + 1, 0:1] > 0.5, apart, 2.0)
     blocks = jnp.where(jnp.logical_and(end > begin, jnp.broadcast_to(apart, (windows, 1)) < 1.0), blocks, 0.0)
-    table[base : base + windows, 0:LANES] = jnp.broadcast_to(first, (windows, LANES))
-    table[base : base + windows, LANES:] = jnp.broadcast_to(blocks.astype(jnp.int32), (windows, LANES))
-
-
-def eval_kernel(points, own, head_a, head_b, rows, cache, work, facts, table, table_smem, sem):
+    return jnp.broadcast_to(first * 64 + blocks.astype(jnp.int32), (windows, LANES))
+
+
+def list_tiles(points, own, heads, work, facts, table, table_smem, sem):
     windows = points // LANES
-    for half, head in enumerate((head_a, head_b)):
-        find_ranges(points, own, head, table, half * windows)
+    found = jnp.concatenate([find_ranges(points, own, head) for head in heads], axis=0)
+    lane = lax.broadcasted_iota(jnp.int32, found.shape, 1)
+    sub = lax.broadcasted_iota(jnp.int32, found.shape, 0)
+    table[...] = jnp.sum(jnp.where(lane == sub, found, 0), axis=0, keepdims=True)
     copy = pltpu.make_async_copy(table, table_smem, sem)
     copy.start()
-    gather_facts(windows, facts, (head_a, head_b))
+    gather_facts(windows, facts, heads)
     copy.wait()
-
-    def window(w, slot):
-        first = table_smem[w, 0]
-        blocks = table_smem[w, LANES]
-
-        def block(b, carry):
+    slot = jnp.int32(0)
+    for w in range(len(heads) * windows):
+        packed = table_smem[0, w]
+        first = lax.shift_right_logical(packed, 6)
+        blocks = lax.bitwise_and(packed, 63)
+        for b in range(2):
             work[0, slot + b] = first + b * ROWS
             work[1, slot + b] = w
+
+        @pl.when(blocks > 2)
+        def _(slot=slot, first=first, blocks=blocks, w=w):
+            def block(b, carry):
+                work[0, slot + b] = first + b * ROWS
+                work[1, slot + b] = w
+                return carry
+
+            lax.fori_loop(2, blocks, block, 0)
+
+        slot = slot + blocks
+    for k in range(UNROLL):
+        work[0, slot + k] = points
+        work[1, slot + k] = 0
+    work[2, 0] = slot
+    return slot
+
+
+def keep_tiles(windows, work, facts, rows, cache, step):
+    for k in range(EVAL_UNROLL):
+        s = step * EVAL_UNROLL + k
+        fill_tile(cache.at[s], rows, facts, work[1, s], windows, pl.multiple_of(work[0, s], 16))
+
+
+def kept_shapes(points, halves, slots):
+    return (
+        pltpu.VMEM((slots, ROWS, 2 * LANES), BF16),
+        jax.ShapeDtypeStruct((3, list_length(points, halves)), jnp.int32),
+        jax.ShapeDtypeStruct((3 * halves * (points // LANES), LANES), F32),
+    )
+
+
+def list_scratch():
+    return [pltpu.VMEM((1, LANES), jnp.int32), pltpu.SMEM((1, LANES), jnp.int32), pltpu.SemaphoreType.DMA]
+
+
+def light_cost():
+    return pl.CostEstimate(flops=1_000_000, bytes_accessed=100_000, transcendentals=0)
+
+
+def split_values(points, values, top, pairs):
+    for half, chunks in enumerate(values):
+        for chunk, start, skip, size in spans(chunks, top):
+            base = half * (points // LANES) + start // LANES
+
+            def split(w, carry):
+                high, low = split2(chunk[pl.ds(pl.multiple_of(skip + w * LANES, 8), LANES), :])
+                both = jnp.concatenate([high, low], axis=1)
+                pairs[base + w, 0:LANES, :] = both
+                pairs[base + w, LANES:, :] = both
+                return carry
+
+            lax.fori_loop(0, size // LANES, split, 0)
+
+
+def multiply(work, cache, pairs, acc, step, count):
+    for k in range(count):
+        s = step * count + k
+        at = pl.multiple_of(work[0, s], 16)
+        acc[pl.ds(at, ROWS), :] += jnp.dot(cache[s], pairs[work[1, s]], preferred_element_type=F32)
+
+
+def multiply_rest(windows, work, facts, rows, cache, pairs, acc, tile, total):
+    slots = cache.shape[0]
+
+    @pl.when(total > slots)
+    def _():
+        def again(s, carry):
+            at = pl.multiple_of(work[0, s], 16)
+            w = work[1, s]
+            fill_tile(tile, rows, facts, w, windows, at)
+            acc[pl.ds(at, ROWS), :] += jnp.dot(tile[...], pairs[w], preferred_element_type=F32)
             return carry
 
-        lax.fori_loop(0, blocks, block, 0)
-        return slot + blocks
-
-    total = lax.fori_loop(0, 2 * windows, window, 0)
-    for k in range(UNROLL):
-        work[0, total + k] = points
-        work[1, total + k] = 0
-    work[2, 0] = total
-
-    def slots(step, carry):
-        for k in range(EVAL_UNROLL):
-            s = step * EVAL_UNROLL + k
-            fill_tile(cache.at[s], rows, facts, work[1, s], 2 * windows, pl.multiple_of(work[0, s], 16))
-        return carry
-
-    kept = jnp.minimum(total, SLOTS)
-    lax.fori_loop(0, (kept + EVAL_UNROLL - 1) // EVAL_UNROLL, slots, 0)
-
-
-def eval_pair(points, own, heads, rows):
-    windows = points // LANES
-    return pl.pallas_call(
-        functools.partial(eval_kernel, points),
-        out_shape=(
-            pltpu.VMEM((SLOTS, ROWS, 2 * LANES), BF16),
-            jax.ShapeDtypeStruct((3, list_length(points)), jnp.int32),
-            jax.ShapeDtypeStruct((6 * windows, LANES), F32),
-        ),
-        in_specs=[vmem_spec()] * 4,
-        out_specs=(vmem_spec(), smem_spec(), vmem_spec()),
-        scratch_shapes=[
-            pltpu.VMEM((2 * windows, 2 * LANES), jnp.int32),
-            pltpu.SMEM((2 * windows, 2 * LANES), jnp.int32),
-            pltpu.SemaphoreType.DMA,
-        ],
-        compiler_params=pltpu.CompilerParams(vmem_limit_bytes=4 * MIB),
-        cost_estimate=pl.CostEstimate(flops=1_000_000, bytes_accessed=100_000, transcendentals=0),
-        name="eval_pair",
-    )(own, *heads, rows)
-
-
-def product_kernel(points, headed, counts, marker, work, facts, rows, cache, *refs):
-    groups = []
-    for count in counts:
-        groups.append(refs[:count])
-        refs = refs[count:]
-    first, second, before, given, once, out, sums = groups
-    values = (first, second)
-    acc, pairs, tile = refs
-    windows = points // LANES
-    header = header_rows(points)
-    top = header if headed else 0
-    total = work[2, 0]
-    acc[...] = jnp.zeros_like(acc)
-
-    @pl.when(total > 0)
-    def _():
-        for half in range(2):
-            for chunk, start, skip, size in spans(values[half], top):
-                base = half * windows + start // LANES
-
-                def split(w, carry):
-                    high, low = split2(chunk[pl.ds(pl.multiple_of(skip + w * LANES, 8), LANES), :])
-                    both = jnp.concatenate([high, low], axis=1)
-                    pairs[base + w, 0:LANES, :] = both
-                    pairs[base + w, LANES:, :] = both
-                    return carry
-
-                lax.fori_loop(0, size // LANES, split, 0)
-
-        def slots(step, carry):
-            for k in range(UNROLL):
-                s = step * UNROLL + k
-                at = pl.multiple_of(work[0, s], 16)
-                acc[pl.ds(at, ROWS), :] += jnp.dot(
-                    cache[s], pairs[work[1, s]], preferred_element_type=F32
-                )
-            return carry
-
-        kept = jnp.minimum(total, SLOTS)
-        lax.fori_loop(0, (kept + UNROLL - 1) // UNROLL, slots, 0)
-
-        @pl.when(total > SLOTS)
-        def _():
-            def again(s, carry):
-                at = pl.multiple_of(work[0, s], 16)
-                w = work[1, s]
-                fill_tile(tile, rows, facts, w, 2 * windows, at)
-                acc[pl.ds(at, ROWS), :] += jnp.dot(tile[...], pairs[w], preferred_element_type=F32)
-                return carry
-
-            lax.fori_loop(SLOTS, total, again, 0)
-
+        lax.fori_loop(slots, total, again, 0)
+
+
+def finish(points, header, top, marker, rows, acc, groups):
+    first, (before, given, once, out, sums) = groups[0], groups[-5:]
     marks = [jnp.zeros((8, LANES), F32)] * 5
     for start in range(0, points, LANES):
         here = slice(start, start + LANES)
@@ -376,39 +363,122 @@
             sums[0][k : k + 1, :] = jnp.sum(marks[k], axis=0, keepdims=True)
 
 
+def take_groups(refs, counts):
+    groups = []
+    for count in counts:
+        groups.append(refs[:count])
+        refs = refs[count:]
+    return groups, refs
+
+
+def product_kernel(points, halves, headed, counts, marker, work, facts, rows, cache, *refs):
+    groups, (acc, pairs, tile) = take_groups(refs, counts)
+    header = header_rows(points)
+    top = header if headed else 0
+    total = work[2, 0]
+    acc[...] = jnp.zeros_like(acc)
+
+    @pl.when(total > 0)
+    def _():
+        split_values(points, groups[:halves], top, pairs)
+
+        def slots(step, carry):
+            multiply(work, cache, pairs, acc, step, UNROLL)
+            return carry
+
+        kept = jnp.minimum(total, cache.shape[0])
+        lax.fori_loop(0, (kept + (UNROLL - 1)) // UNROLL, slots, 0)
+        multiply_rest(halves * (points // LANES), work, facts, rows, cache, pairs, acc, tile, total)
+
+    finish(points, header, top, marker, rows, acc, groups)
+
+
+def both_kernel(points, halves, counts, own, rows, *refs):
+    windows = halves * (points // LANES)
+    groups, refs = take_groups(refs, counts)
+    values = groups[:halves]
+    cache, work, facts, acc, pairs, tile, table, table_smem, sem = refs
+    header = header_rows(points)
+    total = list_tiles(points, own, [half[0] for half in values], work, facts, table, table_smem, sem)
+    acc[...] = jnp.zeros_like(acc)
+
+    @pl.when(total > 0)
+    def _():
+        split_values(points, values, header, pairs)
+        kept = jnp.minimum(total, cache.shape[0])
+        steps = (kept + (EVAL_UNROLL - 1)) // EVAL_UNROLL
+        keep_tiles(windows, work, facts, rows, cache, 0)
+
+        def slots(step, carry):
+            multiply(work, cache, pairs, acc, step - 1, EVAL_UNROLL)
+            keep_tiles(windows, work, facts, rows, cache, step)
+            return carry
+
+        lax.fori_loop(1, steps, slots, 0)
+        multiply(work, cache, pairs, acc, steps - 1, EVAL_UNROLL)
+        multiply_rest(windows, work, facts, rows, cache, pairs, acc, tile, total)
+
+    finish(points, header, header, None, rows, acc, groups)
+
+
+def product_scratch(points, halves):
+    return [
+        pltpu.VMEM((points + ROWS, 2 * LANES), F32),
+        pltpu.VMEM((halves * (points // LANES), 2 * LANES, 2 * LANES), BF16),
+        pltpu.VMEM((ROWS, 2 * LANES), BF16),
+    ]
+
+
+def image_shapes(points, sent):
+    sizes = [*(piece_sizes(points, LATER_SHARE) if sent else []), points]
+    return [jax.ShapeDtypeStruct((size, LANES), F32) for size in sizes]
+
+
 def fold(value):
     return jnp.sum(value.reshape(value.shape[0] // 8, 8, LANES), axis=0)
 
 
-def inner_sums(marks, image, given, once):
+def all_sums(marks, image, given, once):
     terms = (given * given, given * once, once * once, given * image, once * image)
     return [mark + fold(term) for mark, term in zip(marks, terms)]
 
 
-def product_pair(points, evaluated, rows, values, headed, before=(), sent=False, marker=None, given=(), once=()):
+def product(points, evaluated, rows, values, before=(), marker=None, given=(), once=()):
     cache, work, facts = evaluated
-    windows = points // LANES
     groups = (*values, before, given, once)
     operands = (facts, rows, cache, *(x for group in groups for x in group))
-    sizes = [*(piece_sizes(points) if sent else []), points]
     sums = int(marker is not None)
-    counts = [len(group) for group in groups] + [len(sizes), sums]
+    counts = [len(group) for group in groups] + [1, sums]
     out = pl.pallas_call(
-        functools.partial(product_kernel, points, headed, counts, marker),
-        out_shape=[jax.ShapeDtypeStruct((size, LANES), F32) for size in sizes]
-        + [jax.ShapeDtypeStruct((8, LANES), F32)] * sums,
+        functools.partial(product_kernel, points, len(values), False, counts, marker),
+        out_shape=image_shapes(points, False) + [jax.ShapeDtypeStruct((8, LANES), F32)] * sums,
         in_specs=[smem_spec()] + [vmem_spec()] * len(operands),
-        out_specs=[vmem_spec()] * (len(sizes) + sums),
-        scratch_shapes=[
-            pltpu.VMEM((points + ROWS, 2 * LANES), F32),
-            pltpu.VMEM((2 * windows, 2 * LANES, 2 * LANES), BF16),
-            pltpu.VMEM((ROWS, 2 * LANES), BF16),
-        ],
+        out_specs=[vmem_spec()] * (1 + sums),
+        scratch_shapes=product_scratch(points, len(values)),
         compiler_params=pltpu.CompilerParams(vmem_limit_bytes=15 * MIB),
-        cost_estimate=pl.CostEstimate(flops=1_000_000, bytes_accessed=100_000, transcendentals=0),
-        name="product_pair",
+        cost_estimate=light_cost(),
+        name="product",
     )(work, *operands)
     return tuple(out)
+
+
+def eval_product(points, own, rows, values, slots, before=(), sent=False):
+    halves = len(values)
+    groups = (*values, before, (), ())
+    operands = (own, rows, *(x for group in groups for x in group))
+    images = image_shapes(points, sent)
+    counts = [len(group) for group in groups] + [len(images), 0]
+    out = pl.pallas_call(
+        functools.partial(both_kernel, points, halves, counts),
+        out_shape=(*images, *kept_shapes(points, halves, slots)),
+        in_specs=[vmem_spec()] * len(operands),
+        out_specs=(*[vmem_spec()] * (len(images) + 1), smem_spec(), vmem_spec()),
+        scratch_shapes=product_scratch(points, halves) + list_scratch(),
+        compiler_params=pltpu.CompilerParams(vmem_limit_bytes=15 * MIB),
+        cost_estimate=light_cost(),
+        name="eval_product",
+    )(*operands)
+    return tuple(out[: len(images)]), tuple(out[len(images) :])
 
 
 def unsort_kernel(points, ranks, source, out):
@@ -430,7 +500,7 @@
         in_specs=[smem_spec(), vmem_spec()],
         out_specs=vmem_spec(),
         compiler_params=pltpu.CompilerParams(vmem_limit_bytes=8 * MIB),
-        cost_estimate=pl.CostEstimate(flops=1_000_000, bytes_accessed=100_000, transcendentals=0),
+        cost_estimate=light_cost(),
         name="unsort",
     )(ranks, source)
 
@@ -472,10 +542,12 @@
     return steps
 
 
-def total(value):
-    for step in [1] + far_strides():
+def total(value, beside):
+    value = value + core_swap(value)
+    steps = [1] + far_strides()
+    for step in steps[:-1]:
         value = stride_sum(value, step)
-    return value + core_swap(value)
+    return stride_sum(after(value, beside), steps[-1])
 
 
 def local(coords, anomalies, noise_var):
@@ -486,39 +558,33 @@
     near = [pair_swap(c) for c in given]
     turned = pair_shift(given[1], 1)
     mates = core_swap(whole)
-    own_eval = eval_pair(points, given[0], (given[0], mates), rows)
-    image = product_pair(points, own_eval, rows, (given, (after(mates, own_eval[1]),)), True)
+    image, own_eval = eval_product(points, given[0], rows, (given, (mates,)), OWN_SLOTS)
     near[0] = after(near[0], image[0], turned)
     far = [pair_shift(near[0])]
-    near_mates = [core_swap(near[0])]
-    near_eval = eval_pair(points, given[0], (near[0], near_mates[0]), rows)
-    near[1] = after(near[1], near_eval[1])
-    far.append(pair_swap(after(turned, near[1])))
-    near_mates.append(core_swap(near[1]))
-    image = product_pair(points, near_eval, rows, (near, near_mates), True, image)
-    far[0] = after(far[0], image[0])
-    far_mates = [core_swap(far[0])]
-    far_eval = eval_pair(points, given[0], (far[0], far_mates[0]), rows)
-    far[1] = after(far[1], far_eval[1])
-    far_mates.append(core_swap(far[1]))
-    *once, whole = product_pair(points, far_eval, rows, (far, far_mates), True, image, True)
+    far.append(pair_swap(after(turned, near[1], near[0])))
+    near_mates = [core_swap(c) for c in near]
+    image, near_eval = eval_product(points, given[0], rows, (near,), SLOTS, image)
+    far = [after(far[0], image[0], far[1]), far[1]]
+    far_mates = [core_swap(c) for c in far]
+    image, far_eval = eval_product(points, given[0], rows, (far,), SLOTS, image)
+    (*once, whole), mate_eval = eval_product(points, given[0], rows, (near_mates, far_mates), SLOTS, image, True)
 
     near = [pair_swap(c) for c in once]
     turned = pair_shift(once[1], 1)
     mates = core_swap(whole)
     image0 = unsort(ranks, after(whole, mates))
-    image = product_pair(points, own_eval, rows, (once, (after(mates, image0),)), False)
+    image = product(points, own_eval, rows, (once, (after(mates, image0),)))
     near[0] = after(near[0], image[0], turned)
     far = [pair_shift(near[0])]
-    near_mates = [core_swap(near[0])]
     far.append(pair_swap(after(turned, near[1], near[0])))
-    near_mates.append(core_swap(near[1]))
-    image = product_pair(points, near_eval, rows, (near, near_mates), False, image)
-    far_mates = [core_swap(c) for c in far]
-    twice, sums = product_pair(points, far_eval, rows, (far, far_mates), False, image, False, inner_sums, given, once)
+    near_mates = [core_swap(c) for c in near]
+    image = product(points, near_eval, rows, (near,), image)
+    far_mates = [core_swap(far[0]), core_swap(after(far[1], image[0]))]
+    image = product(points, far_eval, rows, (far,), image)
+    twice, sums = product(points, mate_eval, rows, (near_mates, far_mates), image, all_sums, given, once)
     image1 = unsort(ranks, twice)
 
-    sums = total(sums)
+    sums = total(sums, image1)
     rr0, curve0, once_once, given_twice, once_twice = [sums[k : k + 1] for k in range(5)]
     alpha0 = rr0 / curve0
     rr1 = rr0 - 2.0 * alpha0 * curve0 + alpha0 * alpha0 * once_once

time: 136 us -> 123 us (0.904)
  waiting for transfers between devices: 43.7 us -> 29.2 us
  starting transfers between devices: 37.7 us -> 44.1 us
  Pallas kernels: 51.2 us -> 47 us
    ppermute x6, waiting for transfers between devices: 24.9 us -> 17 us  [pair_swap(): return lax.ppermute(block, 'tm', [(i, i ^ 1) for i in range(count)])]
    ppermute x6, starting transfers between devices: 10.2 us -> 17.4 us  [pair_swap(): return lax.ppermute(block, 'tm', [(i, i ^ 1) for i in range(count)])]
    pallas_call x9 -> x8, Pallas kernels: 37.1 us -> 33 us  [the longest x4 22.2 us: eval_product(): pl.pallas_call(functools.partial(both_kernel, points, halves, counts), ou...]
    ppermute x11, starting transfers between devices: 5.46 us -> 9.28 us  [core_swap(): return lax.ppermute(block, 'tile', [(i, i ^ 1) for i in range(count)])]
    ppermute x3, starting transfers between devices: 10.3 us -> 7.64 us  [stride_sum(): lax.ppermute(value, 'tm', [(i, i ^ step) for i in range(count)])]
    ppermute x3, waiting for transfers between devices: 5.84 us -> 3.41 us  [stride_sum(): lax.ppermute(value, 'tm', [(i, i ^ step) for i in range(count)])]
    ppermute x4, waiting for transfers between devices: 8.15 us -> 6.03 us  [pair_shift(): return lax.ppermute(block, 'tm', route)]
    ppermute x11, waiting for transfers between devices: 4.83 us -> 2.78 us  [core_swap(): return lax.ppermute(block, 'tile', [(i, i ^ 1) for i in range(count)])]
  transfers between devices with their start and end apart: 24 -> 24, of which waited for: 15 -> 12; matrix products, arithmetic and copies ran while one was open for 0% -> 0% of each run, Pallas kernels for 30% -> 28%
where the time goes in v2:
time: 123 us
  Pallas kernels  47 us (38%)
  starting transfers between devices  44.1 us (36%)
  waiting for transfers between devices  29.2 us (24%)
  other arithmetic  1.85 us (2%)
    pallas_call x4, Pallas kernels, eval_product(): pl.pallas_call(functools.partial(both_kernel, points, halves, counts), ou...  22.2 us
    ppermute x6, starting transfers between devices, pair_swap(): return lax.ppermute(block, 'tm', [(i, i ^ 1) for i in range(count)])  17.4 us
    ppermute x6, waiting for transfers between devices, pair_swap(): return lax.ppermute(block, 'tm', [(i, i ^ 1) for i in range(count)])  17 us
    pallas_call x4, Pallas kernels, product(): pl.pallas_call(functools.partial(product_kernel, points, len(values), Fal...  10.7 us
    ppermute x4, starting transfers between devices, pair_shift(): return lax.ppermute(block, 'tm', route)  9.77 us
    ppermute x11, starting transfers between devices, core_swap(): return lax.ppermute(block, 'tile', [(i, i ^ 1) for i in range(count)])  9.28 us
    pallas_call x1, Pallas kernels, sort_points(): pl.pallas_call(functools.partial(sort_kernel, points), out_shape=tuple((j...  8.76 us
    ppermute x3, starting transfers between devices, stride_sum(): lax.ppermute(value, 'tm', [(i, i ^ step) for i in range(count)])  7.64 us
  transfers between devices with their start and end apart: 24, of which 12 were waited for; matrix products, arithmetic and copies ran while one was open for 0% of the time, Pallas kernels for 28%

profile of v2, /device:TPU:0, one launch (start us, length us, event | category | flops | bytes accessed | tf_op | source)
XLA Modules:
  0.0 123.0 jit_solution(17526507750983155187)
XLA Ops:
  0.6 8.8 %sort_points.1 = (f32[1208,128]{1,0:T(8,128)S(1)}, f32[896,128]{1,0:T(8,128)S(1)}, f32[2104,128]{1,0:T(8,128)S(1)}, f32[4,2272,128]{2,1,0:T(8,128)S(1)}, s32[1,2048]{1,0:T(1,128)S(1)}) custom-call(f32[3,2048]{1,0:T(4,128)} %coords_hbm.1, f32[1,2048]{1,0:T(1,128)} %bitcast.5, f32[2048,128]{1,0:T(8,128)} %values_hbm.1), custom_call_target="tpu_custom_call" | custom-call | tf_op jit(solution)/shard_map/sort_points/pallas_call | solution.py:163
  9.9 2.6 %collective-permute-start = (f32[1208,128]{1,0:T(8,128)S(1)}, f32[1208,128]{1,0:T(8,128)S(1)}, u32[]{:S(2)}, u32[]{:S(2)}) collective-permute-start(f32[1208,128]{1,0:T(8,128)S(1)} %get-tuple-element.36.own.refs_0_.refs_5_), channel_id=1, source_target_pairs={{0,2},{2,0},{4,6},{6,4},{8,10},{10,8},{12,14},{14,12},{1,3},{3,1},... | collective-permute-start | bytes 1855496 | tf_op jit(solution)/shard_map/ppermute | solution.py:510
  13.8 2.8 %collective-permute-start.4 = (f32[896,128]{1,0:T(8,128)S(1)}, f32[896,128]{1,0:T(8,128)S(1)}, u32[]{:S(2)}, u32[]{:S(2)}) collective-permute-start(f32[896,128]{1,0:T(8,128)S(1)} %get-tuple-element.38.refs_1_.refs_6_), channel_id=1, source_target_pairs={{0,2},{2,0},{4,6},{6,4},{8,10},{10,8},{12,14},{14,12},{1,3},{3,1},... | collective-permute-start | bytes 1376264 | tf_op jit(solution)/shard_map/ppermute | solution.py:510
  16.6 11.8 %eval_product.4 = (f32[2048,128]{1,0:T(8,128)S(1)}, bf16[72,224,256]{2,1,0:T(8,128)(2,1)S(1)}, s32[3,328]{1,0:T(4,128)S(1)}, f32[96,128]{1,0:T(8,128)S(1)}) custom-call(f32[1208,128]{1,0:T(8,128)S(1)} %get-tuple-element.36.own.refs_0_.refs_5_, f32[4,2272,128]{2,1,0:T(8,128)S(1)} %get-tuple-element.37.rows, ...), custom_call_target="tpu_custom_call" | custom-call | flops 1000000 | bytes 100000 | tf_op jit(solution)/shard_map/eval_product/pallas_call | solution.py:471
  28.4 3.2 %collective-permute-start.6 = (f32[1208,128]{1,0:T(8,128)S(1)}, f32[1208,128]{1,0:T(8,128)S(1)}, u32[]{:S(2)}, u32[]{:S(2)}) collective-permute-start(f32[1208,128]{1,0:T(8,128)S(1)} %collective-permute-done.refs_0_), channel_id=1, source_target_pairs={{6,2},{0,4},{10,6},{4,8},{14,10},{8,12},{7,3},{1,5},{11,7},{5,9},{... | collective-permute-start | bytes 1855496 | tf_op jit(solution)/shard_map/ppermute | solution.py:520
  31.7 5.2 %collective-permute-done.4.refs_1_ = f32[896,128]{1,0:T(8,128)S(1)} collective-permute-done((f32[896,128]{1,0:T(8,128)S(1)}, f32[896,128]{1,0:T(8,128)S(1)}, u32[]{:S(2)}, u32[]{:S(2)}) %collective-permute-start.4) | collective-permute-done | bytes 458784 | tf_op jit(solution)/shard_map/ppermute | solution.py:510
  36.9 1.8 %collective-permute-start.7 = (f32[896,128]{1,0:T(8,128)S(1)}, f32[896,128]{1,0:T(8,128)S(1)}, u32[]{:S(2)}, u32[]{:S(2)}) collective-permute-start(f32[896,128]{1,0:T(8,128)S(1)} %collective-permute-done.2), channel_id=1, source_target_pairs={{0,2},{2,0},{4,6},{6,4},{8,10},{10,8},{12,14},{14,12},{1,3},{3,1},... | collective-permute-start | bytes 1376264 | tf_op jit(solution)/shard_map/ppermute | solution.py:510
  38.6 6.6 %eval_product.5 = (f32[2048,128]{1,0:T(8,128)S(1)}, bf16[40,224,256]{2,1,0:T(8,128)(2,1)S(1)}, s32[3,168]{1,0:T(4,128)S(1)}, f32[48,128]{1,0:T(8,128)S(1)}) custom-call(f32[1208,128]{1,0:T(8,128)S(1)} %get-tuple-element.36.own.refs_0_.refs_5_, f32[4,2272,128]{2,1,0:T(8,128)S(1)} %get-tuple-element.37.rows, f32[1208,128]{1,0:T(8,128)S(1)} %collective-permute-done.refs_0_, ...), custom_call_target="tpu_custom_call" | custom-call | flops 1000000 | bytes 100000 | tf_op jit(solution)/shard_map/eval_product/pallas_call | solution.py:471
  45.3 3.9 %collective-permute-done.7.refs_1_ = f32[896,128]{1,0:T(8,128)S(1)} collective-permute-done((f32[896,128]{1,0:T(8,128)S(1)}, f32[896,128]{1,0:T(8,128)S(1)}, u32[]{:S(2)}, u32[]{:S(2)}) %collective-permute-start.7) | collective-permute-done | bytes 458784 | tf_op jit(solution)/shard_map/ppermute | solution.py:510
  49.7 1.8 %eval_product.6 = (f32[2048,128]{1,0:T(8,128)S(1)}, bf16[40,224,256]{2,1,0:T(8,128)(2,1)S(1)}, s32[3,168]{1,0:T(4,128)S(1)}, f32[48,128]{1,0:T(8,128)S(1)}) custom-call(f32[1208,128]{1,0:T(8,128)S(1)} %get-tuple-element.36.own.refs_0_.refs_5_, f32[4,2272,128]{2,1,0:T(8,128)S(1)} %get-tuple-element.37.rows, f32[1208,128]{1,0:T(8,128)S(1)} %collective-permute-done.6.refs_0_, ...), custom_call_target="tpu_custom_call" | custom-call | flops 1000000 | bytes 100000 | tf_op jit(solution)/shard_map/eval_product/pallas_call | solution.py:471
  52.5 2.0 %eval_product.7 = (f32[1152,128]{1,0:T(8,128)S(1)}, f32[896,128]{1,0:T(8,128)S(1)}, f32[2048,128]{1,0:T(8,128)S(1)}, bf16[40,224,256]{2,1,0:T(8,128)(2,1)S(1)}, ...) custom-call(f32[1208,128]{1,0:T(8,128)S(1)} %get-tuple-element.36.own.refs_0_.refs_5_, ...), custom_call_target="tpu_custom_call" | custom-call | flops 1000000 | bytes 100000 | tf_op jit(solution)/shard_map/eval_product/pallas_call | solution.py:471
  54.5 5.3 %collective-permute-start.11 = (f32[2048,128]{1,0:T(8,128)S(1)}, f32[2048,128]{1,0:T(8,128)S(1)}, u32[]{:S(2)}, u32[]{:S(2)}) collective-permute-start(f32[2048,128]{1,0:T(8,128)S(1)} %get-tuple-element.56.source), channel_id=1, source_target_pairs={{0,1},{1,0},{2,3},{3,2},{4,5},{5,4},{6,7},{7,6},{8,9},{9,8},{10,11... | collective-permute-start | bytes 3145736 | tf_op jit(solution)/shard_map/ppermute | solution.py:525
  59.8 5.8 %collective-permute-start.10 = (f32[1152,128]{1,0:T(8,128)S(1)}, f32[1152,128]{1,0:T(8,128)S(1)}, u32[]{:S(2)}, u32[]{:S(2)}) collective-permute-start(f32[1152,128]{1,0:T(8,128)S(1)} %get-tuple-element.49.refs_0_.refs_7_), channel_id=1, source_target_pairs={{0,2},{2,0},{4,6},{6,4},{8,10},{10,8},{12,14},{14,12},{1,3},{3,1},... | collective-permute-start | bytes 1769480 | tf_op jit(solution)/shard_map/ppermute | solution.py:510
  66.9 2.7 %collective-permute-start.14 = (f32[896,128]{1,0:T(8,128)S(1)}, f32[896,128]{1,0:T(8,128)S(1)}, u32[]{:S(2)}, u32[]{:S(2)}) collective-permute-start(f32[896,128]{1,0:T(8,128)S(1)} %get-tuple-element.53.refs_1_.refs_8_), channel_id=1, source_target_pairs={{0,2},{2,0},{4,6},{6,4},{8,10},{10,8},{12,14},{14,12},{1,3},{3,1},... | collective-permute-start | bytes 1376264 | tf_op jit(solution)/shard_map/ppermute | solution.py:510
  69.6 2.7 %unsort.2 = f32[2048,128]{1,0:T(8,128)S(1)} custom-call(s32[1,2048]{1,0:T(1,128)S(1)} %get-tuple-element.55.ranks, f32[2048,128]{1,0:T(8,128)S(1)} %get-tuple-element.56.source), custom_call_target="tpu_custom_call" | custom-call | flops 1000000 | bytes 100000 | tf_op jit(solution)/shard_map/unsort/pallas_call | solution.py:497
  72.3 5.5 %product.4.refs_2_ = f32[2048,128]{1,0:T(8,128)S(1)} custom-call(s32[3,328]{1,0:T(4,128)S(1)} %get-tuple-element.50.work, f32[96,128]{1,0:T(8,128)S(1)} %get-tuple-element.51.facts, f32[4,2272,128]{2,1,0:T(8,128)S(1)} %get-tuple-element.37.rows, bf16[72,224,256]{2,1,0:T(8,128)(2,1)S(1)} %get-tuple-element.52.cache, ...), custom_call_target="tpu_custom_call" | custom-call | flops 1000000 | bytes 100000 | tf_op jit(solution)/shard_map/product/pallas_call | solution.py:452
  77.7 2.0 %collective-permute-done.12 = f32[896,128]{1,0:T(8,128)S(1)} collective-permute-done((f32[896,128]{1,0:T(8,128)S(1)}, f32[896,128]{1,0:T(8,128)S(1)}, u32[]{:S(2)}, u32[]{:S(2)}) %collective-permute-start.12) | collective-permute-done | bytes 458784 | tf_op jit(solution)/shard_map/ppermute | solution.py:520
  79.7 4.0 %collective-permute-start.16 = (f32[1152,128]{1,0:T(8,128)S(1)}, f32[1152,128]{1,0:T(8,128)S(1)}, u32[]{:S(2)}, u32[]{:S(2)}) collective-permute-start(f32[1152,128]{1,0:T(8,128)S(1)} %collective-permute-done.10.refs_0_), channel_id=1, source_target_pairs={{6,2},{0,4},{10,6},{4,8},{14,10},{8,12},{7,3},{1,5},{11,7},{5,9},{... | collective-permute-start | bytes 1769480 | tf_op jit(solution)/shard_map/ppermute | solution.py:520
  83.7 5.3 %collective-permute-done.14.refs_1_ = f32[896,128]{1,0:T(8,128)S(1)} collective-permute-done((f32[896,128]{1,0:T(8,128)S(1)}, f32[896,128]{1,0:T(8,128)S(1)}, u32[]{:S(2)}, u32[]{:S(2)}) %collective-permute-start.14) | collective-permute-done | bytes 458784 | tf_op jit(solution)/shard_map/ppermute | solution.py:510
  89.0 1.7 %collective-permute-start.18 = (f32[896,128]{1,0:T(8,128)S(1)}, f32[896,128]{1,0:T(8,128)S(1)}, u32[]{:S(2)}, u32[]{:S(2)}) collective-permute-start(f32[896,128]{1,0:T(8,128)S(1)} %collective-permute-done.12), channel_id=1, source_target_pairs={{0,2},{2,0},{4,6},{6,4},{8,10},{10,8},{12,14},{14,12},{1,3},{3,1},... | collective-permute-start | bytes 1376264 | tf_op jit(solution)/shard_map/ppermute | solution.py:510
  90.8 4.0 %collective-permute-done.16.refs_0_ = f32[1152,128]{1,0:T(8,128)S(1)} collective-permute-done((f32[1152,128]{1,0:T(8,128)S(1)}, f32[1152,128]{1,0:T(8,128)S(1)}, u32[]{:S(2)}, u32[]{:S(2)}) %collective-permute-start.16) | collective-permute-done | bytes 589856 | tf_op jit(solution)/shard_map/ppermute | solution.py:520
  95.3 3.1 %product.5.refs_2_ = f32[2048,128]{1,0:T(8,128)S(1)} custom-call(s32[3,168]{1,0:T(4,128)S(1)} %get-tuple-element.60.work, f32[48,128]{1,0:T(8,128)S(1)} %get-tuple-element.61.facts, f32[4,2272,128]{2,1,0:T(8,128)S(1)} %get-tuple-element.37.rows, bf16[40,224,256]{2,1,0:T(8,128)(2,1)S(1)} %get-tuple-element.62.cache, ...), custom_call_target="tpu_custom_call" | custom-call | flops 1000000 | bytes 100000 | tf_op jit(solution)/shard_map/product/pallas_call | solution.py:452
  98.4 2.6 %collective-permute-done.18.refs_1_ = f32[896,128]{1,0:T(8,128)S(1)} collective-permute-done((f32[896,128]{1,0:T(8,128)S(1)}, f32[896,128]{1,0:T(8,128)S(1)}, u32[]{:S(2)}, u32[]{:S(2)}) %collective-permute-start.18) | collective-permute-done | bytes 458784 | tf_op jit(solution)/shard_map/ppermute | solution.py:510
  102.8 1.3 %product.7 = (f32[2048,128]{1,0:T(8,128)S(1)}, f32[8,128]{1,0:T(8,128)S(1)}) custom-call(s32[3,328]{1,0:T(4,128)S(1)} %get-tuple-element.46.work, f32[96,128]{1,0:T(8,128)S(1)} %get-tuple-element.47.facts, f32[4,2272,128]{2,1,0:T(8,128)S(1)} %get-tuple-element.37.rows, bf16[40,224,256]{2,1,0:T(8,128)(2,1)S(1)} %get-tuple-element.48.cache, ...), custom_call_target="tpu_custom_call" | custom-call | flops 1000000 | bytes 100000 | tf_op jit(solution)/shard_map/product/pallas_call | solution.py:452
  104.1 2.4 %collective-permute-start.20 = (f32[8,128]{1,0:T(8,128)S(1)}, f32[8,128]{1,0:T(8,128)S(1)}, u32[]{:S(2)}, u32[]{:S(2)}) collective-permute-start(f32[8,128]{1,0:T(8,128)S(1)} %get-tuple-element.67), channel_id=1, source_target_pairs={{0,1},{1,0},{2,3},{3,2},{4,5},{5,4},{6,7},{7,6},{8,9},{9,8},{10,11... | collective-permute-start | bytes 12296 | tf_op jit(solution)/shard_map/ppermute | solution.py:525
  107.4 2.9 %collective-permute-start.21 = (f32[8,128]{1,0:T(8,128)S(1)}, f32[8,128]{1,0:T(8,128)S(1)}, u32[]{:S(2)}, u32[]{:S(2)}) collective-permute-start(f32[8,128]{1,0:T(8,128)S(1)} %add.36), channel_id=1, source_target_pairs={{0,2},{2,0},{4,6},{6,4},{8,10},{10,8},{12,14},{14,12},{1,3},{3,1},... | collective-permute-start | bytes 12296 | tf_op jit(solution)/shard_map/ppermute | solution.py:534
  110.3 1.6 %collective-permute-done.21 = f32[8,128]{1,0:T(8,128)S(1)} collective-permute-done((f32[8,128]{1,0:T(8,128)S(1)}, f32[8,128]{1,0:T(8,128)S(1)}, u32[]{:S(2)}, u32[]{:S(2)}) %collective-permute-start.21) | collective-permute-done | bytes 4128 | tf_op jit(solution)/shard_map/ppermute | solution.py:534
  111.9 2.0 %collective-permute-start.22 = (f32[8,128]{1,0:T(8,128)S(1)}, f32[8,128]{1,0:T(8,128)S(1)}, u32[]{:S(2)}, u32[]{:S(2)}) collective-permute-start(f32[8,128]{1,0:T(8,128)S(1)} %add.37), channel_id=1, source_target_pairs={{0,4},{2,6},{4,0},{6,2},{8,12},{10,14},{12,8},{14,10},{1,5},{3,7},... | collective-permute-start | bytes 12296 | tf_op jit(solution)/shard_map/ppermute | solution.py:534
  113.9 2.7 %unsort.3 = f32[2048,128]{1,0:T(8,128)S(1)} custom-call(s32[1,2048]{1,0:T(1,128)S(1)} %get-tuple-element.55.ranks, f32[2048,128]{1,0:T(8,128)S(1)} %get-tuple-element.68.source), custom_call_target="tpu_custom_call" | custom-call | flops 1000000 | bytes 100000 | tf_op jit(solution)/shard_map/unsort/pallas_call | solution.py:497
  116.6 2.7 %collective-permute-start.23 = (f32[8,128]{1,0:T(8,128)S(1)}, f32[8,128]{1,0:T(8,128)S(1)}, u32[]{:S(2)}, u32[]{:S(2)}) collective-permute-start(f32[8,128]{1,0:T(8,128)S(1)} %add.38), channel_id=1, source_target_pairs={{0,8},{2,10},{4,12},{6,14},{8,0},{10,2},{12,4},{14,6},{1,9},{3,11}... | collective-permute-start | bytes 12296 | tf_op jit(solution)/shard_map/ppermute | solution.py:534
  119.3 1.8 %collective-permute-done.23 = f32[8,128]{1,0:T(8,128)S(1)} collective-permute-done((f32[8,128]{1,0:T(8,128)S(1)}, f32[8,128]{1,0:T(8,128)S(1)}, u32[]{:S(2)}, u32[]{:S(2)}) %collective-permute-start.23) | collective-permute-done | bytes 4128 | tf_op jit(solution)/shard_map/ppermute | solution.py:534
  121.2 1.8 %multiply_subtract_fusion = (f32[2048,128]{1,0:T(8,128)}, f32[2048,128]{1,0:T(8,128)}) fusion(f32[2048,128]{1,0:T(8,128)S(1)} %unsort.2, f32[2048,128]{1,0:T(8,128)S(1)} %unsort.3, f32[2048,128]{1,0:T(8,128)S(1)} %copy-done, f32[128]{0:T(128)S(1)} %bitcast.7, f32[128]{0:T(128)S(1)} %get-tuple-element.70, f32[128]{0:T(128)S(1)} %bitcast.6), kind=kLoop, calls=%fused_computation | loop fusion | flops 3407872 | bytes 5244416 | tf_op jit(solution)/shard_map/sub | solution.py:598
  (36 shorter events, 7.9 us)
Async XLA Ops:
  9.4 7.2 %collective-permute-start.1 = (f32[2104,128]{1,0:T(8,128)S(1)}, f32[2104,128]{1,0:T(8,128)S(1)}, u32[]{:S(2)}, u32[]{:S(2)}) collective-permute-start(f32[2104,128]{1,0:T(8,128)S(1)} %get-tuple-element.39), channel_id=1, source_target_pairs={{0,1},{1,0},{2,3},{3,2},{4,5},{5,4},{6,7},{7,6},{8,9},{9,8},{10,11... | collective-permute-start | bytes 3231752 | tf_op jit(solution)/shard_map/ppermute | solution.py:525
  9.9 18.5 %collective-permute-start = (f32[1208,128]{1,0:T(8,128)S(1)}, f32[1208,128]{1,0:T(8,128)S(1)}, u32[]{:S(2)}, u32[]{:S(2)}) collective-permute-start(f32[1208,128]{1,0:T(8,128)S(1)} %get-tuple-element.36.own.refs_0_.refs_5_), channel_id=1, source_target_pairs={{0,2},{2,0},{4,6},{6,4},{8,10},{10,8},{12,14},{14,12},{1,3},{3,1},... | collective-permute-start | bytes 1855496 | tf_op jit(solution)/shard_map/ppermute | solution.py:510
  12.5 15.9 %collective-permute-start.2 = (f32[896,128]{1,0:T(8,128)S(1)}, f32[896,128]{1,0:T(8,128)S(1)}, u32[]{:S(2)}, u32[]{:S(2)}) collective-permute-start(f32[896,128]{1,0:T(8,128)S(1)} %get-tuple-element.38.refs_1_.refs_6_), channel_id=1, source_target_pairs={{4,0},{8,4},{2,6},{12,8},{6,10},{10,14},{5,1},{9,5},{3,7},{13,9},{... | collective-permute-start | bytes 1376264 | tf_op jit(solution)/shard_map/ppermute | solution.py:520
  13.8 23.1 %collective-permute-start.4 = (f32[896,128]{1,0:T(8,128)S(1)}, f32[896,128]{1,0:T(8,128)S(1)}, u32[]{:S(2)}, u32[]{:S(2)}) collective-permute-start(f32[896,128]{1,0:T(8,128)S(1)} %get-tuple-element.38.refs_1_.refs_6_), channel_id=1, source_target_pairs={{0,2},{2,0},{4,6},{6,4},{8,10},{10,8},{12,14},{14,12},{1,3},{3,1},... | collective-permute-start | bytes 1376264 | tf_op jit(solution)/shard_map/ppermute | solution.py:510
  28.4 20.7 %collective-permute-start.6 = (f32[1208,128]{1,0:T(8,128)S(1)}, f32[1208,128]{1,0:T(8,128)S(1)}, u32[]{:S(2)}, u32[]{:S(2)}) collective-permute-start(f32[1208,128]{1,0:T(8,128)S(1)} %collective-permute-done.refs_0_), channel_id=1, source_target_pairs={{6,2},{0,4},{10,6},{4,8},{14,10},{8,12},{7,3},{1,5},{11,7},{5,9},{... | collective-permute-start | bytes 1855496 | tf_op jit(solution)/shard_map/ppermute | solution.py:520
  36.9 12.3 %collective-permute-start.7 = (f32[896,128]{1,0:T(8,128)S(1)}, f32[896,128]{1,0:T(8,128)S(1)}, u32[]{:S(2)}, u32[]{:S(2)}) collective-permute-start(f32[896,128]{1,0:T(8,128)S(1)} %collective-permute-done.2), channel_id=1, source_target_pairs={{0,2},{2,0},{4,6},{6,4},{8,10},{10,8},{12,14},{14,12},{1,3},{3,1},... | collective-permute-start | bytes 1376264 | tf_op jit(solution)/shard_map/ppermute | solution.py:510
  38.6 13.2 %collective-permute-start.3 = (f32[1208,128]{1,0:T(8,128)S(1)}, f32[1208,128]{1,0:T(8,128)S(1)}, u32[]{:S(2)}, u32[]{:S(2)}) collective-permute-start(f32[1208,128]{1,0:T(8,128)S(1)} %collective-permute-done.refs_0_), channel_id=1, source_target_pairs={{0,1},{1,0},{2,3},{3,2},{4,5},{5,4},{6,7},{7,6},{8,9},{9,8},{10,11... | collective-permute-start | bytes 1855496 | tf_op jit(solution)/shard_map/ppermute | solution.py:525
  49.2 3.4 %collective-permute-start.8 = (f32[1208,128]{1,0:T(8,128)S(1)}, f32[1208,128]{1,0:T(8,128)S(1)}, u32[]{:S(2)}, u32[]{:S(2)}) collective-permute-start(f32[1208,128]{1,0:T(8,128)S(1)} %collective-permute-done.6.refs_0_), channel_id=1, source_target_pairs={{0,1},{1,0},{2,3},{3,2},{4,5},{5,4},{6,7},{7,6},{8,9},{9,8},{10,11... | collective-permute-start | bytes 1855496 | tf_op jit(solution)/shard_map/ppermute | solution.py:525
  49.2 2.7 %collective-permute-start.5 = (f32[896,128]{1,0:T(8,128)S(1)}, f32[896,128]{1,0:T(8,128)S(1)}, u32[]{:S(2)}, u32[]{:S(2)}) collective-permute-start(f32[896,128]{1,0:T(8,128)S(1)} %collective-permute-done.4.refs_1_), channel_id=1, source_target_pairs={{0,1},{1,0},{2,3},{3,2},{4,5},{5,4},{6,7},{7,6},{8,9},{9,8},{10,11... | collective-permute-start | bytes 1376264 | tf_op jit(solution)/shard_map/ppermute | solution.py:525
  49.7 2.8 %collective-permute-start.9 = (f32[896,128]{1,0:T(8,128)S(1)}, f32[896,128]{1,0:T(8,128)S(1)}, u32[]{:S(2)}, u32[]{:S(2)}) collective-permute-start(f32[896,128]{1,0:T(8,128)S(1)} %collective-permute-done.7.refs_1_), channel_id=1, source_target_pairs={{0,1},{1,0},{2,3},{3,2},{4,5},{5,4},{6,7},{7,6},{8,9},{9,8},{10,11... | collective-permute-start | bytes 1376264 | tf_op jit(solution)/shard_map/ppermute | solution.py:525
  54.5 15.1 %collective-permute-start.11 = (f32[2048,128]{1,0:T(8,128)S(1)}, f32[2048,128]{1,0:T(8,128)S(1)}, u32[]{:S(2)}, u32[]{:S(2)}) collective-permute-start(f32[2048,128]{1,0:T(8,128)S(1)} %get-tuple-element.56.source), channel_id=1, source_target_pairs={{0,1},{1,0},{2,3},{3,2},{4,5},{5,4},{6,7},{7,6},{8,9},{9,8},{10,11... | collective-permute-start | bytes 3145736 | tf_op jit(solution)/shard_map/ppermute | solution.py:525
  59.8 19.9 %collective-permute-start.10 = (f32[1152,128]{1,0:T(8,128)S(1)}, f32[1152,128]{1,0:T(8,128)S(1)}, u32[]{:S(2)}, u32[]{:S(2)}) collective-permute-start(f32[1152,128]{1,0:T(8,128)S(1)} %get-tuple-element.49.refs_0_.refs_7_), channel_id=1, source_target_pairs={{0,2},{2,0},{4,6},{6,4},{8,10},{10,8},{12,14},{14,12},{1,3},{3,1},... | collective-permute-start | bytes 1769480 | tf_op jit(solution)/shard_map/ppermute | solution.py:510
  65.6 14.1 %collective-permute-start.12 = (f32[896,128]{1,0:T(8,128)S(1)}, f32[896,128]{1,0:T(8,128)S(1)}, u32[]{:S(2)}, u32[]{:S(2)}) collective-permute-start(f32[896,128]{1,0:T(8,128)S(1)} %get-tuple-element.53.refs_1_.refs_8_), channel_id=1, source_target_pairs={{4,0},{8,4},{2,6},{12,8},{6,10},{10,14},{5,1},{9,5},{3,7},{13,9},{... | collective-permute-start | bytes 1376264 | tf_op jit(solution)/shard_map/ppermute | solution.py:520
  66.9 22.1 %collective-permute-start.14 = (f32[896,128]{1,0:T(8,128)S(1)}, f32[896,128]{1,0:T(8,128)S(1)}, u32[]{:S(2)}, u32[]{:S(2)}) collective-permute-start(f32[896,128]{1,0:T(8,128)S(1)} %get-tuple-element.53.refs_1_.refs_8_), channel_id=1, source_target_pairs={{0,2},{2,0},{4,6},{6,4},{8,10},{10,8},{12,14},{14,12},{1,3},{3,1},... | collective-permute-start | bytes 1376264 | tf_op jit(solution)/shard_map/ppermute | solution.py:510
  79.7 15.1 %collective-permute-start.16 = (f32[1152,128]{1,0:T(8,128)S(1)}, f32[1152,128]{1,0:T(8,128)S(1)}, u32[]{:S(2)}, u32[]{:S(2)}) collective-permute-start(f32[1152,128]{1,0:T(8,128)S(1)} %collective-permute-done.10.refs_0_), channel_id=1, source_target_pairs={{6,2},{0,4},{10,6},{4,8},{14,10},{8,12},{7,3},{1,5},{11,7},{5,9},{... | collective-permute-start | bytes 1769480 | tf_op jit(solution)/shard_map/ppermute | solution.py:520
  89.0 12.0 %collective-permute-start.18 = (f32[896,128]{1,0:T(8,128)S(1)}, f32[896,128]{1,0:T(8,128)S(1)}, u32[]{:S(2)}, u32[]{:S(2)}) collective-permute-start(f32[896,128]{1,0:T(8,128)S(1)} %collective-permute-done.12), channel_id=1, source_target_pairs={{0,2},{2,0},{4,6},{6,4},{8,10},{10,8},{12,14},{14,12},{1,3},{3,1},... | collective-permute-start | bytes 1376264 | tf_op jit(solution)/shard_map/ppermute | solution.py:510
  90.8 11.2 %collective-permute-start.13 = (f32[1152,128]{1,0:T(8,128)S(1)}, f32[1152,128]{1,0:T(8,128)S(1)}, u32[]{:S(2)}, u32[]{:S(2)}) collective-permute-start(f32[1152,128]{1,0:T(8,128)S(1)} %collective-permute-done.10.refs_0_), channel_id=1, source_target_pairs={{0,1},{1,0},{2,3},{3,2},{4,5},{5,4},{6,7},{7,6},{8,9},{9,8},{10,11... | collective-permute-start | bytes 1769480 | tf_op jit(solution)/shard_map/ppermute | solution.py:525
  94.8 8.0 %collective-permute-start.17 = (f32[1152,128]{1,0:T(8,128)S(1)}, f32[1152,128]{1,0:T(8,128)S(1)}, u32[]{:S(2)}, u32[]{:S(2)}) collective-permute-start(f32[1152,128]{1,0:T(8,128)S(1)} %collective-permute-done.16.refs_0_), channel_id=1, source_target_pairs={{0,1},{1,0},{2,3},{3,2},{4,5},{5,4},{6,7},{7,6},{8,9},{9,8},{10,11... | collective-permute-start | bytes 1769480 | tf_op jit(solution)/shard_map/ppermute | solution.py:525
  94.8 7.1 %collective-permute-start.15 = (f32[896,128]{1,0:T(8,128)S(1)}, f32[896,128]{1,0:T(8,128)S(1)}, u32[]{:S(2)}, u32[]{:S(2)}) collective-permute-start(f32[896,128]{1,0:T(8,128)S(1)} %collective-permute-done.14.refs_1_), channel_id=1, source_target_pairs={{0,1},{1,0},{2,3},{3,2},{4,5},{5,4},{6,7},{7,6},{8,9},{9,8},{10,11... | collective-permute-start | bytes 1376264 | tf_op jit(solution)/shard_map/ppermute | solution.py:525
  101.0 1.8 %collective-permute-start.19 = (f32[896,128]{1,0:T(8,128)S(1)}, f32[896,128]{1,0:T(8,128)S(1)}, u32[]{:S(2)}, u32[]{:S(2)}) collective-permute-start(f32[896,128]{1,0:T(8,128)S(1)} %collective-permute-done.18.refs_1_), channel_id=1, source_target_pairs={{0,1},{1,0},{2,3},{3,2},{4,5},{5,4},{6,7},{7,6},{8,9},{9,8},{10,11... | collective-permute-start | bytes 1376264 | tf_op jit(solution)/shard_map/ppermute | solution.py:525
  102.8 18.3 %copy-start = (f32[2048,128]{1,0:T(8,128)S(1)}, f32[2048,128]{1,0:T(8,128)}, u32[]{:S(2)}) copy-start(f32[2048,128]{1,0:T(8,128)} %values_hbm.1) | copy-start | bytes 3145732
  104.1 3.3 %collective-permute-start.20 = (f32[8,128]{1,0:T(8,128)S(1)}, f32[8,128]{1,0:T(8,128)S(1)}, u32[]{:S(2)}, u32[]{:S(2)}) collective-permute-start(f32[8,128]{1,0:T(8,128)S(1)} %get-tuple-element.67), channel_id=1, source_target_pairs={{0,1},{1,0},{2,3},{3,2},{4,5},{5,4},{6,7},{7,6},{8,9},{9,8},{10,11... | collective-permute-start | bytes 12296 | tf_op jit(solution)/shard_map/ppermute | solution.py:525
  107.4 4.5 %collective-permute-start.21 = (f32[8,128]{1,0:T(8,128)S(1)}, f32[8,128]{1,0:T(8,128)S(1)}, u32[]{:S(2)}, u32[]{:S(2)}) collective-permute-start(f32[8,128]{1,0:T(8,128)S(1)} %add.36), channel_id=1, source_target_pairs={{0,2},{2,0},{4,6},{6,4},{8,10},{10,8},{12,14},{14,12},{1,3},{3,1},... | collective-permute-start | bytes 12296 | tf_op jit(solution)/shard_map/ppermute | solution.py:534
  111.9 4.7 %collective-permute-start.22 = (f32[8,128]{1,0:T(8,128)S(1)}, f32[8,128]{1,0:T(8,128)S(1)}, u32[]{:S(2)}, u32[]{:S(2)}) collective-permute-start(f32[8,128]{1,0:T(8,128)S(1)} %add.37), channel_id=1, source_target_pairs={{0,4},{2,6},{4,0},{6,2},{8,12},{10,14},{12,8},{14,10},{1,5},{3,7},... | collective-permute-start | bytes 12296 | tf_op jit(solution)/shard_map/ppermute | solution.py:534
  116.6 4.6 %collective-permute-start.23 = (f32[8,128]{1,0:T(8,128)S(1)}, f32[8,128]{1,0:T(8,128)S(1)}, u32[]{:S(2)}, u32[]{:S(2)}) collective-permute-start(f32[8,128]{1,0:T(8,128)S(1)} %add.38), channel_id=1, source_target_pairs={{0,8},{2,10},{4,12},{6,14},{8,0},{10,2},{12,4},{14,6},{1,9},{3,11}... | collective-permute-start | bytes 12296 | tf_op jit(solution)/shard_map/ppermute | solution.py:534

commit v3 on v2

--- a/solution.py
+++ b/solution.py
@@ -13,9 +13,8 @@
 SLOTS = 40
 UNROLL = 8
 EVAL_UNROLL = 2
-PIECES = 2
-FIRST_SHARE = 9
-LATER_SHARE = 9
+FIRST_CUTS = (0, 10, 16)
+LATER_CUTS = (0, 6, 12, 16)
 FAR = 1.0e6
 F32 = jnp.float32
 BF16 = jnp.bfloat16
@@ -44,9 +43,9 @@
     return -(-(3 * (points // LANES) + 3) // 8) * 8
 
 
-def piece_sizes(points, share):
-    large = points // LANES * share // 16 * LANES
-    return [large, points - large]
+def piece_sizes(points, cuts):
+    rows = [points // LANES * cut // 16 * LANES for cut in cuts]
+    return [b - a for a, b in zip(rows, rows[1:])]
 
 
 def spans(chunks, top):
@@ -71,7 +70,8 @@
 
 
 def sort_kernel(points, coords_hbm, noise_hbm, values_hbm, *refs):
-    out_values, refs = refs[: PIECES + 1], refs[PIECES + 1 :]
+    pieces = len(FIRST_CUTS) - 1
+    out_values, refs = refs[: pieces + 1], refs[pieces + 1 :]
     rows, ranks, coords, noise, values, xcol, facts, sorted_facts, sorted_values, rank_row, rank_smem, sems = refs
     fetches = [
         pltpu.make_async_copy(source, target, sems.at[k])
@@ -134,9 +134,9 @@
 
     lax.fori_loop(0, points // 8, scatter, 0, unroll=4)
     header = header_rows(points)
-    whole = out_values[PIECES]
+    whole = out_values[pieces]
     whole[header:, :] = sorted_values[...]
-    for chunk, start, skip, size in spans(out_values[:PIECES], header):
+    for chunk, start, skip, size in spans(out_values[:pieces], header):
         chunk[skip:, :] = sorted_values[start : start + size, :]
     head = out_values[0]
     for g in range(groups):
@@ -160,18 +160,19 @@
 def sort_points(coords, noise, values):
     points, width = values.shape
     header = header_rows(points)
+    sizes = piece_sizes(points, FIRST_CUTS)
     out = pl.pallas_call(
         functools.partial(sort_kernel, points),
         out_shape=tuple(
-            jax.ShapeDtypeStruct((size + (header if c in (0, PIECES) else 0), width), F32)
-            for c, size in enumerate([*piece_sizes(points, FIRST_SHARE), points])
+            jax.ShapeDtypeStruct((size + (header if c in (0, len(sizes)) else 0), width), F32)
+            for c, size in enumerate([*sizes, points])
         )
         + (
             pltpu.VMEM((4, points + ROWS, LANES), F32),
             jax.ShapeDtypeStruct((1, points), jnp.int32),
         ),
         in_specs=[pl.BlockSpec(memory_space=pltpu.HBM)] * 3,
-        out_specs=[vmem_spec()] * (PIECES + 3),
+        out_specs=[vmem_spec()] * (len(sizes) + 3),
         scratch_shapes=[
             pltpu.VMEM((3, points), F32),
             pltpu.VMEM((1, points), F32),
@@ -187,7 +188,7 @@
         compiler_params=pltpu.CompilerParams(vmem_limit_bytes=14 * MIB),
         name="sort_points",
     )(coords, noise, values)
-    return out[:PIECES], *out[PIECES:]
+    return out[: len(sizes)], *out[len(sizes) :]
 
 
 def tile_values(rows, cols, at, count):
@@ -246,7 +247,7 @@
     return jnp.broadcast_to(first * 64 + blocks.astype(jnp.int32), (windows, LANES))
 
 
-def list_tiles(points, own, heads, work, facts, table, table_smem, sem):
+def list_tiles(points, own, heads, work, facts, table, table_smem, sem, beside):
     windows = points // LANES
     found = jnp.concatenate([find_ranges(points, own, head) for head in heads], axis=0)
     lane = lax.broadcasted_iota(jnp.int32, found.shape, 1)
@@ -255,6 +256,7 @@
     copy = pltpu.make_async_copy(table, table_smem, sem)
     copy.start()
     gather_facts(windows, facts, heads)
+    beside()
     copy.wait()
     slot = jnp.int32(0)
     for w in range(len(heads) * windows):
@@ -399,12 +401,16 @@
     values = groups[:halves]
     cache, work, facts, acc, pairs, tile, table, table_smem, sem = refs
     header = header_rows(points)
-    total = list_tiles(points, own, [half[0] for half in values], work, facts, table, table_smem, sem)
-    acc[...] = jnp.zeros_like(acc)
+
+    def prepare():
+        acc[...] = jnp.zeros_like(acc)
+        split_values(points, values, header, pairs)
+
+    heads = [half[0] for half in values]
+    total = list_tiles(points, own, heads, work, facts, table, table_smem, sem, prepare)
 
     @pl.when(total > 0)
     def _():
-        split_values(points, values, header, pairs)
         kept = jnp.minimum(total, cache.shape[0])
         steps = (kept + (EVAL_UNROLL - 1)) // EVAL_UNROLL
         keep_tiles(windows, work, facts, rows, cache, 0)
@@ -430,7 +436,7 @@
 
 
 def image_shapes(points, sent):
-    sizes = [*(piece_sizes(points, LATER_SHARE) if sent else []), points]
+    sizes = [*(piece_sizes(points, LATER_CUTS) if sent else []), points]
     return [jax.ShapeDtypeStruct((size, LANES), F32) for size in sizes]
 
 
@@ -443,14 +449,14 @@
     return [mark + fold(term) for mark, term in zip(marks, terms)]
 
 
-def product(points, evaluated, rows, values, before=(), marker=None, given=(), once=()):
+def product(points, evaluated, rows, values, before=(), headed=False, marker=None, given=(), once=()):
     cache, work, facts = evaluated
     groups = (*values, before, given, once)
     operands = (facts, rows, cache, *(x for group in groups for x in group))
     sums = int(marker is not None)
     counts = [len(group) for group in groups] + [1, sums]
     out = pl.pallas_call(
-        functools.partial(product_kernel, points, len(values), False, counts, marker),
+        functools.partial(product_kernel, points, len(values), headed, counts, marker),
         out_shape=image_shapes(points, False) + [jax.ShapeDtypeStruct((8, LANES), F32)] * sums,
         in_specs=[smem_spec()] + [vmem_spec()] * len(operands),
         out_specs=[vmem_spec()] * (1 + sums),
@@ -570,18 +576,18 @@
     (*once, whole), mate_eval = eval_product(points, given[0], rows, (near_mates, far_mates), SLOTS, image, True)
 
     near = [pair_swap(c) for c in once]
-    turned = pair_shift(once[1], 1)
+    turned = pair_shift(once[-1], 1)
     mates = core_swap(whole)
     image0 = unsort(ranks, after(whole, mates))
     image = product(points, own_eval, rows, (once, (after(mates, image0),)))
     near[0] = after(near[0], image[0], turned)
-    far = [pair_shift(near[0])]
-    far.append(pair_swap(after(turned, near[1], near[0])))
+    far = [pair_shift(c) for c in near[:-1]]
+    far.append(pair_swap(after(turned, near[-1], near[0])))
     near_mates = [core_swap(c) for c in near]
     image = product(points, near_eval, rows, (near,), image)
-    far_mates = [core_swap(far[0]), core_swap(after(far[1], image[0]))]
+    far_mates = [core_swap(after(c, image[0])) for c in far]
     image = product(points, far_eval, rows, (far,), image)
-    twice, sums = product(points, mate_eval, rows, (near_mates, far_mates), image, all_sums, given, once)
+    twice, sums = product(points, mate_eval, rows, (near_mates, far_mates), image, False, all_sums, given, once)
     image1 = unsort(ranks, twice)
 
     sums = total(sums, image1)

time: 123 us -> 119 us (0.967)
  waiting for transfers between devices: 29.2 us -> 21.8 us
  starting transfers between devices: 44.1 us -> 48.8 us
  Pallas kernels: 47 us -> 45.5 us
    ppermute x6 -> x7, waiting for transfers between devices: 17 us -> 12.5 us  [pair_swap(): return lax.ppermute(block, 'tm', [(i, i ^ 1) for i in range(count)])]
    ppermute x4 -> x5, starting transfers between devices: 9.77 us -> 14.1 us  [pair_shift(): return lax.ppermute(block, 'tm', route)]
    ppermute x4 -> x5, waiting for transfers between devices: 6.03 us -> 2.67 us  [pair_shift(): return lax.ppermute(block, 'tm', route)]
    ppermute x6 -> x7, starting transfers between devices: 17.4 us -> 17 us  [pair_swap(): return lax.ppermute(block, 'tm', [(i, i ^ 1) for i in range(count)])]
    ppermute x11 -> x13, starting transfers between devices: 9.28 us -> 9.57 us  [core_swap(): return lax.ppermute(block, 'tile', [(i, i ^ 1) for i in range(count)])]
    ppermute x11 -> x13, waiting for transfers between devices: 2.78 us -> 3 us  [core_swap(): return lax.ppermute(block, 'tile', [(i, i ^ 1) for i in range(count)])]
  transfers between devices with their start and end apart: 24 -> 28, of which waited for: 12 -> 12; matrix products, arithmetic and copies ran while one was open for 0% -> 0% of each run, Pallas kernels for 28% -> 28%
where the time goes in v3:
time: 119 us
  starting transfers between devices  48.8 us (41%)
  Pallas kernels  45.5 us (38%)
  waiting for transfers between devices  21.8 us (18%)
  other arithmetic  1.85 us (2%)
    pallas_call x4, Pallas kernels, eval_product(): pl.pallas_call(functools.partial(both_kernel, points, halves, counts), ou...  21.1 us
    ppermute x7, starting transfers between devices, pair_swap(): return lax.ppermute(block, 'tm', [(i, i ^ 1) for i in range(count)])  17 us
    ppermute x5, starting transfers between devices, pair_shift(): return lax.ppermute(block, 'tm', route)  14.1 us
    ppermute x7, waiting for transfers between devices, pair_swap(): return lax.ppermute(block, 'tm', [(i, i ^ 1) for i in range(count)])  12.5 us
    pallas_call x4, Pallas kernels, product(): pl.pallas_call(functools.partial(product_kernel, points, len(values), hea...  10.3 us
    ppermute x13, starting transfers between devices, core_swap(): return lax.ppermute(block, 'tile', [(i, i ^ 1) for i in range(count)])  9.57 us
    pallas_call x1, Pallas kernels, sort_points(): pl.pallas_call(functools.partial(sort_kernel, points), out_shape=tuple((j...  8.76 us
    ppermute x3, starting transfers between devices, stride_sum(): lax.ppermute(value, 'tm', [(i, i ^ step) for i in range(count)])  8.18 us
  transfers between devices with their start and end apart: 28, of which 12 were waited for; matrix products, arithmetic and copies ran while one was open for 0% of the time, Pallas kernels for 28%

profile of v3, /device:TPU:0, one launch (start us, length us, event | category | flops | bytes accessed | tf_op | source)
XLA Modules:
  0.0 118.8 jit_solution(2762748336746148287)
XLA Ops:
  0.6 8.8 %sort_points.1 = (f32[1336,128]{1,0:T(8,128)S(1)}, f32[768,128]{1,0:T(8,128)S(1)}, f32[2104,128]{1,0:T(8,128)S(1)}, f32[4,2272,128]{2,1,0:T(8,128)S(1)}, s32[1,2048]{1,0:T(1,128)S(1)}) custom-call(f32[3,2048]{1,0:T(4,128)} %coords_hbm.1, f32[1,2048]{1,0:T(1,128)} %bitcast.5, f32[2048,128]{1,0:T(8,128)} %values_hbm.1), custom_call_target="tpu_custom_call" | custom-call | tf_op jit(solution)/shard_map/sort_points/pallas_call | solution.py:164
  9.9 2.6 %collective-permute-start = (f32[1336,128]{1,0:T(8,128)S(1)}, f32[1336,128]{1,0:T(8,128)S(1)}, u32[]{:S(2)}, u32[]{:S(2)}) collective-permute-start(f32[1336,128]{1,0:T(8,128)S(1)} %get-tuple-element.39.own.refs_0_.refs_7_), channel_id=1, source_target_pairs={{0,2},{2,0},{4,6},{6,4},{8,10},{10,8},{12,14},{14,12},{1,3},{3,1},... | collective-permute-start | bytes 2052104 | tf_op jit(solution)/shard_map/ppermute | solution.py:516
  12.5 1.3 %collective-permute-start.2 = (f32[768,128]{1,0:T(8,128)S(1)}, f32[768,128]{1,0:T(8,128)S(1)}, u32[]{:S(2)}, u32[]{:S(2)}) collective-permute-start(f32[768,128]{1,0:T(8,128)S(1)} %get-tuple-element.41.refs_1_.refs_8_), channel_id=1, source_target_pairs={{4,0},{8,4},{2,6},{12,8},{6,10},{10,14},{5,1},{9,5},{3,7},{13,9},{... | collective-permute-start | bytes 1179656 | tf_op jit(solution)/shard_map/ppermute | solution.py:526
  13.8 2.8 %collective-permute-start.4 = (f32[768,128]{1,0:T(8,128)S(1)}, f32[768,128]{1,0:T(8,128)S(1)}, u32[]{:S(2)}, u32[]{:S(2)}) collective-permute-start(f32[768,128]{1,0:T(8,128)S(1)} %get-tuple-element.41.refs_1_.refs_8_), channel_id=1, source_target_pairs={{0,2},{2,0},{4,6},{6,4},{8,10},{10,8},{12,14},{14,12},{1,3},{3,1},... | collective-permute-start | bytes 1179656 | tf_op jit(solution)/shard_map/ppermute | solution.py:516
  16.6 11.0 %eval_product.4 = (f32[2048,128]{1,0:T(8,128)S(1)}, bf16[72,224,256]{2,1,0:T(8,128)(2,1)S(1)}, s32[3,328]{1,0:T(4,128)S(1)}, f32[96,128]{1,0:T(8,128)S(1)}) custom-call(f32[1336,128]{1,0:T(8,128)S(1)} %get-tuple-element.39.own.refs_0_.refs_7_, f32[4,2272,128]{2,1,0:T(8,128)S(1)} %get-tuple-element.40.rows, ...), custom_call_target="tpu_custom_call" | custom-call | flops 1000000 | bytes 100000 | tf_op jit(solution)/shard_map/eval_product/pallas_call | solution.py:477
  28.7 3.9 %collective-permute-start.6 = (f32[1336,128]{1,0:T(8,128)S(1)}, f32[1336,128]{1,0:T(8,128)S(1)}, u32[]{:S(2)}, u32[]{:S(2)}) collective-permute-start(f32[1336,128]{1,0:T(8,128)S(1)} %collective-permute-done.refs_0_), channel_id=1, source_target_pairs={{6,2},{0,4},{10,6},{4,8},{14,10},{8,12},{7,3},{1,5},{11,7},{5,9},{... | collective-permute-start | bytes 2052104 | tf_op jit(solution)/shard_map/ppermute | solution.py:526
  32.7 4.2 %collective-permute-done.4.refs_1_ = f32[768,128]{1,0:T(8,128)S(1)} collective-permute-done((f32[768,128]{1,0:T(8,128)S(1)}, f32[768,128]{1,0:T(8,128)S(1)}, u32[]{:S(2)}, u32[]{:S(2)}) %collective-permute-start.4) | collective-permute-done | bytes 393248 | tf_op jit(solution)/shard_map/ppermute | solution.py:516
  36.9 1.8 %collective-permute-start.7 = (f32[768,128]{1,0:T(8,128)S(1)}, f32[768,128]{1,0:T(8,128)S(1)}, u32[]{:S(2)}, u32[]{:S(2)}) collective-permute-start(f32[768,128]{1,0:T(8,128)S(1)} %collective-permute-done.2), channel_id=1, source_target_pairs={{0,2},{2,0},{4,6},{6,4},{8,10},{10,8},{12,14},{14,12},{1,3},{3,1},... | collective-permute-start | bytes 1179656 | tf_op jit(solution)/shard_map/ppermute | solution.py:516
  38.6 6.3 %eval_product.5 = (f32[2048,128]{1,0:T(8,128)S(1)}, bf16[40,224,256]{2,1,0:T(8,128)(2,1)S(1)}, s32[3,168]{1,0:T(4,128)S(1)}, f32[48,128]{1,0:T(8,128)S(1)}) custom-call(f32[1336,128]{1,0:T(8,128)S(1)} %get-tuple-element.39.own.refs_0_.refs_7_, f32[4,2272,128]{2,1,0:T(8,128)S(1)} %get-tuple-element.40.rows, f32[1336,128]{1,0:T(8,128)S(1)} %collective-permute-done.refs_0_, ...), custom_call_target="tpu_custom_call" | custom-call | flops 1000000 | bytes 100000 | tf_op jit(solution)/shard_map/eval_product/pallas_call | solution.py:477
  45.0 2.8 %collective-permute-done.7.refs_1_ = f32[768,128]{1,0:T(8,128)S(1)} collective-permute-done((f32[768,128]{1,0:T(8,128)S(1)}, f32[768,128]{1,0:T(8,128)S(1)}, u32[]{:S(2)}, u32[]{:S(2)}) %collective-permute-start.7) | collective-permute-done | bytes 393248 | tf_op jit(solution)/shard_map/ppermute | solution.py:516
  48.3 1.7 %eval_product.6 = (f32[2048,128]{1,0:T(8,128)S(1)}, bf16[40,224,256]{2,1,0:T(8,128)(2,1)S(1)}, s32[3,168]{1,0:T(4,128)S(1)}, f32[48,128]{1,0:T(8,128)S(1)}) custom-call(f32[1336,128]{1,0:T(8,128)S(1)} %get-tuple-element.39.own.refs_0_.refs_7_, f32[4,2272,128]{2,1,0:T(8,128)S(1)} %get-tuple-element.40.rows, f32[1336,128]{1,0:T(8,128)S(1)} %collective-permute-done.6.refs_0_, ...), custom_call_target="tpu_custom_call" | custom-call | flops 1000000 | bytes 100000 | tf_op jit(solution)/shard_map/eval_product/pallas_call | solution.py:477
  51.0 2.0 %eval_product.7 = (f32[768,128]{1,0:T(8,128)S(1)}, f32[768,128]{1,0:T(8,128)S(1)}, f32[512,128]{1,0:T(8,128)S(1)}, f32[2048,128]{1,0:T(8,128)S(1)}, bf16[40,224,...) custom-call(f32[1336,128]{1,0:T(8,128)S(1)} %get-tuple-element.39.own.refs_0_.refs_7_, ...), custom_call_target="tpu_custom_call" | custom-call | flops 1000000 | bytes 100000 | tf_op jit(solution)/shard_map/eval_product/pallas_call | solution.py:477
  53.0 4.8 %collective-permute-start.11 = (f32[2048,128]{1,0:T(8,128)S(1)}, f32[2048,128]{1,0:T(8,128)S(1)}, u32[]{:S(2)}, u32[]{:S(2)}) collective-permute-start(f32[2048,128]{1,0:T(8,128)S(1)} %get-tuple-element.60.source), channel_id=1, source_target_pairs={{0,1},{1,0},{2,3},{3,2},{4,5},{5,4},{6,7},{7,6},{8,9},{9,8},{10,11... | collective-permute-start | bytes 3145736 | tf_op jit(solution)/shard_map/ppermute | solution.py:531
  57.8 5.6 %collective-permute-start.14 = (f32[768,128]{1,0:T(8,128)S(1)}, f32[768,128]{1,0:T(8,128)S(1)}, u32[]{:S(2)}, u32[]{:S(2)}) collective-permute-start(f32[768,128]{1,0:T(8,128)S(1)} %get-tuple-element.56.refs_1_.refs_10_), channel_id=1, source_target_pairs={{0,2},{2,0},{4,6},{6,4},{8,10},{10,8},{12,14},{14,12},{1,3},{3,1},... | collective-permute-start | bytes 1179656 | tf_op jit(solution)/shard_map/ppermute | solution.py:516
  63.4 1.3 %collective-permute-start.12 = (f32[512,128]{1,0:T(8,128)S(1)}, f32[512,128]{1,0:T(8,128)S(1)}, u32[]{:S(2)}, u32[]{:S(2)}) collective-permute-start(f32[512,128]{1,0:T(8,128)S(1)} %get-tuple-element.57.refs_2_.refs_11_), channel_id=1, source_target_pairs={{4,0},{8,4},{2,6},{12,8},{6,10},{10,14},{5,1},{9,5},{3,7},{13,9},{... | collective-permute-start | bytes 786440 | tf_op jit(solution)/shard_map/ppermute | solution.py:526
  64.7 4.2 %collective-permute-start.16 = (f32[512,128]{1,0:T(8,128)S(1)}, f32[512,128]{1,0:T(8,128)S(1)}, u32[]{:S(2)}, u32[]{:S(2)}) collective-permute-start(f32[512,128]{1,0:T(8,128)S(1)} %get-tuple-element.57.refs_2_.refs_11_), channel_id=1, source_target_pairs={{0,2},{2,0},{4,6},{6,4},{8,10},{10,8},{12,14},{14,12},{1,3},{3,1},... | collective-permute-start | bytes 786440 | tf_op jit(solution)/shard_map/ppermute | solution.py:516
  68.9 4.4 %collective-permute-done.14.refs_1_ = f32[768,128]{1,0:T(8,128)S(1)} collective-permute-done((f32[768,128]{1,0:T(8,128)S(1)}, f32[768,128]{1,0:T(8,128)S(1)}, u32[]{:S(2)}, u32[]{:S(2)}) %collective-permute-start.14) | collective-permute-done | bytes 393248 | tf_op jit(solution)/shard_map/ppermute | solution.py:516
  73.3 4.0 %collective-permute-start.20 = (f32[768,128]{1,0:T(8,128)S(1)}, f32[768,128]{1,0:T(8,128)S(1)}, u32[]{:S(2)}, u32[]{:S(2)}) collective-permute-start(f32[768,128]{1,0:T(8,128)S(1)} %collective-permute-done.14.refs_1_), channel_id=1, source_target_pairs={{6,2},{0,4},{10,6},{4,8},{14,10},{8,12},{7,3},{1,5},{11,7},{5,9},{... | collective-permute-start | bytes 1179656 | tf_op jit(solution)/shard_map/ppermute | solution.py:526
  77.3 2.7 %unsort.2 = f32[2048,128]{1,0:T(8,128)S(1)} custom-call(s32[1,2048]{1,0:T(1,128)S(1)} %get-tuple-element.59.ranks, f32[2048,128]{1,0:T(8,128)S(1)} %get-tuple-element.60.source), custom_call_target="tpu_custom_call" | custom-call | flops 1000000 | bytes 100000 | tf_op jit(solution)/shard_map/unsort/pallas_call | solution.py:503
  80.0 5.1 %product.4.refs_3_ = f32[2048,128]{1,0:T(8,128)S(1)} custom-call(s32[3,328]{1,0:T(4,128)S(1)} %get-tuple-element.53.work, f32[96,128]{1,0:T(8,128)S(1)} %get-tuple-element.54.facts, f32[4,2272,128]{2,1,0:T(8,128)S(1)} %get-tuple-element.40.rows, bf16[72,224,256]{2,1,0:T(8,128)(2,1)S(1)} %get-tuple-element.55.cache, ...), custom_call_target="tpu_custom_call" | custom-call | flops 1000000 | bytes 100000 | tf_op jit(solution)/shard_map/product/pallas_call | solution.py:458
  85.1 3.6 %collective-permute-start.18 = (f32[768,128]{1,0:T(8,128)S(1)}, f32[768,128]{1,0:T(8,128)S(1)}, u32[]{:S(2)}, u32[]{:S(2)}) collective-permute-start(f32[768,128]{1,0:T(8,128)S(1)} %collective-permute-done.10.refs_0_), channel_id=1, source_target_pairs={{6,2},{0,4},{10,6},{4,8},{14,10},{8,12},{7,3},{1,5},{11,7},{5,9},{... | collective-permute-start | bytes 1179656 | tf_op jit(solution)/shard_map/ppermute | solution.py:526
  89.3 3.1 %product.5.refs_3_ = f32[2048,128]{1,0:T(8,128)S(1)} custom-call(s32[3,168]{1,0:T(4,128)S(1)} %get-tuple-element.63.work, f32[48,128]{1,0:T(8,128)S(1)} %get-tuple-element.64.facts, f32[4,2272,128]{2,1,0:T(8,128)S(1)} %get-tuple-element.40.rows, bf16[40,224,256]{2,1,0:T(8,128)(2,1)S(1)} %get-tuple-element.65.cache, ...), custom_call_target="tpu_custom_call" | custom-call | flops 1000000 | bytes 100000 | tf_op jit(solution)/shard_map/product/pallas_call | solution.py:458
  92.6 2.7 %collective-permute-done.18.refs_0_ = f32[768,128]{1,0:T(8,128)S(1)} collective-permute-done((f32[768,128]{1,0:T(8,128)S(1)}, f32[768,128]{1,0:T(8,128)S(1)}, u32[]{:S(2)}, u32[]{:S(2)}) %collective-permute-start.18) | collective-permute-done | bytes 393248 | tf_op jit(solution)/shard_map/ppermute | solution.py:526
  97.9 1.3 %product.7 = (f32[2048,128]{1,0:T(8,128)S(1)}, f32[8,128]{1,0:T(8,128)S(1)}) custom-call(s32[3,328]{1,0:T(4,128)S(1)} %get-tuple-element.49.work, f32[96,128]{1,0:T(8,128)S(1)} %get-tuple-element.50.facts, f32[4,2272,128]{2,1,0:T(8,128)S(1)} %get-tuple-element.40.rows, bf16[40,224,256]{2,1,0:T(8,128)(2,1)S(1)} %get-tuple-element.51.cache, ...), custom_call_target="tpu_custom_call" | custom-call | flops 1000000 | bytes 100000 | tf_op jit(solution)/shard_map/product/pallas_call | solution.py:458
  99.2 2.4 %collective-permute-start.24 = (f32[8,128]{1,0:T(8,128)S(1)}, f32[8,128]{1,0:T(8,128)S(1)}, u32[]{:S(2)}, u32[]{:S(2)}) collective-permute-start(f32[8,128]{1,0:T(8,128)S(1)} %get-tuple-element.73), channel_id=1, source_target_pairs={{0,1},{1,0},{2,3},{3,2},{4,5},{5,4},{6,7},{7,6},{8,9},{9,8},{10,11... | collective-permute-start | bytes 12296 | tf_op jit(solution)/shard_map/ppermute | solution.py:531
  102.4 2.3 %collective-permute-start.25 = (f32[8,128]{1,0:T(8,128)S(1)}, f32[8,128]{1,0:T(8,128)S(1)}, u32[]{:S(2)}, u32[]{:S(2)}) collective-permute-start(f32[8,128]{1,0:T(8,128)S(1)} %add.36), channel_id=1, source_target_pairs={{0,2},{2,0},{4,6},{6,4},{8,10},{10,8},{12,14},{14,12},{1,3},{3,1},... | collective-permute-start | bytes 12296 | tf_op jit(solution)/shard_map/ppermute | solution.py:540
  104.7 1.6 %collective-permute-done.25 = f32[8,128]{1,0:T(8,128)S(1)} collective-permute-done((f32[8,128]{1,0:T(8,128)S(1)}, f32[8,128]{1,0:T(8,128)S(1)}, u32[]{:S(2)}, u32[]{:S(2)}) %collective-permute-start.25) | collective-permute-done | bytes 4128 | tf_op jit(solution)/shard_map/ppermute | solution.py:540
  106.3 3.4 %collective-permute-start.26 = (f32[8,128]{1,0:T(8,128)S(1)}, f32[8,128]{1,0:T(8,128)S(1)}, u32[]{:S(2)}, u32[]{:S(2)}) collective-permute-start(f32[8,128]{1,0:T(8,128)S(1)} %add.37), channel_id=1, source_target_pairs={{0,4},{2,6},{4,0},{6,2},{8,12},{10,14},{12,8},{14,10},{1,5},{3,7},... | collective-permute-start | bytes 12296 | tf_op jit(solution)/shard_map/ppermute | solution.py:540
  109.7 2.7 %unsort.3 = f32[2048,128]{1,0:T(8,128)S(1)} custom-call(s32[1,2048]{1,0:T(1,128)S(1)} %get-tuple-element.59.ranks, f32[2048,128]{1,0:T(8,128)S(1)} %get-tuple-element.74.source), custom_call_target="tpu_custom_call" | custom-call | flops 1000000 | bytes 100000 | tf_op jit(solution)/shard_map/unsort/pallas_call | solution.py:503
  112.4 2.5 %collective-permute-start.27 = (f32[8,128]{1,0:T(8,128)S(1)}, f32[8,128]{1,0:T(8,128)S(1)}, u32[]{:S(2)}, u32[]{:S(2)}) collective-permute-start(f32[8,128]{1,0:T(8,128)S(1)} %add.38), channel_id=1, source_target_pairs={{0,8},{2,10},{4,12},{6,14},{8,0},{10,2},{12,4},{14,6},{1,9},{3,11}... | collective-permute-start | bytes 12296 | tf_op jit(solution)/shard_map/ppermute | solution.py:540
  114.9 2.1 %collective-permute-done.27 = f32[8,128]{1,0:T(8,128)S(1)} collective-permute-done((f32[8,128]{1,0:T(8,128)S(1)}, f32[8,128]{1,0:T(8,128)S(1)}, u32[]{:S(2)}, u32[]{:S(2)}) %collective-permute-start.27) | collective-permute-done | bytes 4128 | tf_op jit(solution)/shard_map/ppermute | solution.py:540
  117.0 1.8 %multiply_subtract_fusion = (f32[2048,128]{1,0:T(8,128)}, f32[2048,128]{1,0:T(8,128)}) fusion(f32[2048,128]{1,0:T(8,128)S(1)} %unsort.2, f32[2048,128]{1,0:T(8,128)S(1)} %unsort.3, f32[2048,128]{1,0:T(8,128)S(1)} %copy-done, f32[128]{0:T(128)S(1)} %bitcast.7, f32[128]{0:T(128)S(1)} %get-tuple-element.76, f32[128]{0:T(128)S(1)} %bitcast.6), kind=kLoop, calls=%fused_computation | loop fusion | flops 3407872 | bytes 5244416 | tf_op jit(solution)/shard_map/sub | solution.py:604
  (44 shorter events, 7.5 us)
Async XLA Ops:
  9.4 7.2 %collective-permute-start.1 = (f32[2104,128]{1,0:T(8,128)S(1)}, f32[2104,128]{1,0:T(8,128)S(1)}, u32[]{:S(2)}, u32[]{:S(2)}) collective-permute-start(f32[2104,128]{1,0:T(8,128)S(1)} %get-tuple-element.42), channel_id=1, source_target_pairs={{0,1},{1,0},{2,3},{3,2},{4,5},{5,4},{6,7},{7,6},{8,9},{9,8},{10,11... | collective-permute-start | bytes 3231752 | tf_op jit(solution)/shard_map/ppermute | solution.py:531
  9.9 18.8 %collective-permute-start = (f32[1336,128]{1,0:T(8,128)S(1)}, f32[1336,128]{1,0:T(8,128)S(1)}, u32[]{:S(2)}, u32[]{:S(2)}) collective-permute-start(f32[1336,128]{1,0:T(8,128)S(1)} %get-tuple-element.39.own.refs_0_.refs_7_), channel_id=1, source_target_pairs={{0,2},{2,0},{4,6},{6,4},{8,10},{10,8},{12,14},{14,12},{1,3},{3,1},... | collective-permute-start | bytes 2052104 | tf_op jit(solution)/shard_map/ppermute | solution.py:516
  12.5 15.1 %collective-permute-start.2 = (f32[768,128]{1,0:T(8,128)S(1)}, f32[768,128]{1,0:T(8,128)S(1)}, u32[]{:S(2)}, u32[]{:S(2)}) collective-permute-start(f32[768,128]{1,0:T(8,128)S(1)} %get-tuple-element.41.refs_1_.refs_8_), channel_id=1, source_target_pairs={{4,0},{8,4},{2,6},{12,8},{6,10},{10,14},{5,1},{9,5},{3,7},{13,9},{... | collective-permute-start | bytes 1179656 | tf_op jit(solution)/shard_map/ppermute | solution.py:526
  13.8 23.1 %collective-permute-start.4 = (f32[768,128]{1,0:T(8,128)S(1)}, f32[768,128]{1,0:T(8,128)S(1)}, u32[]{:S(2)}, u32[]{:S(2)}) collective-permute-start(f32[768,128]{1,0:T(8,128)S(1)} %get-tuple-element.41.refs_1_.refs_8_), channel_id=1, source_target_pairs={{0,2},{2,0},{4,6},{6,4},{8,10},{10,8},{12,14},{14,12},{1,3},{3,1},... | collective-permute-start | bytes 1179656 | tf_op jit(solution)/shard_map/ppermute | solution.py:516
  28.7 19.0 %collective-permute-start.6 = (f32[1336,128]{1,0:T(8,128)S(1)}, f32[1336,128]{1,0:T(8,128)S(1)}, u32[]{:S(2)}, u32[]{:S(2)}) collective-permute-start(f32[1336,128]{1,0:T(8,128)S(1)} %collective-permute-done.refs_0_), channel_id=1, source_target_pairs={{6,2},{0,4},{10,6},{4,8},{14,10},{8,12},{7,3},{1,5},{11,7},{5,9},{... | collective-permute-start | bytes 2052104 | tf_op jit(solution)/shard_map/ppermute | solution.py:526
  36.9 10.9 %collective-permute-start.7 = (f32[768,128]{1,0:T(8,128)S(1)}, f32[768,128]{1,0:T(8,128)S(1)}, u32[]{:S(2)}, u32[]{:S(2)}) collective-permute-start(f32[768,128]{1,0:T(8,128)S(1)} %collective-permute-done.2), channel_id=1, source_target_pairs={{0,2},{2,0},{4,6},{6,4},{8,10},{10,8},{12,14},{14,12},{1,3},{3,1},... | collective-permute-start | bytes 1179656 | tf_op jit(solution)/shard_map/ppermute | solution.py:516
  38.6 11.8 %collective-permute-start.3 = (f32[1336,128]{1,0:T(8,128)S(1)}, f32[1336,128]{1,0:T(8,128)S(1)}, u32[]{:S(2)}, u32[]{:S(2)}) collective-permute-start(f32[1336,128]{1,0:T(8,128)S(1)} %collective-permute-done.refs_0_), channel_id=1, source_target_pairs={{0,1},{1,0},{2,3},{3,2},{4,5},{5,4},{6,7},{7,6},{8,9},{9,8},{10,11... | collective-permute-start | bytes 2052104 | tf_op jit(solution)/shard_map/ppermute | solution.py:531
  47.8 3.3 %collective-permute-start.8 = (f32[1336,128]{1,0:T(8,128)S(1)}, f32[1336,128]{1,0:T(8,128)S(1)}, u32[]{:S(2)}, u32[]{:S(2)}) collective-permute-start(f32[1336,128]{1,0:T(8,128)S(1)} %collective-permute-done.6.refs_0_), channel_id=1, source_target_pairs={{0,1},{1,0},{2,3},{3,2},{4,5},{5,4},{6,7},{7,6},{8,9},{9,8},{10,11... | collective-permute-start | bytes 2052104 | tf_op jit(solution)/shard_map/ppermute | solution.py:531
  47.8 2.7 %collective-permute-start.5 = (f32[768,128]{1,0:T(8,128)S(1)}, f32[768,128]{1,0:T(8,128)S(1)}, u32[]{:S(2)}, u32[]{:S(2)}) collective-permute-start(f32[768,128]{1,0:T(8,128)S(1)} %collective-permute-done.4.refs_1_), channel_id=1, source_target_pairs={{0,1},{1,0},{2,3},{3,2},{4,5},{5,4},{6,7},{7,6},{8,9},{9,8},{10,11... | collective-permute-start | bytes 1179656 | tf_op jit(solution)/shard_map/ppermute | solution.py:531
  48.3 2.8 %collective-permute-start.9 = (f32[768,128]{1,0:T(8,128)S(1)}, f32[768,128]{1,0:T(8,128)S(1)}, u32[]{:S(2)}, u32[]{:S(2)}) collective-permute-start(f32[768,128]{1,0:T(8,128)S(1)} %collective-permute-done.7.refs_1_), channel_id=1, source_target_pairs={{0,1},{1,0},{2,3},{3,2},{4,5},{5,4},{6,7},{7,6},{8,9},{9,8},{10,11... | collective-permute-start | bytes 1179656 | tf_op jit(solution)/shard_map/ppermute | solution.py:531
  53.0 24.3 %collective-permute-start.11 = (f32[2048,128]{1,0:T(8,128)S(1)}, f32[2048,128]{1,0:T(8,128)S(1)}, u32[]{:S(2)}, u32[]{:S(2)}) collective-permute-start(f32[2048,128]{1,0:T(8,128)S(1)} %get-tuple-element.60.source), channel_id=1, source_target_pairs={{0,1},{1,0},{2,3},{3,2},{4,5},{5,4},{6,7},{7,6},{8,9},{9,8},{10,11... | collective-permute-start | bytes 3145736 | tf_op jit(solution)/shard_map/ppermute | solution.py:531
  57.8 15.5 %collective-permute-start.14 = (f32[768,128]{1,0:T(8,128)S(1)}, f32[768,128]{1,0:T(8,128)S(1)}, u32[]{:S(2)}, u32[]{:S(2)}) collective-permute-start(f32[768,128]{1,0:T(8,128)S(1)} %get-tuple-element.56.refs_1_.refs_10_), channel_id=1, source_target_pairs={{0,2},{2,0},{4,6},{6,4},{8,10},{10,8},{12,14},{14,12},{1,3},{3,1},... | collective-permute-start | bytes 1179656 | tf_op jit(solution)/shard_map/ppermute | solution.py:516
  63.4 21.6 %collective-permute-start.10 = (f32[768,128]{1,0:T(8,128)S(1)}, f32[768,128]{1,0:T(8,128)S(1)}, u32[]{:S(2)}, u32[]{:S(2)}) collective-permute-start(f32[768,128]{1,0:T(8,128)S(1)} %get-tuple-element.52.refs_0_.refs_9_), channel_id=1, source_target_pairs={{0,2},{2,0},{4,6},{6,4},{8,10},{10,8},{12,14},{14,12},{1,3},{3,1},... | collective-permute-start | bytes 1179656 | tf_op jit(solution)/shard_map/ppermute | solution.py:516
  63.4 21.6 %collective-permute-start.12 = (f32[512,128]{1,0:T(8,128)S(1)}, f32[512,128]{1,0:T(8,128)S(1)}, u32[]{:S(2)}, u32[]{:S(2)}) collective-permute-start(f32[512,128]{1,0:T(8,128)S(1)} %get-tuple-element.57.refs_2_.refs_11_), channel_id=1, source_target_pairs={{4,0},{8,4},{2,6},{12,8},{6,10},{10,14},{5,1},{9,5},{3,7},{13,9},{... | collective-permute-start | bytes 786440 | tf_op jit(solution)/shard_map/ppermute | solution.py:526
  64.7 23.9 %collective-permute-start.16 = (f32[512,128]{1,0:T(8,128)S(1)}, f32[512,128]{1,0:T(8,128)S(1)}, u32[]{:S(2)}, u32[]{:S(2)}) collective-permute-start(f32[512,128]{1,0:T(8,128)S(1)} %get-tuple-element.57.refs_2_.refs_11_), channel_id=1, source_target_pairs={{0,2},{2,0},{4,6},{6,4},{8,10},{10,8},{12,14},{14,12},{1,3},{3,1},... | collective-permute-start | bytes 786440 | tf_op jit(solution)/shard_map/ppermute | solution.py:516
  73.3 19.1 %collective-permute-start.20 = (f32[768,128]{1,0:T(8,128)S(1)}, f32[768,128]{1,0:T(8,128)S(1)}, u32[]{:S(2)}, u32[]{:S(2)}) collective-permute-start(f32[768,128]{1,0:T(8,128)S(1)} %collective-permute-done.14.refs_1_), channel_id=1, source_target_pairs={{6,2},{0,4},{10,6},{4,8},{14,10},{8,12},{7,3},{1,5},{11,7},{5,9},{... | collective-permute-start | bytes 1179656 | tf_op jit(solution)/shard_map/ppermute | solution.py:526
  85.1 10.2 %collective-permute-start.18 = (f32[768,128]{1,0:T(8,128)S(1)}, f32[768,128]{1,0:T(8,128)S(1)}, u32[]{:S(2)}, u32[]{:S(2)}) collective-permute-start(f32[768,128]{1,0:T(8,128)S(1)} %collective-permute-done.10.refs_0_), channel_id=1, source_target_pairs={{6,2},{0,4},{10,6},{4,8},{14,10},{8,12},{7,3},{1,5},{11,7},{5,9},{... | collective-permute-start | bytes 1179656 | tf_op jit(solution)/shard_map/ppermute | solution.py:526
  88.7 6.6 %collective-permute-start.22 = (f32[512,128]{1,0:T(8,128)S(1)}, f32[512,128]{1,0:T(8,128)S(1)}, u32[]{:S(2)}, u32[]{:S(2)}) collective-permute-start(f32[512,128]{1,0:T(8,128)S(1)} %collective-permute-done.12), channel_id=1, source_target_pairs={{0,2},{2,0},{4,6},{6,4},{8,10},{10,8},{12,14},{14,12},{1,3},{3,1},... | collective-permute-start | bytes 786440 | tf_op jit(solution)/shard_map/ppermute | solution.py:516
  88.7 7.0 %collective-permute-start.17 = (f32[512,128]{1,0:T(8,128)S(1)}, f32[512,128]{1,0:T(8,128)S(1)}, u32[]{:S(2)}, u32[]{:S(2)}) collective-permute-start(f32[512,128]{1,0:T(8,128)S(1)} %collective-permute-done.16.refs_2_), channel_id=1, source_target_pairs={{0,1},{1,0},{2,3},{3,2},{4,5},{5,4},{6,7},{7,6},{8,9},{9,8},{10,11... | collective-permute-start | bytes 786440 | tf_op jit(solution)/shard_map/ppermute | solution.py:531
  88.8 7.9 %collective-permute-start.15 = (f32[768,128]{1,0:T(8,128)S(1)}, f32[768,128]{1,0:T(8,128)S(1)}, u32[]{:S(2)}, u32[]{:S(2)}) collective-permute-start(f32[768,128]{1,0:T(8,128)S(1)} %collective-permute-done.14.refs_1_), channel_id=1, source_target_pairs={{0,1},{1,0},{2,3},{3,2},{4,5},{5,4},{6,7},{7,6},{8,9},{9,8},{10,11... | collective-permute-start | bytes 1179656 | tf_op jit(solution)/shard_map/ppermute | solution.py:531
  92.4 4.3 %collective-permute-start.13 = (f32[768,128]{1,0:T(8,128)S(1)}, f32[768,128]{1,0:T(8,128)S(1)}, u32[]{:S(2)}, u32[]{:S(2)}) collective-permute-start(f32[768,128]{1,0:T(8,128)S(1)} %collective-permute-done.10.refs_0_), channel_id=1, source_target_pairs={{0,1},{1,0},{2,3},{3,2},{4,5},{5,4},{6,7},{7,6},{8,9},{9,8},{10,11... | collective-permute-start | bytes 1179656 | tf_op jit(solution)/shard_map/ppermute | solution.py:531
  95.2 1.7 %collective-permute-start.21 = (f32[768,128]{1,0:T(8,128)S(1)}, f32[768,128]{1,0:T(8,128)S(1)}, u32[]{:S(2)}, u32[]{:S(2)}) collective-permute-start(f32[768,128]{1,0:T(8,128)S(1)} %collective-permute-done.20.refs_1_), channel_id=1, source_target_pairs={{0,1},{1,0},{2,3},{3,2},{4,5},{5,4},{6,7},{7,6},{8,9},{9,8},{10,11... | collective-permute-start | bytes 1179656 | tf_op jit(solution)/shard_map/ppermute | solution.py:531
  95.2 2.7 %collective-permute-start.19 = (f32[768,128]{1,0:T(8,128)S(1)}, f32[768,128]{1,0:T(8,128)S(1)}, u32[]{:S(2)}, u32[]{:S(2)}) collective-permute-start(f32[768,128]{1,0:T(8,128)S(1)} %collective-permute-done.18.refs_0_), channel_id=1, source_target_pairs={{0,1},{1,0},{2,3},{3,2},{4,5},{5,4},{6,7},{7,6},{8,9},{9,8},{10,11... | collective-permute-start | bytes 1179656 | tf_op jit(solution)/shard_map/ppermute | solution.py:531
  95.7 2.1 %collective-permute-start.23 = (f32[512,128]{1,0:T(8,128)S(1)}, f32[512,128]{1,0:T(8,128)S(1)}, u32[]{:S(2)}, u32[]{:S(2)}) collective-permute-start(f32[512,128]{1,0:T(8,128)S(1)} %collective-permute-done.22.refs_2_), channel_id=1, source_target_pairs={{0,1},{1,0},{2,3},{3,2},{4,5},{5,4},{6,7},{7,6},{8,9},{9,8},{10,11... | collective-permute-start | bytes 786440 | tf_op jit(solution)/shard_map/ppermute | solution.py:531
  97.9 19.1 %copy-start = (f32[2048,128]{1,0:T(8,128)S(1)}, f32[2048,128]{1,0:T(8,128)}, u32[]{:S(2)}) copy-start(f32[2048,128]{1,0:T(8,128)} %values_hbm.1) | copy-start | bytes 3145732
  99.2 3.3 %collective-permute-start.24 = (f32[8,128]{1,0:T(8,128)S(1)}, f32[8,128]{1,0:T(8,128)S(1)}, u32[]{:S(2)}, u32[]{:S(2)}) collective-permute-start(f32[8,128]{1,0:T(8,128)S(1)} %get-tuple-element.73), channel_id=1, source_target_pairs={{0,1},{1,0},{2,3},{3,2},{4,5},{5,4},{6,7},{7,6},{8,9},{9,8},{10,11... | collective-permute-start | bytes 12296 | tf_op jit(solution)/shard_map/ppermute | solution.py:531
  102.4 3.9 %collective-permute-start.25 = (f32[8,128]{1,0:T(8,128)S(1)}, f32[8,128]{1,0:T(8,128)S(1)}, u32[]{:S(2)}, u32[]{:S(2)}) collective-permute-start(f32[8,128]{1,0:T(8,128)S(1)} %add.36), channel_id=1, source_target_pairs={{0,2},{2,0},{4,6},{6,4},{8,10},{10,8},{12,14},{14,12},{1,3},{3,1},... | collective-permute-start | bytes 12296 | tf_op jit(solution)/shard_map/ppermute | solution.py:540
  106.3 6.1 %collective-permute-start.26 = (f32[8,128]{1,0:T(8,128)S(1)}, f32[8,128]{1,0:T(8,128)S(1)}, u32[]{:S(2)}, u32[]{:S(2)}) collective-permute-start(f32[8,128]{1,0:T(8,128)S(1)} %add.37), channel_id=1, source_target_pairs={{0,4},{2,6},{4,0},{6,2},{8,12},{10,14},{12,8},{14,10},{1,5},{3,7},... | collective-permute-start | bytes 12296 | tf_op jit(solution)/shard_map/ppermute | solution.py:540
  112.4 4.6 %collective-permute-start.27 = (f32[8,128]{1,0:T(8,128)S(1)}, f32[8,128]{1,0:T(8,128)S(1)}, u32[]{:S(2)}, u32[]{:S(2)}) collective-permute-start(f32[8,128]{1,0:T(8,128)S(1)} %add.38), channel_id=1, source_target_pairs={{0,8},{2,10},{4,12},{6,14},{8,0},{10,2},{12,4},{14,6},{1,9},{3,11}... | collective-permute-start | bytes 12296 | tf_op jit(solution)/shard_map/ppermute | solution.py:540

commit v4 on v3

--- a/solution.py
+++ b/solution.py
@@ -9,11 +9,10 @@
 
 LANES = 128
 ROWS = 224
-OWN_SLOTS = 72
 SLOTS = 40
 UNROLL = 8
-EVAL_UNROLL = 2
-FIRST_CUTS = (0, 10, 16)
+EVAL_UNROLL = 4
+FIRST_CUTS = (0, 6, 12, 16)
 LATER_CUTS = (0, 6, 12, 16)
 FAR = 1.0e6
 F32 = jnp.float32
@@ -290,9 +289,9 @@
         fill_tile(cache.at[s], rows, facts, work[1, s], windows, pl.multiple_of(work[0, s], 16))
 
 
-def kept_shapes(points, halves, slots):
+def kept_shapes(points, halves):
     return (
-        pltpu.VMEM((slots, ROWS, 2 * LANES), BF16),
+        pltpu.VMEM((SLOTS, ROWS, 2 * LANES), BF16),
         jax.ShapeDtypeStruct((3, list_length(points, halves)), jnp.int32),
         jax.ShapeDtypeStruct((3 * halves * (points // LANES), LANES), F32),
     )
@@ -468,7 +467,7 @@
     return tuple(out)
 
 
-def eval_product(points, own, rows, values, slots, before=(), sent=False):
+def eval_product(points, own, rows, values, before=(), sent=False):
     halves = len(values)
     groups = (*values, before, (), ())
     operands = (own, rows, *(x for group in groups for x in group))
@@ -476,7 +475,7 @@
     counts = [len(group) for group in groups] + [len(images), 0]
     out = pl.pallas_call(
         functools.partial(both_kernel, points, halves, counts),
-        out_shape=(*images, *kept_shapes(points, halves, slots)),
+        out_shape=(*images, *kept_shapes(points, halves)),
         in_specs=[vmem_spec()] * len(operands),
         out_specs=(*[vmem_spec()] * (len(images) + 1), smem_spec(), vmem_spec()),
         scratch_shapes=product_scratch(points, halves) + list_scratch(),
@@ -562,32 +561,36 @@
     given, whole, rows, ranks = sort_points(*operands)
 
     near = [pair_swap(c) for c in given]
-    turned = pair_shift(given[1], 1)
+    turned = pair_shift(given[-1], 1)
     mates = core_swap(whole)
-    image, own_eval = eval_product(points, given[0], rows, (given, (mates,)), OWN_SLOTS)
+    image, own_eval = eval_product(points, given[0], rows, (given,))
     near[0] = after(near[0], image[0], turned)
     far = [pair_shift(near[0])]
-    far.append(pair_swap(after(turned, near[1], near[0])))
+    image, mate_eval = eval_product(points, given[0], rows, ((after(mates, near[0]),),), image)
+    near[1] = after(near[1], image[0])
+    far.append(pair_shift(near[1]))
+    far.append(pair_swap(after(turned, near[2], near[1])))
     near_mates = [core_swap(c) for c in near]
-    image, near_eval = eval_product(points, given[0], rows, (near,), SLOTS, image)
-    far = [after(far[0], image[0], far[1]), far[1]]
+    image, near_eval = eval_product(points, given[0], rows, (near,), image)
+    far = [after(c, image[0]) for c in far]
     far_mates = [core_swap(c) for c in far]
-    image, far_eval = eval_product(points, given[0], rows, (far,), SLOTS, image)
-    (*once, whole), mate_eval = eval_product(points, given[0], rows, (near_mates, far_mates), SLOTS, image, True)
+    image, far_eval = eval_product(points, given[0], rows, (far,), image)
+    (*once, whole), rest_eval = eval_product(points, given[0], rows, (near_mates, far_mates), image, True)
 
     near = [pair_swap(c) for c in once]
     turned = pair_shift(once[-1], 1)
     mates = core_swap(whole)
     image0 = unsort(ranks, after(whole, mates))
-    image = product(points, own_eval, rows, (once, (after(mates, image0),)))
+    image = product(points, own_eval, rows, (once,))
+    image = product(points, mate_eval, rows, ((after(mates, image0),),), image)
     near[0] = after(near[0], image[0], turned)
     far = [pair_shift(c) for c in near[:-1]]
     far.append(pair_swap(after(turned, near[-1], near[0])))
     near_mates = [core_swap(c) for c in near]
     image = product(points, near_eval, rows, (near,), image)
-    far_mates = [core_swap(after(c, image[0])) for c in far]
+    far_mates = [core_swap(after(far[0], image[0])), core_swap(far[1]), core_swap(after(far[2], image[0]))]
     image = product(points, far_eval, rows, (far,), image)
-    twice, sums = product(points, mate_eval, rows, (near_mates, far_mates), image, False, all_sums, given, once)
+    twice, sums = product(points, rest_eval, rows, (near_mates, far_mates), image, False, all_sums, given, once)
     image1 = unsort(ranks, twice)
 
     sums = total(sums, image1)

time: 119 us -> 116 us (0.975)
  waiting for transfers between devices: 21.8 us -> 9.93 us
  starting transfers between devices: 48.8 us -> 55.8 us
  Pallas kernels: 45.5 us -> 47.5 us
    ppermute x7 -> x8, waiting for transfers between devices: 12.5 us -> 3.43 us  [pair_swap(): return lax.ppermute(block, 'tm', [(i, i ^ 1) for i in range(count)])]
    ppermute x5 -> x6, starting transfers between devices: 14.1 us -> 17.3 us  [pair_shift(): return lax.ppermute(block, 'tm', route)]
    ppermute x13 -> x15, starting transfers between devices: 9.57 us -> 11.2 us  [core_swap(): return lax.ppermute(block, 'tile', [(i, i ^ 1) for i in range(count)])]
    ppermute x7 -> x8, starting transfers between devices: 17 us -> 18.5 us  [pair_swap(): return lax.ppermute(block, 'tm', [(i, i ^ 1) for i in range(count)])]
    ppermute x13 -> x15, waiting for transfers between devices: 3 us -> 1.75 us  [core_swap(): return lax.ppermute(block, 'tile', [(i, i ^ 1) for i in range(count)])]
    pallas_call x4 -> x5, Pallas kernels: 21.1 us -> 22.2 us  [eval_product(): pl.pallas_call(functools.partial(both_kernel, points, halves, counts), ou...]
    ppermute x5 -> x6, waiting for transfers between devices: 2.67 us -> 1.58 us  [pair_shift(): return lax.ppermute(block, 'tm', route)]
    pallas_call x4 -> x5, Pallas kernels: 10.3 us -> 11.3 us  [product(): pl.pallas_call(functools.partial(product_kernel, points, len(values), hea...]
  transfers between devices with their start and end apart: 28 -> 32, of which waited for: 12 -> 9; matrix products, arithmetic and copies ran while one was open for 0% -> 0% of each run, Pallas kernels for 28% -> 31%
where the time goes in v4:
time: 116 us
  starting transfers between devices  55.8 us (48%)
  Pallas kernels  47.5 us (41%)
  waiting for transfers between devices  9.93 us (9%)
  other arithmetic  1.85 us (2%)
    pallas_call x5, Pallas kernels, eval_product(): pl.pallas_call(functools.partial(both_kernel, points, halves, counts), ou...  22.2 us
    ppermute x8, starting transfers between devices, pair_swap(): return lax.ppermute(block, 'tm', [(i, i ^ 1) for i in range(count)])  18.5 us
    ppermute x6, starting transfers between devices, pair_shift(): return lax.ppermute(block, 'tm', route)  17.3 us
    pallas_call x5, Pallas kernels, product(): pl.pallas_call(functools.partial(product_kernel, points, len(values), hea...  11.3 us
    ppermute x15, starting transfers between devices, core_swap(): return lax.ppermute(block, 'tile', [(i, i ^ 1) for i in range(count)])  11.2 us
    ppermute x3, starting transfers between devices, stride_sum(): lax.ppermute(value, 'tm', [(i, i ^ step) for i in range(count)])  8.82 us
    pallas_call x1, Pallas kernels, sort_points(): pl.pallas_call(functools.partial(sort_kernel, points), out_shape=tuple((j...  8.75 us
    pallas_call x2, Pallas kernels, unsort(): pl.pallas_call(functools.partial(unsort_kernel, points), out_shape=jax.Sh...  5.31 us
  transfers between devices with their start and end apart: 32, of which 9 were waited for; matrix products, arithmetic and copies ran while one was open for 0% of the time, Pallas kernels for 31%

profile of v4, /device:TPU:0, one launch (start us, length us, event | category | flops | bytes accessed | tf_op | source)
XLA Modules:
  0.0 116.1 jit_solution(16525992635487802841)
XLA Ops:
  0.6 8.8 %sort_points.1 = (f32[824,128]{1,0:T(8,128)S(1)}, f32[768,128]{1,0:T(8,128)S(1)}, f32[512,128]{1,0:T(8,128)S(1)}, f32[2104,128]{1,0:T(8,128)S(1)}, f32[4,2272,128]{2,1,0:T(8,128)S(1)}, /*index=5*/s32[1,2048]{1,0:T(1,128)S(1)}) custom-call(f32[3,2048]{1,0:T(4,128)} %coords_hbm.1, f32[1,2048]{1,0:T(1,128)} %bitcast.5, f32[2048,128]{1,0:T(8,128)} %values_hbm.1), custom_call_target="tpu_custom_call" | custom-call | tf_op jit(solution)/shard_map/sort_points/pallas_call | solution.py:163
  9.9 2.6 %collective-permute-start = (f32[824,128]{1,0:T(8,128)S(1)}, f32[824,128]{1,0:T(8,128)S(1)}, u32[]{:S(2)}, u32[]{:S(2)}) collective-permute-start(f32[824,128]{1,0:T(8,128)S(1)} %get-tuple-element.47.own.refs_0_.refs_7_), channel_id=1, source_target_pairs={{0,2},{2,0},{4,6},{6,4},{8,10},{10,8},{12,14},{14,12},{1,3},{3,1},... | collective-permute-start | bytes 1265672 | tf_op jit(solution)/shard_map/ppermute | solution.py:515
  13.9 4.2 %collective-permute-start.6 = (f32[512,128]{1,0:T(8,128)S(1)}, f32[512,128]{1,0:T(8,128)S(1)}, u32[]{:S(2)}, u32[]{:S(2)}) collective-permute-start(f32[512,128]{1,0:T(8,128)S(1)} %get-tuple-element.50.refs_2_.refs_9_), channel_id=1, source_target_pairs={{0,2},{2,0},{4,6},{6,4},{8,10},{10,8},{12,14},{14,12},{1,3},{3,1},... | collective-permute-start | bytes 786440 | tf_op jit(solution)/shard_map/ppermute | solution.py:515
  18.1 6.1 %eval_product.5 = (f32[2048,128]{1,0:T(8,128)S(1)}, bf16[40,224,256]{2,1,0:T(8,128)(2,1)S(1)}, s32[3,168]{1,0:T(4,128)S(1)}, f32[48,128]{1,0:T(8,128)S(1)}) custom-call(f32[824,128]{1,0:T(8,128)S(1)} %get-tuple-element.47.own.refs_0_.refs_7_, f32[4,2272,128]{2,1,0:T(8,128)S(1)} %get-tuple-element.48.rows, ...), custom_call_target="tpu_custom_call" | custom-call | flops 1000000 | bytes 100000 | tf_op jit(solution)/shard_map/eval_product/pallas_call | solution.py:476
  24.2 3.5 %collective-permute-start.8 = (f32[824,128]{1,0:T(8,128)S(1)}, f32[824,128]{1,0:T(8,128)S(1)}, u32[]{:S(2)}, u32[]{:S(2)}) collective-permute-start(f32[824,128]{1,0:T(8,128)S(1)} %collective-permute-done.refs_0_), channel_id=1, source_target_pairs={{6,2},{0,4},{10,6},{4,8},{14,10},{8,12},{7,3},{1,5},{11,7},{5,9},{... | collective-permute-start | bytes 1265672 | tf_op jit(solution)/shard_map/ppermute | solution.py:525
  27.7 6.1 %eval_product.6 = (f32[2048,128]{1,0:T(8,128)S(1)}, bf16[40,224,256]{2,1,0:T(8,128)(2,1)S(1)}, s32[3,168]{1,0:T(4,128)S(1)}, f32[48,128]{1,0:T(8,128)S(1)}) custom-call(f32[824,128]{1,0:T(8,128)S(1)} %get-tuple-element.47.own.refs_0_.refs_7_, f32[4,2272,128]{2,1,0:T(8,128)S(1)} %get-tuple-element.48.rows, f32[2104,128]{1,0:T(8,128)S(1)} %collective-permute-done.4.refs_0_, ...), custom_call_target="tpu_custom_call" | custom-call | flops 1000000 | bytes 100000 | tf_op jit(solution)/shard_map/eval_product/pallas_call | solution.py:476
  33.8 3.5 %collective-permute-start.10 = (f32[768,128]{1,0:T(8,128)S(1)}, f32[768,128]{1,0:T(8,128)S(1)}, u32[]{:S(2)}, u32[]{:S(2)}) collective-permute-start(f32[768,128]{1,0:T(8,128)S(1)} %collective-permute-done.3.refs_1_), channel_id=1, source_target_pairs={{6,2},{0,4},{10,6},{4,8},{14,10},{8,12},{7,3},{1,5},{11,7},{5,9},{... | collective-permute-start | bytes 1179656 | tf_op jit(solution)/shard_map/ppermute | solution.py:525
  37.3 1.3 %collective-permute-start.12 = (f32[512,128]{1,0:T(8,128)S(1)}, f32[512,128]{1,0:T(8,128)S(1)}, u32[]{:S(2)}, u32[]{:S(2)}) collective-permute-start(f32[512,128]{1,0:T(8,128)S(1)} %collective-permute-done.1), channel_id=1, source_target_pairs={{0,2},{2,0},{4,6},{6,4},{8,10},{10,8},{12,14},{14,12},{1,3},{3,1},... | collective-permute-start | bytes 786440 | tf_op jit(solution)/shard_map/ppermute | solution.py:515
  39.1 6.1 %eval_product.7 = (f32[2048,128]{1,0:T(8,128)S(1)}, bf16[40,224,256]{2,1,0:T(8,128)(2,1)S(1)}, s32[3,168]{1,0:T(4,128)S(1)}, f32[48,128]{1,0:T(8,128)S(1)}) custom-call(f32[824,128]{1,0:T(8,128)S(1)} %get-tuple-element.47.own.refs_0_.refs_7_, f32[4,2272,128]{2,1,0:T(8,128)S(1)} %get-tuple-element.48.rows, f32[824,128]{1,0:T(8,128)S(1)} %collective-permute-done.refs_0_, ...), custom_call_target="tpu_custom_call" | custom-call | flops 1000000 | bytes 100000 | tf_op jit(solution)/shard_map/eval_product/pallas_call | solution.py:476
  46.3 1.9 %eval_product.8 = (f32[2048,128]{1,0:T(8,128)S(1)}, bf16[40,224,256]{2,1,0:T(8,128)(2,1)S(1)}, s32[3,168]{1,0:T(4,128)S(1)}, f32[48,128]{1,0:T(8,128)S(1)}) custom-call(f32[824,128]{1,0:T(8,128)S(1)} %get-tuple-element.47.own.refs_0_.refs_7_, f32[4,2272,128]{2,1,0:T(8,128)S(1)} %get-tuple-element.48.rows, f32[824,128]{1,0:T(8,128)S(1)} %collective-permute-done.8.refs_0_, ...), custom_call_target="tpu_custom_call" | custom-call | flops 1000000 | bytes 100000 | tf_op jit(solution)/shard_map/eval_product/pallas_call | solution.py:476
  48.6 2.0 %eval_product.9 = (f32[768,128]{1,0:T(8,128)S(1)}, f32[768,128]{1,0:T(8,128)S(1)}, f32[512,128]{1,0:T(8,128)S(1)}, f32[2048,128]{1,0:T(8,128)S(1)}, bf16[40,224,...) custom-call(f32[824,128]{1,0:T(8,128)S(1)} %get-tuple-element.47.own.refs_0_.refs_7_, ...), custom_call_target="tpu_custom_call" | custom-call | flops 1000000 | bytes 100000 | tf_op jit(solution)/shard_map/eval_product/pallas_call | solution.py:476
  50.6 5.1 %collective-permute-start.15 = (f32[2048,128]{1,0:T(8,128)S(1)}, f32[2048,128]{1,0:T(8,128)S(1)}, u32[]{:S(2)}, u32[]{:S(2)}) collective-permute-start(f32[2048,128]{1,0:T(8,128)S(1)} %get-tuple-element.72.source), channel_id=1, source_target_pairs={{0,1},{1,0},{2,3},{3,2},{4,5},{5,4},{6,7},{7,6},{8,9},{9,8},{10,11... | collective-permute-start | bytes 3145736 | tf_op jit(solution)/shard_map/ppermute | solution.py:530
  55.7 4.8 %collective-permute-start.18 = (f32[768,128]{1,0:T(8,128)S(1)}, f32[768,128]{1,0:T(8,128)S(1)}, u32[]{:S(2)}, u32[]{:S(2)}) collective-permute-start(f32[768,128]{1,0:T(8,128)S(1)} %get-tuple-element.77.refs_1_.refs_11_), channel_id=1, source_target_pairs={{0,2},{2,0},{4,6},{6,4},{8,10},{10,8},{12,14},{14,12},{1,3},{3,1},... | collective-permute-start | bytes 1179656 | tf_op jit(solution)/shard_map/ppermute | solution.py:515
  61.9 3.7 %collective-permute-start.20 = (f32[512,128]{1,0:T(8,128)S(1)}, f32[512,128]{1,0:T(8,128)S(1)}, u32[]{:S(2)}, u32[]{:S(2)}) collective-permute-start(f32[512,128]{1,0:T(8,128)S(1)} %get-tuple-element.78.refs_2_.refs_12_), channel_id=1, source_target_pairs={{0,2},{2,0},{4,6},{6,4},{8,10},{10,8},{12,14},{14,12},{1,3},{3,1},... | collective-permute-start | bytes 786440 | tf_op jit(solution)/shard_map/ppermute | solution.py:515
  65.5 3.1 %product.5.refs_1_ = f32[2048,128]{1,0:T(8,128)S(1)} custom-call(s32[3,168]{1,0:T(4,128)S(1)} %get-tuple-element.74.work, f32[48,128]{1,0:T(8,128)S(1)} %get-tuple-element.75.facts, f32[4,2272,128]{2,1,0:T(8,128)S(1)} %get-tuple-element.48.rows, bf16[40,224,256]{2,1,0:T(8,128)(2,1)S(1)} %get-tuple-element.76.cache, ...), custom_call_target="tpu_custom_call" | custom-call | flops 1000000 | bytes 100000 | tf_op jit(solution)/shard_map/product/pallas_call | solution.py:457
  68.7 1.8 %collective-permute-done.18.refs_1_ = f32[768,128]{1,0:T(8,128)S(1)} collective-permute-done((f32[768,128]{1,0:T(8,128)S(1)}, f32[768,128]{1,0:T(8,128)S(1)}, u32[]{:S(2)}, u32[]{:S(2)}) %collective-permute-start.18) | collective-permute-done | bytes 393248 | tf_op jit(solution)/shard_map/ppermute | solution.py:515
  70.5 4.5 %collective-permute-start.24 = (f32[768,128]{1,0:T(8,128)S(1)}, f32[768,128]{1,0:T(8,128)S(1)}, u32[]{:S(2)}, u32[]{:S(2)}) collective-permute-start(f32[768,128]{1,0:T(8,128)S(1)} %collective-permute-done.18.refs_1_), channel_id=1, source_target_pairs={{6,2},{0,4},{10,6},{4,8},{14,10},{8,12},{7,3},{1,5},{11,7},{5,9},{... | collective-permute-start | bytes 1179656 | tf_op jit(solution)/shard_map/ppermute | solution.py:525
  75.0 2.7 %unsort.2 = f32[2048,128]{1,0:T(8,128)S(1)} custom-call(s32[1,2048]{1,0:T(1,128)S(1)} %get-tuple-element.71.ranks, f32[2048,128]{1,0:T(8,128)S(1)} %get-tuple-element.72.source), custom_call_target="tpu_custom_call" | custom-call | flops 1000000 | bytes 100000 | tf_op jit(solution)/shard_map/unsort/pallas_call | solution.py:502
  77.7 3.0 %product.6.refs_3_ = f32[2048,128]{1,0:T(8,128)S(1)} custom-call(s32[3,168]{1,0:T(4,128)S(1)} %get-tuple-element.67.work, f32[48,128]{1,0:T(8,128)S(1)} %get-tuple-element.68.facts, f32[4,2272,128]{2,1,0:T(8,128)S(1)} %get-tuple-element.48.rows, bf16[40,224,256]{2,1,0:T(8,128)(2,1)S(1)} %get-tuple-element.69.cache, ...), custom_call_target="tpu_custom_call" | custom-call | flops 1000000 | bytes 100000 | tf_op jit(solution)/shard_map/product/pallas_call | solution.py:457
  80.7 3.1 %collective-permute-start.22 = (f32[768,128]{1,0:T(8,128)S(1)}, f32[768,128]{1,0:T(8,128)S(1)}, u32[]{:S(2)}, u32[]{:S(2)}) collective-permute-start(f32[768,128]{1,0:T(8,128)S(1)} %collective-permute-done.14.refs_0_), channel_id=1, source_target_pairs={{6,2},{0,4},{10,6},{4,8},{14,10},{8,12},{7,3},{1,5},{11,7},{5,9},{... | collective-permute-start | bytes 1179656 | tf_op jit(solution)/shard_map/ppermute | solution.py:525
  84.2 1.8 %collective-permute-start.26 = (f32[512,128]{1,0:T(8,128)S(1)}, f32[512,128]{1,0:T(8,128)S(1)}, u32[]{:S(2)}, u32[]{:S(2)}) collective-permute-start(f32[512,128]{1,0:T(8,128)S(1)} %collective-permute-done.16), channel_id=1, source_target_pairs={{0,2},{2,0},{4,6},{6,4},{8,10},{10,8},{12,14},{14,12},{1,3},{3,1},... | collective-permute-start | bytes 786440 | tf_op jit(solution)/shard_map/ppermute | solution.py:515
  86.5 3.0 %product.7.refs_3_ = f32[2048,128]{1,0:T(8,128)S(1)} custom-call(s32[3,168]{1,0:T(4,128)S(1)} %get-tuple-element.80.work, f32[48,128]{1,0:T(8,128)S(1)} %get-tuple-element.81.facts, f32[4,2272,128]{2,1,0:T(8,128)S(1)} %get-tuple-element.48.rows, bf16[40,224,256]{2,1,0:T(8,128)(2,1)S(1)} %get-tuple-element.82.cache, ...), custom_call_target="tpu_custom_call" | custom-call | flops 1000000 | bytes 100000 | tf_op jit(solution)/shard_map/product/pallas_call | solution.py:457
  89.5 1.6 %collective-permute-done.22.refs_0_ = f32[768,128]{1,0:T(8,128)S(1)} collective-permute-done((f32[768,128]{1,0:T(8,128)S(1)}, f32[768,128]{1,0:T(8,128)S(1)}, u32[]{:S(2)}, u32[]{:S(2)}) %collective-permute-start.22) | collective-permute-done | bytes 393248 | tf_op jit(solution)/shard_map/ppermute | solution.py:525
  94.4 1.3 %product.9 = (f32[2048,128]{1,0:T(8,128)S(1)}, f32[8,128]{1,0:T(8,128)S(1)}) custom-call(s32[3,328]{1,0:T(4,128)S(1)} %get-tuple-element.63.work, f32[96,128]{1,0:T(8,128)S(1)} %get-tuple-element.64.facts, f32[4,2272,128]{2,1,0:T(8,128)S(1)} %get-tuple-element.48.rows, bf16[40,224,256]{2,1,0:T(8,128)(2,1)S(1)} %get-tuple-element.65.cache, ...), custom_call_target="tpu_custom_call" | custom-call | flops 1000000 | bytes 100000 | tf_op jit(solution)/shard_map/product/pallas_call | solution.py:457
  95.7 3.0 %collective-permute-start.28 = (f32[8,128]{1,0:T(8,128)S(1)}, f32[8,128]{1,0:T(8,128)S(1)}, u32[]{:S(2)}, u32[]{:S(2)}) collective-permute-start(f32[8,128]{1,0:T(8,128)S(1)} %get-tuple-element.89), channel_id=1, source_target_pairs={{0,1},{1,0},{2,3},{3,2},{4,5},{5,4},{6,7},{7,6},{8,9},{9,8},{10,11... | collective-permute-start | bytes 12296 | tf_op jit(solution)/shard_map/ppermute | solution.py:530
  99.5 3.3 %collective-permute-start.29 = (f32[8,128]{1,0:T(8,128)S(1)}, f32[8,128]{1,0:T(8,128)S(1)}, u32[]{:S(2)}, u32[]{:S(2)}) collective-permute-start(f32[8,128]{1,0:T(8,128)S(1)} %add.36), channel_id=1, source_target_pairs={{0,2},{2,0},{4,6},{6,4},{8,10},{10,8},{12,14},{14,12},{1,3},{3,1},... | collective-permute-start | bytes 12296 | tf_op jit(solution)/shard_map/ppermute | solution.py:539
  102.8 1.6 %collective-permute-done.29 = f32[8,128]{1,0:T(8,128)S(1)} collective-permute-done((f32[8,128]{1,0:T(8,128)S(1)}, f32[8,128]{1,0:T(8,128)S(1)}, u32[]{:S(2)}, u32[]{:S(2)}) %collective-permute-start.29) | collective-permute-done | bytes 4128 | tf_op jit(solution)/shard_map/ppermute | solution.py:539
  104.4 1.4 %collective-permute-start.30 = (f32[8,128]{1,0:T(8,128)S(1)}, f32[8,128]{1,0:T(8,128)S(1)}, u32[]{:S(2)}, u32[]{:S(2)}) collective-permute-start(f32[8,128]{1,0:T(8,128)S(1)} %add.37), channel_id=1, source_target_pairs={{0,4},{2,6},{4,0},{6,2},{8,12},{10,14},{12,8},{14,10},{1,5},{3,7},... | collective-permute-start | bytes 12296 | tf_op jit(solution)/shard_map/ppermute | solution.py:539
  105.8 2.7 %unsort.3 = f32[2048,128]{1,0:T(8,128)S(1)} custom-call(s32[1,2048]{1,0:T(1,128)S(1)} %get-tuple-element.71.ranks, f32[2048,128]{1,0:T(8,128)S(1)} %get-tuple-element.90.source), custom_call_target="tpu_custom_call" | custom-call | flops 1000000 | bytes 100000 | tf_op jit(solution)/shard_map/unsort/pallas_call | solution.py:502
  108.5 4.1 %collective-permute-start.31 = (f32[8,128]{1,0:T(8,128)S(1)}, f32[8,128]{1,0:T(8,128)S(1)}, u32[]{:S(2)}, u32[]{:S(2)}) collective-permute-start(f32[8,128]{1,0:T(8,128)S(1)} %add.38), channel_id=1, source_target_pairs={{0,8},{2,10},{4,12},{6,14},{8,0},{10,2},{12,4},{14,6},{1,9},{3,11}... | collective-permute-start | bytes 12296 | tf_op jit(solution)/shard_map/ppermute | solution.py:539
  112.6 1.6 %collective-permute-done.31 = f32[8,128]{1,0:T(8,128)S(1)} collective-permute-done((f32[8,128]{1,0:T(8,128)S(1)}, f32[8,128]{1,0:T(8,128)S(1)}, u32[]{:S(2)}, u32[]{:S(2)}) %collective-permute-start.31) | collective-permute-done | bytes 4128 | tf_op jit(solution)/shard_map/ppermute | solution.py:539
  114.3 1.8 %multiply_subtract_fusion = (f32[2048,128]{1,0:T(8,128)}, f32[2048,128]{1,0:T(8,128)}) fusion(f32[2048,128]{1,0:T(8,128)S(1)} %unsort.2, f32[2048,128]{1,0:T(8,128)S(1)} %unsort.3, f32[2048,128]{1,0:T(8,128)S(1)} %copy-done, f32[128]{0:T(128)S(1)} %bitcast.7, f32[128]{0:T(128)S(1)} %get-tuple-element.92, f32[128]{0:T(128)S(1)} %bitcast.6), kind=kLoop, calls=%fused_computation | loop fusion | flops 3407872 | bytes 5244416 | tf_op jit(solution)/shard_map/sub | solution.py:607
  (54 shorter events, 10.2 us)
Async XLA Ops:
  9.4 18.3 %collective-permute-start.4 = (f32[2104,128]{1,0:T(8,128)S(1)}, f32[2104,128]{1,0:T(8,128)S(1)}, u32[]{:S(2)}, u32[]{:S(2)}) collective-permute-start(f32[2104,128]{1,0:T(8,128)S(1)} %get-tuple-element.53), channel_id=1, source_target_pairs={{0,1},{1,0},{2,3},{3,2},{4,5},{5,4},{6,7},{7,6},{8,9},{9,8},{10,11... | collective-permute-start | bytes 3231752 | tf_op jit(solution)/shard_map/ppermute | solution.py:530
  9.9 14.3 %collective-permute-start = (f32[824,128]{1,0:T(8,128)S(1)}, f32[824,128]{1,0:T(8,128)S(1)}, u32[]{:S(2)}, u32[]{:S(2)}) collective-permute-start(f32[824,128]{1,0:T(8,128)S(1)} %get-tuple-element.47.own.refs_0_.refs_7_), channel_id=1, source_target_pairs={{0,2},{2,0},{4,6},{6,4},{8,10},{10,8},{12,14},{14,12},{1,3},{3,1},... | collective-permute-start | bytes 1265672 | tf_op jit(solution)/shard_map/ppermute | solution.py:515
  12.5 21.3 %collective-permute-start.3 = (f32[768,128]{1,0:T(8,128)S(1)}, f32[768,128]{1,0:T(8,128)S(1)}, u32[]{:S(2)}, u32[]{:S(2)}) collective-permute-start(f32[768,128]{1,0:T(8,128)S(1)} %get-tuple-element.49.refs_1_.refs_8_), channel_id=1, source_target_pairs={{0,2},{2,0},{4,6},{6,4},{8,10},{10,8},{12,14},{14,12},{1,3},{3,1},... | collective-permute-start | bytes 1179656 | tf_op jit(solution)/shard_map/ppermute | solution.py:515
  12.6 11.6 %collective-permute-start.1 = (f32[512,128]{1,0:T(8,128)S(1)}, f32[512,128]{1,0:T(8,128)S(1)}, u32[]{:S(2)}, u32[]{:S(2)}) collective-permute-start(f32[512,128]{1,0:T(8,128)S(1)} %get-tuple-element.50.refs_2_.refs_9_), channel_id=1, source_target_pairs={{4,0},{8,4},{2,6},{12,8},{6,10},{10,14},{5,1},{9,5},{3,7},{13,9},{... | collective-permute-start | bytes 786440 | tf_op jit(solution)/shard_map/ppermute | solution.py:525
  13.9 23.5 %collective-permute-start.6 = (f32[512,128]{1,0:T(8,128)S(1)}, f32[512,128]{1,0:T(8,128)S(1)}, u32[]{:S(2)}, u32[]{:S(2)}) collective-permute-start(f32[512,128]{1,0:T(8,128)S(1)} %get-tuple-element.50.refs_2_.refs_9_), channel_id=1, source_target_pairs={{0,2},{2,0},{4,6},{6,4},{8,10},{10,8},{12,14},{14,12},{1,3},{3,1},... | collective-permute-start | bytes 786440 | tf_op jit(solution)/shard_map/ppermute | solution.py:515
  24.2 21.0 %collective-permute-start.8 = (f32[824,128]{1,0:T(8,128)S(1)}, f32[824,128]{1,0:T(8,128)S(1)}, u32[]{:S(2)}, u32[]{:S(2)}) collective-permute-start(f32[824,128]{1,0:T(8,128)S(1)} %collective-permute-done.refs_0_), channel_id=1, source_target_pairs={{6,2},{0,4},{10,6},{4,8},{14,10},{8,12},{7,3},{1,5},{11,7},{5,9},{... | collective-permute-start | bytes 1265672 | tf_op jit(solution)/shard_map/ppermute | solution.py:525
  33.8 11.5 %collective-permute-start.10 = (f32[768,128]{1,0:T(8,128)S(1)}, f32[768,128]{1,0:T(8,128)S(1)}, u32[]{:S(2)}, u32[]{:S(2)}) collective-permute-start(f32[768,128]{1,0:T(8,128)S(1)} %collective-permute-done.3.refs_1_), channel_id=1, source_target_pairs={{6,2},{0,4},{10,6},{4,8},{14,10},{8,12},{7,3},{1,5},{11,7},{5,9},{... | collective-permute-start | bytes 1179656 | tf_op jit(solution)/shard_map/ppermute | solution.py:525
  37.3 8.5 %collective-permute-start.12 = (f32[512,128]{1,0:T(8,128)S(1)}, f32[512,128]{1,0:T(8,128)S(1)}, u32[]{:S(2)}, u32[]{:S(2)}) collective-permute-start(f32[512,128]{1,0:T(8,128)S(1)} %collective-permute-done.1), channel_id=1, source_target_pairs={{0,2},{2,0},{4,6},{6,4},{8,10},{10,8},{12,14},{14,12},{1,3},{3,1},... | collective-permute-start | bytes 786440 | tf_op jit(solution)/shard_map/ppermute | solution.py:515
  38.6 7.3 %collective-permute-start.7 = (f32[512,128]{1,0:T(8,128)S(1)}, f32[512,128]{1,0:T(8,128)S(1)}, u32[]{:S(2)}, u32[]{:S(2)}) collective-permute-start(f32[512,128]{1,0:T(8,128)S(1)} %collective-permute-done.6.refs_2_), channel_id=1, source_target_pairs={{0,1},{1,0},{2,3},{3,2},{4,5},{5,4},{6,7},{7,6},{8,9},{9,8},{10,11... | collective-permute-start | bytes 786440 | tf_op jit(solution)/shard_map/ppermute | solution.py:530
  38.6 9.6 %collective-permute-start.2 = (f32[824,128]{1,0:T(8,128)S(1)}, f32[824,128]{1,0:T(8,128)S(1)}, u32[]{:S(2)}, u32[]{:S(2)}) collective-permute-start(f32[824,128]{1,0:T(8,128)S(1)} %collective-permute-done.refs_0_), channel_id=1, source_target_pairs={{0,1},{1,0},{2,3},{3,2},{4,5},{5,4},{6,7},{7,6},{8,9},{9,8},{10,11... | collective-permute-start | bytes 1265672 | tf_op jit(solution)/shard_map/ppermute | solution.py:530
  45.2 3.1 %collective-permute-start.9 = (f32[824,128]{1,0:T(8,128)S(1)}, f32[824,128]{1,0:T(8,128)S(1)}, u32[]{:S(2)}, u32[]{:S(2)}) collective-permute-start(f32[824,128]{1,0:T(8,128)S(1)} %collective-permute-done.8.refs_0_), channel_id=1, source_target_pairs={{0,1},{1,0},{2,3},{3,2},{4,5},{5,4},{6,7},{7,6},{8,9},{9,8},{10,11... | collective-permute-start | bytes 1265672 | tf_op jit(solution)/shard_map/ppermute | solution.py:530
  45.3 3.0 %collective-permute-start.5 = (f32[768,128]{1,0:T(8,128)S(1)}, f32[768,128]{1,0:T(8,128)S(1)}, u32[]{:S(2)}, u32[]{:S(2)}) collective-permute-start(f32[768,128]{1,0:T(8,128)S(1)} %collective-permute-done.3.refs_1_), channel_id=1, source_target_pairs={{0,1},{1,0},{2,3},{3,2},{4,5},{5,4},{6,7},{7,6},{8,9},{9,8},{10,11... | collective-permute-start | bytes 1179656 | tf_op jit(solution)/shard_map/ppermute | solution.py:530
  45.8 2.7 %collective-permute-start.11 = (f32[768,128]{1,0:T(8,128)S(1)}, f32[768,128]{1,0:T(8,128)S(1)}, u32[]{:S(2)}, u32[]{:S(2)}) collective-permute-start(f32[768,128]{1,0:T(8,128)S(1)} %collective-permute-done.10.refs_1_), channel_id=1, source_target_pairs={{0,1},{1,0},{2,3},{3,2},{4,5},{5,4},{6,7},{7,6},{8,9},{9,8},{10,11... | collective-permute-start | bytes 1179656 | tf_op jit(solution)/shard_map/ppermute | solution.py:530
  45.9 2.7 %collective-permute-start.13 = (f32[512,128]{1,0:T(8,128)S(1)}, f32[512,128]{1,0:T(8,128)S(1)}, u32[]{:S(2)}, u32[]{:S(2)}) collective-permute-start(f32[512,128]{1,0:T(8,128)S(1)} %collective-permute-done.12.refs_2_), channel_id=1, source_target_pairs={{0,1},{1,0},{2,3},{3,2},{4,5},{5,4},{6,7},{7,6},{8,9},{9,8},{10,11... | collective-permute-start | bytes 786440 | tf_op jit(solution)/shard_map/ppermute | solution.py:530
  50.6 24.4 %collective-permute-start.15 = (f32[2048,128]{1,0:T(8,128)S(1)}, f32[2048,128]{1,0:T(8,128)S(1)}, u32[]{:S(2)}, u32[]{:S(2)}) collective-permute-start(f32[2048,128]{1,0:T(8,128)S(1)} %get-tuple-element.72.source), channel_id=1, source_target_pairs={{0,1},{1,0},{2,3},{3,2},{4,5},{5,4},{6,7},{7,6},{8,9},{9,8},{10,11... | collective-permute-start | bytes 3145736 | tf_op jit(solution)/shard_map/ppermute | solution.py:530
  55.7 14.8 %collective-permute-start.18 = (f32[768,128]{1,0:T(8,128)S(1)}, f32[768,128]{1,0:T(8,128)S(1)}, u32[]{:S(2)}, u32[]{:S(2)}) collective-permute-start(f32[768,128]{1,0:T(8,128)S(1)} %get-tuple-element.77.refs_1_.refs_11_), channel_id=1, source_target_pairs={{0,2},{2,0},{4,6},{6,4},{8,10},{10,8},{12,14},{14,12},{1,3},{3,1},... | collective-permute-start | bytes 1179656 | tf_op jit(solution)/shard_map/ppermute | solution.py:515
  60.5 20.2 %collective-permute-start.14 = (f32[768,128]{1,0:T(8,128)S(1)}, f32[768,128]{1,0:T(8,128)S(1)}, u32[]{:S(2)}, u32[]{:S(2)}) collective-permute-start(f32[768,128]{1,0:T(8,128)S(1)} %get-tuple-element.66.refs_0_.refs_10_), channel_id=1, source_target_pairs={{0,2},{2,0},{4,6},{6,4},{8,10},{10,8},{12,14},{14,12},{1,3},{3,1},... | collective-permute-start | bytes 1179656 | tf_op jit(solution)/shard_map/ppermute | solution.py:515
  60.6 20.1 %collective-permute-start.16 = (f32[512,128]{1,0:T(8,128)S(1)}, f32[512,128]{1,0:T(8,128)S(1)}, u32[]{:S(2)}, u32[]{:S(2)}) collective-permute-start(f32[512,128]{1,0:T(8,128)S(1)} %get-tuple-element.78.refs_2_.refs_12_), channel_id=1, source_target_pairs={{4,0},{8,4},{2,6},{12,8},{6,10},{10,14},{5,1},{9,5},{3,7},{13,9},{... | collective-permute-start | bytes 786440 | tf_op jit(solution)/shard_map/ppermute | solution.py:525
  61.9 22.4 %collective-permute-start.20 = (f32[512,128]{1,0:T(8,128)S(1)}, f32[512,128]{1,0:T(8,128)S(1)}, u32[]{:S(2)}, u32[]{:S(2)}) collective-permute-start(f32[512,128]{1,0:T(8,128)S(1)} %get-tuple-element.78.refs_2_.refs_12_), channel_id=1, source_target_pairs={{0,2},{2,0},{4,6},{6,4},{8,10},{10,8},{12,14},{14,12},{1,3},{3,1},... | collective-permute-start | bytes 786440 | tf_op jit(solution)/shard_map/ppermute | solution.py:515
  70.5 16.1 %collective-permute-start.24 = (f32[768,128]{1,0:T(8,128)S(1)}, f32[768,128]{1,0:T(8,128)S(1)}, u32[]{:S(2)}, u32[]{:S(2)}) collective-permute-start(f32[768,128]{1,0:T(8,128)S(1)} %collective-permute-done.18.refs_1_), channel_id=1, source_target_pairs={{6,2},{0,4},{10,6},{4,8},{14,10},{8,12},{7,3},{1,5},{11,7},{5,9},{... | collective-permute-start | bytes 1179656 | tf_op jit(solution)/shard_map/ppermute | solution.py:525
  80.7 10.4 %collective-permute-start.22 = (f32[768,128]{1,0:T(8,128)S(1)}, f32[768,128]{1,0:T(8,128)S(1)}, u32[]{:S(2)}, u32[]{:S(2)}) collective-permute-start(f32[768,128]{1,0:T(8,128)S(1)} %collective-permute-done.14.refs_0_), channel_id=1, source_target_pairs={{6,2},{0,4},{10,6},{4,8},{14,10},{8,12},{7,3},{1,5},{11,7},{5,9},{... | collective-permute-start | bytes 1179656 | tf_op jit(solution)/shard_map/ppermute | solution.py:525
  84.2 8.1 %collective-permute-start.26 = (f32[512,128]{1,0:T(8,128)S(1)}, f32[512,128]{1,0:T(8,128)S(1)}, u32[]{:S(2)}, u32[]{:S(2)}) collective-permute-start(f32[512,128]{1,0:T(8,128)S(1)} %collective-permute-done.16), channel_id=1, source_target_pairs={{0,2},{2,0},{4,6},{6,4},{8,10},{10,8},{12,14},{14,12},{1,3},{3,1},... | collective-permute-start | bytes 786440 | tf_op jit(solution)/shard_map/ppermute | solution.py:515
  86.0 6.3 %collective-permute-start.21 = (f32[512,128]{1,0:T(8,128)S(1)}, f32[512,128]{1,0:T(8,128)S(1)}, u32[]{:S(2)}, u32[]{:S(2)}) collective-permute-start(f32[512,128]{1,0:T(8,128)S(1)} %collective-permute-done.20.refs_2_), channel_id=1, source_target_pairs={{0,1},{1,0},{2,3},{3,2},{4,5},{5,4},{6,7},{7,6},{8,9},{9,8},{10,11... | collective-permute-start | bytes 786440 | tf_op jit(solution)/shard_map/ppermute | solution.py:530
  86.0 7.7 %collective-permute-start.19 = (f32[768,128]{1,0:T(8,128)S(1)}, f32[768,128]{1,0:T(8,128)S(1)}, u32[]{:S(2)}, u32[]{:S(2)}) collective-permute-start(f32[768,128]{1,0:T(8,128)S(1)} %collective-permute-done.18.refs_1_), channel_id=1, source_target_pairs={{0,1},{1,0},{2,3},{3,2},{4,5},{5,4},{6,7},{7,6},{8,9},{9,8},{10,11... | collective-permute-start | bytes 1179656 | tf_op jit(solution)/shard_map/ppermute | solution.py:530
  86.5 7.2 %collective-permute-start.25 = (f32[768,128]{1,0:T(8,128)S(1)}, f32[768,128]{1,0:T(8,128)S(1)}, u32[]{:S(2)}, u32[]{:S(2)}) collective-permute-start(f32[768,128]{1,0:T(8,128)S(1)} %collective-permute-done.24.refs_1_), channel_id=1, source_target_pairs={{0,1},{1,0},{2,3},{3,2},{4,5},{5,4},{6,7},{7,6},{8,9},{9,8},{10,11... | collective-permute-start | bytes 1179656 | tf_op jit(solution)/shard_map/ppermute | solution.py:530
  91.1 2.7 %collective-permute-start.17 = (f32[768,128]{1,0:T(8,128)S(1)}, f32[768,128]{1,0:T(8,128)S(1)}, u32[]{:S(2)}, u32[]{:S(2)}) collective-permute-start(f32[768,128]{1,0:T(8,128)S(1)} %collective-permute-done.14.refs_0_), channel_id=1, source_target_pairs={{0,1},{1,0},{2,3},{3,2},{4,5},{5,4},{6,7},{7,6},{8,9},{9,8},{10,11... | collective-permute-start | bytes 1179656 | tf_op jit(solution)/shard_map/ppermute | solution.py:530
  92.3 2.1 %collective-permute-start.23 = (f32[768,128]{1,0:T(8,128)S(1)}, f32[768,128]{1,0:T(8,128)S(1)}, u32[]{:S(2)}, u32[]{:S(2)}) collective-permute-start(f32[768,128]{1,0:T(8,128)S(1)} %collective-permute-done.22.refs_0_), channel_id=1, source_target_pairs={{0,1},{1,0},{2,3},{3,2},{4,5},{5,4},{6,7},{7,6},{8,9},{9,8},{10,11... | collective-permute-start | bytes 1179656 | tf_op jit(solution)/shard_map/ppermute | solution.py:530
  92.3 2.1 %collective-permute-start.27 = (f32[512,128]{1,0:T(8,128)S(1)}, f32[512,128]{1,0:T(8,128)S(1)}, u32[]{:S(2)}, u32[]{:S(2)}) collective-permute-start(f32[512,128]{1,0:T(8,128)S(1)} %collective-permute-done.26.refs_2_), channel_id=1, source_target_pairs={{0,1},{1,0},{2,3},{3,2},{4,5},{5,4},{6,7},{7,6},{8,9},{9,8},{10,11... | collective-permute-start | bytes 786440 | tf_op jit(solution)/shard_map/ppermute | solution.py:530
  95.7 3.8 %collective-permute-start.28 = (f32[8,128]{1,0:T(8,128)S(1)}, f32[8,128]{1,0:T(8,128)S(1)}, u32[]{:S(2)}, u32[]{:S(2)}) collective-permute-start(f32[8,128]{1,0:T(8,128)S(1)} %get-tuple-element.89), channel_id=1, source_target_pairs={{0,1},{1,0},{2,3},{3,2},{4,5},{5,4},{6,7},{7,6},{8,9},{9,8},{10,11... | collective-permute-start | bytes 12296 | tf_op jit(solution)/shard_map/ppermute | solution.py:530
  99.5 4.9 %collective-permute-start.29 = (f32[8,128]{1,0:T(8,128)S(1)}, f32[8,128]{1,0:T(8,128)S(1)}, u32[]{:S(2)}, u32[]{:S(2)}) collective-permute-start(f32[8,128]{1,0:T(8,128)S(1)} %add.36), channel_id=1, source_target_pairs={{0,2},{2,0},{4,6},{6,4},{8,10},{10,8},{12,14},{14,12},{1,3},{3,1},... | collective-permute-start | bytes 12296 | tf_op jit(solution)/shard_map/ppermute | solution.py:539
  104.4 4.1 %collective-permute-start.30 = (f32[8,128]{1,0:T(8,128)S(1)}, f32[8,128]{1,0:T(8,128)S(1)}, u32[]{:S(2)}, u32[]{:S(2)}) collective-permute-start(f32[8,128]{1,0:T(8,128)S(1)} %add.37), channel_id=1, source_target_pairs={{0,4},{2,6},{4,0},{6,2},{8,12},{10,14},{12,8},{14,10},{1,5},{3,7},... | collective-permute-start | bytes 12296 | tf_op jit(solution)/shard_map/ppermute | solution.py:539
  108.5 5.7 %collective-permute-start.31 = (f32[8,128]{1,0:T(8,128)S(1)}, f32[8,128]{1,0:T(8,128)S(1)}, u32[]{:S(2)}, u32[]{:S(2)}) collective-permute-start(f32[8,128]{1,0:T(8,128)S(1)} %add.38), channel_id=1, source_target_pairs={{0,8},{2,10},{4,12},{6,14},{8,0},{10,2},{12,4},{14,6},{1,9},{3,11}... | collective-permute-start | bytes 12296 | tf_op jit(solution)/shard_map/ppermute | solution.py:539
  (1 other events, 19.8 us)

commit v5 on v4

--- a/solution.py
+++ b/solution.py
@@ -107,7 +107,7 @@
                 out.append(carry[ig] + jnp.where(before, 1.0, 0.0))
             return tuple(out)
 
-        counts = lax.fori_loop(0, LANES // 8, count, counts, unroll=2)
+        counts = lax.fori_loop(0, LANES // 8, count, counts, unroll=4)
     for g in range(groups):
         rank_row[0:1, g * LANES : (g + 1) * LANES] = jnp.sum(counts[g], axis=0, keepdims=True).astype(jnp.int32)
     ranks[...] = rank_row[...]
@@ -131,7 +131,7 @@
             sorted_values[pl.ds(to, 1), :] = block[k : k + 1, :]
         return carry
 
-    lax.fori_loop(0, points // 8, scatter, 0, unroll=4)
+    lax.fori_loop(0, points // 8, scatter, 0, unroll=8)
     header = header_rows(points)
     whole = out_values[pieces]
     whole[header:, :] = sorted_values[...]
@@ -317,7 +317,7 @@
                 pairs[base + w, LANES:, :] = both
                 return carry
 
-            lax.fori_loop(0, size // LANES, split, 0)
+            lax.fori_loop(0, size // LANES, split, 0, unroll=2)
 
 
 def multiply(work, cache, pairs, acc, step, count):
@@ -494,7 +494,7 @@
         )
         return carry
 
-    lax.fori_loop(0, points // 8, gather, 0, unroll=4)
+    lax.fori_loop(0, points // 8, gather, 0, unroll=8)
 
 
 def unsort(ranks, source):

time: 116 us -> 115 us (level)
  no operation moved by 1% of the time
where the time goes in v5:
time: 115 us; the launch traced here: 114 us
  starting transfers between devices  55.6 us (48%)
  Pallas kernels  46.6 us (41%)
  waiting for transfers between devices  9.18 us (8%)
  other arithmetic  1.85 us (2%)
    pallas_call x5, Pallas kernels, eval_product(): pl.pallas_call(functools.partial(both_kernel, points, halves, counts), ou...  22.2 us
    ppermute x8, starting transfers between devices, pair_swap(): return lax.ppermute(block, 'tm', [(i, i ^ 1) for i in range(count)])  19.1 us
    ppermute x6, starting transfers between devices, pair_shift(): return lax.ppermute(block, 'tm', route)  17.8 us
    pallas_call x5, Pallas kernels, product(): pl.pallas_call(functools.partial(product_kernel, points, len(values), hea...  11.1 us
    ppermute x15, starting transfers between devices, core_swap(): return lax.ppermute(block, 'tile', [(i, i ^ 1) for i in range(count)])  10.1 us
    ppermute x3, starting transfers between devices, stride_sum(): lax.ppermute(value, 'tm', [(i, i ^ step) for i in range(count)])  8.67 us
    pallas_call x1, Pallas kernels, sort_points(): pl.pallas_call(functools.partial(sort_kernel, points), out_shape=tuple((j...  8.37 us
    pallas_call x2, Pallas kernels, unsort(): pl.pallas_call(functools.partial(unsort_kernel, points), out_shape=jax.Sh...  4.94 us
  transfers between devices with their start and end apart: 32, of which 9 were waited for; matrix products, arithmetic and copies ran while one was open for 0% of the time, Pallas kernels for 31%

profile of v5, /device:TPU:0, one launch (start us, length us, event | category | flops | bytes accessed | tf_op | source)
XLA Modules:
  0.0 114.2 jit_solution(13537715721986998359)
XLA Ops:
  0.6 8.4 %sort_points.1 = (f32[824,128]{1,0:T(8,128)S(1)}, f32[768,128]{1,0:T(8,128)S(1)}, f32[512,128]{1,0:T(8,128)S(1)}, f32[2104,128]{1,0:T(8,128)S(1)}, f32[4,2272,128]{2,1,0:T(8,128)S(1)}, /*index=5*/s32[1,2048]{1,0:T(1,128)S(1)}) custom-call(f32[3,2048]{1,0:T(4,128)} %coords_hbm.1, f32[1,2048]{1,0:T(1,128)} %bitcast.5, f32[2048,128]{1,0:T(8,128)} %values_hbm.1), custom_call_target="tpu_custom_call" | custom-call | tf_op jit(solution)/shard_map/sort_points/pallas_call | solution.py:163
  9.5 2.6 %collective-permute-start = (f32[824,128]{1,0:T(8,128)S(1)}, f32[824,128]{1,0:T(8,128)S(1)}, u32[]{:S(2)}, u32[]{:S(2)}) collective-permute-start(f32[824,128]{1,0:T(8,128)S(1)} %get-tuple-element.47.own.refs_0_.refs_7_), channel_id=1, source_target_pairs={{0,2},{2,0},{4,6},{6,4},{8,10},{10,8},{12,14},{14,12},{1,3},{3,1},... | collective-permute-start | bytes 1265672 | tf_op jit(solution)/shard_map/ppermute | solution.py:515
  13.5 4.2 %collective-permute-start.6 = (f32[512,128]{1,0:T(8,128)S(1)}, f32[512,128]{1,0:T(8,128)S(1)}, u32[]{:S(2)}, u32[]{:S(2)}) collective-permute-start(f32[512,128]{1,0:T(8,128)S(1)} %get-tuple-element.50.refs_2_.refs_9_), channel_id=1, source_target_pairs={{0,2},{2,0},{4,6},{6,4},{8,10},{10,8},{12,14},{14,12},{1,3},{3,1},... | collective-permute-start | bytes 786440 | tf_op jit(solution)/shard_map/ppermute | solution.py:515
  17.7 6.1 %eval_product.5 = (f32[2048,128]{1,0:T(8,128)S(1)}, bf16[40,224,256]{2,1,0:T(8,128)(2,1)S(1)}, s32[3,168]{1,0:T(4,128)S(1)}, f32[48,128]{1,0:T(8,128)S(1)}) custom-call(f32[824,128]{1,0:T(8,128)S(1)} %get-tuple-element.47.own.refs_0_.refs_7_, f32[4,2272,128]{2,1,0:T(8,128)S(1)} %get-tuple-element.48.rows, ...), custom_call_target="tpu_custom_call" | custom-call | flops 1000000 | bytes 100000 | tf_op jit(solution)/shard_map/eval_product/pallas_call | solution.py:476
  23.8 3.5 %collective-permute-start.8 = (f32[824,128]{1,0:T(8,128)S(1)}, f32[824,128]{1,0:T(8,128)S(1)}, u32[]{:S(2)}, u32[]{:S(2)}) collective-permute-start(f32[824,128]{1,0:T(8,128)S(1)} %collective-permute-done.refs_0_), channel_id=1, source_target_pairs={{6,2},{0,4},{10,6},{4,8},{14,10},{8,12},{7,3},{1,5},{11,7},{5,9},{... | collective-permute-start | bytes 1265672 | tf_op jit(solution)/shard_map/ppermute | solution.py:525
  27.3 6.1 %eval_product.6 = (f32[2048,128]{1,0:T(8,128)S(1)}, bf16[40,224,256]{2,1,0:T(8,128)(2,1)S(1)}, s32[3,168]{1,0:T(4,128)S(1)}, f32[48,128]{1,0:T(8,128)S(1)}) custom-call(f32[824,128]{1,0:T(8,128)S(1)} %get-tuple-element.47.own.refs_0_.refs_7_, f32[4,2272,128]{2,1,0:T(8,128)S(1)} %get-tuple-element.48.rows, f32[2104,128]{1,0:T(8,128)S(1)} %collective-permute-done.4.refs_0_, ...), custom_call_target="tpu_custom_call" | custom-call | flops 1000000 | bytes 100000 | tf_op jit(solution)/shard_map/eval_product/pallas_call | solution.py:476
  33.4 3.5 %collective-permute-start.10 = (f32[768,128]{1,0:T(8,128)S(1)}, f32[768,128]{1,0:T(8,128)S(1)}, u32[]{:S(2)}, u32[]{:S(2)}) collective-permute-start(f32[768,128]{1,0:T(8,128)S(1)} %collective-permute-done.3.refs_1_), channel_id=1, source_target_pairs={{6,2},{0,4},{10,6},{4,8},{14,10},{8,12},{7,3},{1,5},{11,7},{5,9},{... | collective-permute-start | bytes 1179656 | tf_op jit(solution)/shard_map/ppermute | solution.py:525
  36.9 1.3 %collective-permute-start.12 = (f32[512,128]{1,0:T(8,128)S(1)}, f32[512,128]{1,0:T(8,128)S(1)}, u32[]{:S(2)}, u32[]{:S(2)}) collective-permute-start(f32[512,128]{1,0:T(8,128)S(1)} %collective-permute-done.1), channel_id=1, source_target_pairs={{0,2},{2,0},{4,6},{6,4},{8,10},{10,8},{12,14},{14,12},{1,3},{3,1},... | collective-permute-start | bytes 786440 | tf_op jit(solution)/shard_map/ppermute | solution.py:515
  38.8 6.1 %eval_product.7 = (f32[2048,128]{1,0:T(8,128)S(1)}, bf16[40,224,256]{2,1,0:T(8,128)(2,1)S(1)}, s32[3,168]{1,0:T(4,128)S(1)}, f32[48,128]{1,0:T(8,128)S(1)}) custom-call(f32[824,128]{1,0:T(8,128)S(1)} %get-tuple-element.47.own.refs_0_.refs_7_, f32[4,2272,128]{2,1,0:T(8,128)S(1)} %get-tuple-element.48.rows, f32[824,128]{1,0:T(8,128)S(1)} %collective-permute-done.refs_0_, ...), custom_call_target="tpu_custom_call" | custom-call | flops 1000000 | bytes 100000 | tf_op jit(solution)/shard_map/eval_product/pallas_call | solution.py:476
  46.0 1.9 %eval_product.8 = (f32[2048,128]{1,0:T(8,128)S(1)}, bf16[40,224,256]{2,1,0:T(8,128)(2,1)S(1)}, s32[3,168]{1,0:T(4,128)S(1)}, f32[48,128]{1,0:T(8,128)S(1)}) custom-call(f32[824,128]{1,0:T(8,128)S(1)} %get-tuple-element.47.own.refs_0_.refs_7_, f32[4,2272,128]{2,1,0:T(8,128)S(1)} %get-tuple-element.48.rows, f32[824,128]{1,0:T(8,128)S(1)} %collective-permute-done.8.refs_0_, ...), custom_call_target="tpu_custom_call" | custom-call | flops 1000000 | bytes 100000 | tf_op jit(solution)/shard_map/eval_product/pallas_call | solution.py:476
  48.2 2.0 %eval_product.9 = (f32[768,128]{1,0:T(8,128)S(1)}, f32[768,128]{1,0:T(8,128)S(1)}, f32[512,128]{1,0:T(8,128)S(1)}, f32[2048,128]{1,0:T(8,128)S(1)}, bf16[40,224,...) custom-call(f32[824,128]{1,0:T(8,128)S(1)} %get-tuple-element.47.own.refs_0_.refs_7_, ...), custom_call_target="tpu_custom_call" | custom-call | flops 1000000 | bytes 100000 | tf_op jit(solution)/shard_map/eval_product/pallas_call | solution.py:476
  50.2 4.6 %collective-permute-start.15 = (f32[2048,128]{1,0:T(8,128)S(1)}, f32[2048,128]{1,0:T(8,128)S(1)}, u32[]{:S(2)}, u32[]{:S(2)}) collective-permute-start(f32[2048,128]{1,0:T(8,128)S(1)} %get-tuple-element.72.source), channel_id=1, source_target_pairs={{0,1},{1,0},{2,3},{3,2},{4,5},{5,4},{6,7},{7,6},{8,9},{9,8},{10,11... | collective-permute-start | bytes 3145736 | tf_op jit(solution)/shard_map/ppermute | solution.py:530
  54.8 4.8 %collective-permute-start.18 = (f32[768,128]{1,0:T(8,128)S(1)}, f32[768,128]{1,0:T(8,128)S(1)}, u32[]{:S(2)}, u32[]{:S(2)}) collective-permute-start(f32[768,128]{1,0:T(8,128)S(1)} %get-tuple-element.77.refs_1_.refs_11_), channel_id=1, source_target_pairs={{0,2},{2,0},{4,6},{6,4},{8,10},{10,8},{12,14},{14,12},{1,3},{3,1},... | collective-permute-start | bytes 1179656 | tf_op jit(solution)/shard_map/ppermute | solution.py:515
  61.0 4.2 %collective-permute-start.20 = (f32[512,128]{1,0:T(8,128)S(1)}, f32[512,128]{1,0:T(8,128)S(1)}, u32[]{:S(2)}, u32[]{:S(2)}) collective-permute-start(f32[512,128]{1,0:T(8,128)S(1)} %get-tuple-element.78.refs_2_.refs_12_), channel_id=1, source_target_pairs={{0,2},{2,0},{4,6},{6,4},{8,10},{10,8},{12,14},{14,12},{1,3},{3,1},... | collective-permute-start | bytes 786440 | tf_op jit(solution)/shard_map/ppermute | solution.py:515
  65.2 3.1 %product.5.refs_1_ = f32[2048,128]{1,0:T(8,128)S(1)} custom-call(s32[3,168]{1,0:T(4,128)S(1)} %get-tuple-element.74.work, f32[48,128]{1,0:T(8,128)S(1)} %get-tuple-element.75.facts, f32[4,2272,128]{2,1,0:T(8,128)S(1)} %get-tuple-element.48.rows, bf16[40,224,256]{2,1,0:T(8,128)(2,1)S(1)} %get-tuple-element.76.cache, ...), custom_call_target="tpu_custom_call" | custom-call | flops 1000000 | bytes 100000 | tf_op jit(solution)/shard_map/product/pallas_call | solution.py:457
  68.2 1.3 %collective-permute-done.18.refs_1_ = f32[768,128]{1,0:T(8,128)S(1)} collective-permute-done((f32[768,128]{1,0:T(8,128)S(1)}, f32[768,128]{1,0:T(8,128)S(1)}, u32[]{:S(2)}, u32[]{:S(2)}) %collective-permute-start.18) | collective-permute-done | bytes 393248 | tf_op jit(solution)/shard_map/ppermute | solution.py:515
  69.5 5.1 %collective-permute-start.24 = (f32[768,128]{1,0:T(8,128)S(1)}, f32[768,128]{1,0:T(8,128)S(1)}, u32[]{:S(2)}, u32[]{:S(2)}) collective-permute-start(f32[768,128]{1,0:T(8,128)S(1)} %collective-permute-done.18.refs_1_), channel_id=1, source_target_pairs={{6,2},{0,4},{10,6},{4,8},{14,10},{8,12},{7,3},{1,5},{11,7},{5,9},{... | collective-permute-start | bytes 1179656 | tf_op jit(solution)/shard_map/ppermute | solution.py:525
  74.6 2.5 %unsort.2 = f32[2048,128]{1,0:T(8,128)S(1)} custom-call(s32[1,2048]{1,0:T(1,128)S(1)} %get-tuple-element.71.ranks, f32[2048,128]{1,0:T(8,128)S(1)} %get-tuple-element.72.source), custom_call_target="tpu_custom_call" | custom-call | flops 1000000 | bytes 100000 | tf_op jit(solution)/shard_map/unsort/pallas_call | solution.py:502
  77.1 3.0 %product.6.refs_3_ = f32[2048,128]{1,0:T(8,128)S(1)} custom-call(s32[3,168]{1,0:T(4,128)S(1)} %get-tuple-element.67.work, f32[48,128]{1,0:T(8,128)S(1)} %get-tuple-element.68.facts, f32[4,2272,128]{2,1,0:T(8,128)S(1)} %get-tuple-element.48.rows, bf16[40,224,256]{2,1,0:T(8,128)(2,1)S(1)} %get-tuple-element.69.cache, ...), custom_call_target="tpu_custom_call" | custom-call | flops 1000000 | bytes 100000 | tf_op jit(solution)/shard_map/product/pallas_call | solution.py:457
  80.1 3.2 %collective-permute-start.22 = (f32[768,128]{1,0:T(8,128)S(1)}, f32[768,128]{1,0:T(8,128)S(1)}, u32[]{:S(2)}, u32[]{:S(2)}) collective-permute-start(f32[768,128]{1,0:T(8,128)S(1)} %collective-permute-done.14.refs_0_), channel_id=1, source_target_pairs={{6,2},{0,4},{10,6},{4,8},{14,10},{8,12},{7,3},{1,5},{11,7},{5,9},{... | collective-permute-start | bytes 1179656 | tf_op jit(solution)/shard_map/ppermute | solution.py:525
  83.3 1.8 %collective-permute-start.26 = (f32[512,128]{1,0:T(8,128)S(1)}, f32[512,128]{1,0:T(8,128)S(1)}, u32[]{:S(2)}, u32[]{:S(2)}) collective-permute-start(f32[512,128]{1,0:T(8,128)S(1)} %collective-permute-done.16), channel_id=1, source_target_pairs={{0,2},{2,0},{4,6},{6,4},{8,10},{10,8},{12,14},{14,12},{1,3},{3,1},... | collective-permute-start | bytes 786440 | tf_op jit(solution)/shard_map/ppermute | solution.py:515
  85.6 2.9 %product.7.refs_3_ = f32[2048,128]{1,0:T(8,128)S(1)} custom-call(s32[3,168]{1,0:T(4,128)S(1)} %get-tuple-element.80.work, f32[48,128]{1,0:T(8,128)S(1)} %get-tuple-element.81.facts, f32[4,2272,128]{2,1,0:T(8,128)S(1)} %get-tuple-element.48.rows, bf16[40,224,256]{2,1,0:T(8,128)(2,1)S(1)} %get-tuple-element.82.cache, ...), custom_call_target="tpu_custom_call" | custom-call | flops 1000000 | bytes 100000 | tf_op jit(solution)/shard_map/product/pallas_call | solution.py:457
  88.5 1.9 %collective-permute-done.22.refs_0_ = f32[768,128]{1,0:T(8,128)S(1)} collective-permute-done((f32[768,128]{1,0:T(8,128)S(1)}, f32[768,128]{1,0:T(8,128)S(1)}, u32[]{:S(2)}, u32[]{:S(2)}) %collective-permute-start.22) | collective-permute-done | bytes 393248 | tf_op jit(solution)/shard_map/ppermute | solution.py:525
  93.5 1.3 %product.9 = (f32[2048,128]{1,0:T(8,128)S(1)}, f32[8,128]{1,0:T(8,128)S(1)}) custom-call(s32[3,328]{1,0:T(4,128)S(1)} %get-tuple-element.63.work, f32[96,128]{1,0:T(8,128)S(1)} %get-tuple-element.64.facts, f32[4,2272,128]{2,1,0:T(8,128)S(1)} %get-tuple-element.48.rows, bf16[40,224,256]{2,1,0:T(8,128)(2,1)S(1)} %get-tuple-element.65.cache, ...), custom_call_target="tpu_custom_call" | custom-call | flops 1000000 | bytes 100000 | tf_op jit(solution)/shard_map/product/pallas_call | solution.py:457
  94.8 2.4 %collective-permute-start.28 = (f32[8,128]{1,0:T(8,128)S(1)}, f32[8,128]{1,0:T(8,128)S(1)}, u32[]{:S(2)}, u32[]{:S(2)}) collective-permute-start(f32[8,128]{1,0:T(8,128)S(1)} %get-tuple-element.89), channel_id=1, source_target_pairs={{0,1},{1,0},{2,3},{3,2},{4,5},{5,4},{6,7},{7,6},{8,9},{9,8},{10,11... | collective-permute-start | bytes 12296 | tf_op jit(solution)/shard_map/ppermute | solution.py:530
  98.0 3.2 %collective-permute-start.29 = (f32[8,128]{1,0:T(8,128)S(1)}, f32[8,128]{1,0:T(8,128)S(1)}, u32[]{:S(2)}, u32[]{:S(2)}) collective-permute-start(f32[8,128]{1,0:T(8,128)S(1)} %add.36), channel_id=1, source_target_pairs={{0,2},{2,0},{4,6},{6,4},{8,10},{10,8},{12,14},{14,12},{1,3},{3,1},... | collective-permute-start | bytes 12296 | tf_op jit(solution)/shard_map/ppermute | solution.py:539
  101.2 1.6 %collective-permute-done.29 = f32[8,128]{1,0:T(8,128)S(1)} collective-permute-done((f32[8,128]{1,0:T(8,128)S(1)}, f32[8,128]{1,0:T(8,128)S(1)}, u32[]{:S(2)}, u32[]{:S(2)}) %collective-permute-start.29) | collective-permute-done | bytes 4128 | tf_op jit(solution)/shard_map/ppermute | solution.py:539
  102.8 2.4 %collective-permute-start.30 = (f32[8,128]{1,0:T(8,128)S(1)}, f32[8,128]{1,0:T(8,128)S(1)}, u32[]{:S(2)}, u32[]{:S(2)}) collective-permute-start(f32[8,128]{1,0:T(8,128)S(1)} %add.37), channel_id=1, source_target_pairs={{0,4},{2,6},{4,0},{6,2},{8,12},{10,14},{12,8},{14,10},{1,5},{3,7},... | collective-permute-start | bytes 12296 | tf_op jit(solution)/shard_map/ppermute | solution.py:539
  105.2 2.5 %unsort.3 = f32[2048,128]{1,0:T(8,128)S(1)} custom-call(s32[1,2048]{1,0:T(1,128)S(1)} %get-tuple-element.71.ranks, f32[2048,128]{1,0:T(8,128)S(1)} %get-tuple-element.90.source), custom_call_target="tpu_custom_call" | custom-call | flops 1000000 | bytes 100000 | tf_op jit(solution)/shard_map/unsort/pallas_call | solution.py:502
  107.7 3.1 %collective-permute-start.31 = (f32[8,128]{1,0:T(8,128)S(1)}, f32[8,128]{1,0:T(8,128)S(1)}, u32[]{:S(2)}, u32[]{:S(2)}) collective-permute-start(f32[8,128]{1,0:T(8,128)S(1)} %add.38), channel_id=1, source_target_pairs={{0,8},{2,10},{4,12},{6,14},{8,0},{10,2},{12,4},{14,6},{1,9},{3,11}... | collective-permute-start | bytes 12296 | tf_op jit(solution)/shard_map/ppermute | solution.py:539
  110.8 1.6 %collective-permute-done.31 = f32[8,128]{1,0:T(8,128)S(1)} collective-permute-done((f32[8,128]{1,0:T(8,128)S(1)}, f32[8,128]{1,0:T(8,128)S(1)}, u32[]{:S(2)}, u32[]{:S(2)}) %collective-permute-start.31) | collective-permute-done | bytes 4128 | tf_op jit(solution)/shard_map/ppermute | solution.py:539
  112.4 1.8 %multiply_subtract_fusion = (f32[2048,128]{1,0:T(8,128)}, f32[2048,128]{1,0:T(8,128)}) fusion(f32[2048,128]{1,0:T(8,128)S(1)} %unsort.2, f32[2048,128]{1,0:T(8,128)S(1)} %unsort.3, f32[2048,128]{1,0:T(8,128)S(1)} %copy-done, f32[128]{0:T(128)S(1)} %bitcast.7, f32[128]{0:T(128)S(1)} %get-tuple-element.92, f32[128]{0:T(128)S(1)} %bitcast.6), kind=kLoop, calls=%fused_computation | loop fusion | flops 3407872 | bytes 5244416 | tf_op jit(solution)/shard_map/sub | solution.py:607
  (54 shorter events, 9.6 us)
Async XLA Ops:
  9.0 18.3 %collective-permute-start.4 = (f32[2104,128]{1,0:T(8,128)S(1)}, f32[2104,128]{1,0:T(8,128)S(1)}, u32[]{:S(2)}, u32[]{:S(2)}) collective-permute-start(f32[2104,128]{1,0:T(8,128)S(1)} %get-tuple-element.53), channel_id=1, source_target_pairs={{0,1},{1,0},{2,3},{3,2},{4,5},{5,4},{6,7},{7,6},{8,9},{9,8},{10,11... | collective-permute-start | bytes 3231752 | tf_op jit(solution)/shard_map/ppermute | solution.py:530
  9.5 14.3 %collective-permute-start = (f32[824,128]{1,0:T(8,128)S(1)}, f32[824,128]{1,0:T(8,128)S(1)}, u32[]{:S(2)}, u32[]{:S(2)}) collective-permute-start(f32[824,128]{1,0:T(8,128)S(1)} %get-tuple-element.47.own.refs_0_.refs_7_), channel_id=1, source_target_pairs={{0,2},{2,0},{4,6},{6,4},{8,10},{10,8},{12,14},{14,12},{1,3},{3,1},... | collective-permute-start | bytes 1265672 | tf_op jit(solution)/shard_map/ppermute | solution.py:515
  12.1 21.3 %collective-permute-start.3 = (f32[768,128]{1,0:T(8,128)S(1)}, f32[768,128]{1,0:T(8,128)S(1)}, u32[]{:S(2)}, u32[]{:S(2)}) collective-permute-start(f32[768,128]{1,0:T(8,128)S(1)} %get-tuple-element.49.refs_1_.refs_8_), channel_id=1, source_target_pairs={{0,2},{2,0},{4,6},{6,4},{8,10},{10,8},{12,14},{14,12},{1,3},{3,1},... | collective-permute-start | bytes 1179656 | tf_op jit(solution)/shard_map/ppermute | solution.py:515
  12.2 11.6 %collective-permute-start.1 = (f32[512,128]{1,0:T(8,128)S(1)}, f32[512,128]{1,0:T(8,128)S(1)}, u32[]{:S(2)}, u32[]{:S(2)}) collective-permute-start(f32[512,128]{1,0:T(8,128)S(1)} %get-tuple-element.50.refs_2_.refs_9_), channel_id=1, source_target_pairs={{4,0},{8,4},{2,6},{12,8},{6,10},{10,14},{5,1},{9,5},{3,7},{13,9},{... | collective-permute-start | bytes 786440 | tf_op jit(solution)/shard_map/ppermute | solution.py:525
  13.5 23.4 %collective-permute-start.6 = (f32[512,128]{1,0:T(8,128)S(1)}, f32[512,128]{1,0:T(8,128)S(1)}, u32[]{:S(2)}, u32[]{:S(2)}) collective-permute-start(f32[512,128]{1,0:T(8,128)S(1)} %get-tuple-element.50.refs_2_.refs_9_), channel_id=1, source_target_pairs={{0,2},{2,0},{4,6},{6,4},{8,10},{10,8},{12,14},{14,12},{1,3},{3,1},... | collective-permute-start | bytes 786440 | tf_op jit(solution)/shard_map/ppermute | solution.py:515
  23.8 21.0 %collective-permute-start.8 = (f32[824,128]{1,0:T(8,128)S(1)}, f32[824,128]{1,0:T(8,128)S(1)}, u32[]{:S(2)}, u32[]{:S(2)}) collective-permute-start(f32[824,128]{1,0:T(8,128)S(1)} %collective-permute-done.refs_0_), channel_id=1, source_target_pairs={{6,2},{0,4},{10,6},{4,8},{14,10},{8,12},{7,3},{1,5},{11,7},{5,9},{... | collective-permute-start | bytes 1265672 | tf_op jit(solution)/shard_map/ppermute | solution.py:525
  33.4 11.5 %collective-permute-start.10 = (f32[768,128]{1,0:T(8,128)S(1)}, f32[768,128]{1,0:T(8,128)S(1)}, u32[]{:S(2)}, u32[]{:S(2)}) collective-permute-start(f32[768,128]{1,0:T(8,128)S(1)} %collective-permute-done.3.refs_1_), channel_id=1, source_target_pairs={{6,2},{0,4},{10,6},{4,8},{14,10},{8,12},{7,3},{1,5},{11,7},{5,9},{... | collective-permute-start | bytes 1179656 | tf_op jit(solution)/shard_map/ppermute | solution.py:525
  36.9 8.5 %collective-permute-start.12 = (f32[512,128]{1,0:T(8,128)S(1)}, f32[512,128]{1,0:T(8,128)S(1)}, u32[]{:S(2)}, u32[]{:S(2)}) collective-permute-start(f32[512,128]{1,0:T(8,128)S(1)} %collective-permute-done.1), channel_id=1, source_target_pairs={{0,2},{2,0},{4,6},{6,4},{8,10},{10,8},{12,14},{14,12},{1,3},{3,1},... | collective-permute-start | bytes 786440 | tf_op jit(solution)/shard_map/ppermute | solution.py:515
  38.2 7.3 %collective-permute-start.7 = (f32[512,128]{1,0:T(8,128)S(1)}, f32[512,128]{1,0:T(8,128)S(1)}, u32[]{:S(2)}, u32[]{:S(2)}) collective-permute-start(f32[512,128]{1,0:T(8,128)S(1)} %collective-permute-done.6.refs_2_), channel_id=1, source_target_pairs={{0,1},{1,0},{2,3},{3,2},{4,5},{5,4},{6,7},{7,6},{8,9},{9,8},{10,11... | collective-permute-start | bytes 786440 | tf_op jit(solution)/shard_map/ppermute | solution.py:530
  38.2 9.6 %collective-permute-start.2 = (f32[824,128]{1,0:T(8,128)S(1)}, f32[824,128]{1,0:T(8,128)S(1)}, u32[]{:S(2)}, u32[]{:S(2)}) collective-permute-start(f32[824,128]{1,0:T(8,128)S(1)} %collective-permute-done.refs_0_), channel_id=1, source_target_pairs={{0,1},{1,0},{2,3},{3,2},{4,5},{5,4},{6,7},{7,6},{8,9},{9,8},{10,11... | collective-permute-start | bytes 1265672 | tf_op jit(solution)/shard_map/ppermute | solution.py:530
  44.9 3.1 %collective-permute-start.9 = (f32[824,128]{1,0:T(8,128)S(1)}, f32[824,128]{1,0:T(8,128)S(1)}, u32[]{:S(2)}, u32[]{:S(2)}) collective-permute-start(f32[824,128]{1,0:T(8,128)S(1)} %collective-permute-done.8.refs_0_), channel_id=1, source_target_pairs={{0,1},{1,0},{2,3},{3,2},{4,5},{5,4},{6,7},{7,6},{8,9},{9,8},{10,11... | collective-permute-start | bytes 1265672 | tf_op jit(solution)/shard_map/ppermute | solution.py:530
  44.9 3.0 %collective-permute-start.5 = (f32[768,128]{1,0:T(8,128)S(1)}, f32[768,128]{1,0:T(8,128)S(1)}, u32[]{:S(2)}, u32[]{:S(2)}) collective-permute-start(f32[768,128]{1,0:T(8,128)S(1)} %collective-permute-done.3.refs_1_), channel_id=1, source_target_pairs={{0,1},{1,0},{2,3},{3,2},{4,5},{5,4},{6,7},{7,6},{8,9},{9,8},{10,11... | collective-permute-start | bytes 1179656 | tf_op jit(solution)/shard_map/ppermute | solution.py:530
  45.4 2.7 %collective-permute-start.11 = (f32[768,128]{1,0:T(8,128)S(1)}, f32[768,128]{1,0:T(8,128)S(1)}, u32[]{:S(2)}, u32[]{:S(2)}) collective-permute-start(f32[768,128]{1,0:T(8,128)S(1)} %collective-permute-done.10.refs_1_), channel_id=1, source_target_pairs={{0,1},{1,0},{2,3},{3,2},{4,5},{5,4},{6,7},{7,6},{8,9},{9,8},{10,11... | collective-permute-start | bytes 1179656 | tf_op jit(solution)/shard_map/ppermute | solution.py:530
  45.5 2.7 %collective-permute-start.13 = (f32[512,128]{1,0:T(8,128)S(1)}, f32[512,128]{1,0:T(8,128)S(1)}, u32[]{:S(2)}, u32[]{:S(2)}) collective-permute-start(f32[512,128]{1,0:T(8,128)S(1)} %collective-permute-done.12.refs_2_), channel_id=1, source_target_pairs={{0,1},{1,0},{2,3},{3,2},{4,5},{5,4},{6,7},{7,6},{8,9},{9,8},{10,11... | collective-permute-start | bytes 786440 | tf_op jit(solution)/shard_map/ppermute | solution.py:530
  50.2 24.4 %collective-permute-start.15 = (f32[2048,128]{1,0:T(8,128)S(1)}, f32[2048,128]{1,0:T(8,128)S(1)}, u32[]{:S(2)}, u32[]{:S(2)}) collective-permute-start(f32[2048,128]{1,0:T(8,128)S(1)} %get-tuple-element.72.source), channel_id=1, source_target_pairs={{0,1},{1,0},{2,3},{3,2},{4,5},{5,4},{6,7},{7,6},{8,9},{9,8},{10,11... | collective-permute-start | bytes 3145736 | tf_op jit(solution)/shard_map/ppermute | solution.py:530
  54.8 14.8 %collective-permute-start.18 = (f32[768,128]{1,0:T(8,128)S(1)}, f32[768,128]{1,0:T(8,128)S(1)}, u32[]{:S(2)}, u32[]{:S(2)}) collective-permute-start(f32[768,128]{1,0:T(8,128)S(1)} %get-tuple-element.77.refs_1_.refs_11_), channel_id=1, source_target_pairs={{0,2},{2,0},{4,6},{6,4},{8,10},{10,8},{12,14},{14,12},{1,3},{3,1},... | collective-permute-start | bytes 1179656 | tf_op jit(solution)/shard_map/ppermute | solution.py:515
  59.6 20.5 %collective-permute-start.14 = (f32[768,128]{1,0:T(8,128)S(1)}, f32[768,128]{1,0:T(8,128)S(1)}, u32[]{:S(2)}, u32[]{:S(2)}) collective-permute-start(f32[768,128]{1,0:T(8,128)S(1)} %get-tuple-element.66.refs_0_.refs_10_), channel_id=1, source_target_pairs={{0,2},{2,0},{4,6},{6,4},{8,10},{10,8},{12,14},{14,12},{1,3},{3,1},... | collective-permute-start | bytes 1179656 | tf_op jit(solution)/shard_map/ppermute | solution.py:515
  59.7 20.4 %collective-permute-start.16 = (f32[512,128]{1,0:T(8,128)S(1)}, f32[512,128]{1,0:T(8,128)S(1)}, u32[]{:S(2)}, u32[]{:S(2)}) collective-permute-start(f32[512,128]{1,0:T(8,128)S(1)} %get-tuple-element.78.refs_2_.refs_12_), channel_id=1, source_target_pairs={{4,0},{8,4},{2,6},{12,8},{6,10},{10,14},{5,1},{9,5},{3,7},{13,9},{... | collective-permute-start | bytes 786440 | tf_op jit(solution)/shard_map/ppermute | solution.py:525
  61.0 22.4 %collective-permute-start.20 = (f32[512,128]{1,0:T(8,128)S(1)}, f32[512,128]{1,0:T(8,128)S(1)}, u32[]{:S(2)}, u32[]{:S(2)}) collective-permute-start(f32[512,128]{1,0:T(8,128)S(1)} %get-tuple-element.78.refs_2_.refs_12_), channel_id=1, source_target_pairs={{0,2},{2,0},{4,6},{6,4},{8,10},{10,8},{12,14},{14,12},{1,3},{3,1},... | collective-permute-start | bytes 786440 | tf_op jit(solution)/shard_map/ppermute | solution.py:515
  69.5 16.1 %collective-permute-start.24 = (f32[768,128]{1,0:T(8,128)S(1)}, f32[768,128]{1,0:T(8,128)S(1)}, u32[]{:S(2)}, u32[]{:S(2)}) collective-permute-start(f32[768,128]{1,0:T(8,128)S(1)} %collective-permute-done.18.refs_1_), channel_id=1, source_target_pairs={{6,2},{0,4},{10,6},{4,8},{14,10},{8,12},{7,3},{1,5},{11,7},{5,9},{... | collective-permute-start | bytes 1179656 | tf_op jit(solution)/shard_map/ppermute | solution.py:525
  80.1 10.3 %collective-permute-start.22 = (f32[768,128]{1,0:T(8,128)S(1)}, f32[768,128]{1,0:T(8,128)S(1)}, u32[]{:S(2)}, u32[]{:S(2)}) collective-permute-start(f32[768,128]{1,0:T(8,128)S(1)} %collective-permute-done.14.refs_0_), channel_id=1, source_target_pairs={{6,2},{0,4},{10,6},{4,8},{14,10},{8,12},{7,3},{1,5},{11,7},{5,9},{... | collective-permute-start | bytes 1179656 | tf_op jit(solution)/shard_map/ppermute | solution.py:525
  83.3 8.1 %collective-permute-start.26 = (f32[512,128]{1,0:T(8,128)S(1)}, f32[512,128]{1,0:T(8,128)S(1)}, u32[]{:S(2)}, u32[]{:S(2)}) collective-permute-start(f32[512,128]{1,0:T(8,128)S(1)} %collective-permute-done.16), channel_id=1, source_target_pairs={{0,2},{2,0},{4,6},{6,4},{8,10},{10,8},{12,14},{14,12},{1,3},{3,1},... | collective-permute-start | bytes 786440 | tf_op jit(solution)/shard_map/ppermute | solution.py:515
  85.1 6.3 %collective-permute-start.21 = (f32[512,128]{1,0:T(8,128)S(1)}, f32[512,128]{1,0:T(8,128)S(1)}, u32[]{:S(2)}, u32[]{:S(2)}) collective-permute-start(f32[512,128]{1,0:T(8,128)S(1)} %collective-permute-done.20.refs_2_), channel_id=1, source_target_pairs={{0,1},{1,0},{2,3},{3,2},{4,5},{5,4},{6,7},{7,6},{8,9},{9,8},{10,11... | collective-permute-start | bytes 786440 | tf_op jit(solution)/shard_map/ppermute | solution.py:530
  85.1 7.7 %collective-permute-start.19 = (f32[768,128]{1,0:T(8,128)S(1)}, f32[768,128]{1,0:T(8,128)S(1)}, u32[]{:S(2)}, u32[]{:S(2)}) collective-permute-start(f32[768,128]{1,0:T(8,128)S(1)} %collective-permute-done.18.refs_1_), channel_id=1, source_target_pairs={{0,1},{1,0},{2,3},{3,2},{4,5},{5,4},{6,7},{7,6},{8,9},{9,8},{10,11... | collective-permute-start | bytes 1179656 | tf_op jit(solution)/shard_map/ppermute | solution.py:530
  85.6 7.2 %collective-permute-start.25 = (f32[768,128]{1,0:T(8,128)S(1)}, f32[768,128]{1,0:T(8,128)S(1)}, u32[]{:S(2)}, u32[]{:S(2)}) collective-permute-start(f32[768,128]{1,0:T(8,128)S(1)} %collective-permute-done.24.refs_1_), channel_id=1, source_target_pairs={{0,1},{1,0},{2,3},{3,2},{4,5},{5,4},{6,7},{7,6},{8,9},{9,8},{10,11... | collective-permute-start | bytes 1179656 | tf_op jit(solution)/shard_map/ppermute | solution.py:530
  90.4 2.4 %collective-permute-start.17 = (f32[768,128]{1,0:T(8,128)S(1)}, f32[768,128]{1,0:T(8,128)S(1)}, u32[]{:S(2)}, u32[]{:S(2)}) collective-permute-start(f32[768,128]{1,0:T(8,128)S(1)} %collective-permute-done.14.refs_0_), channel_id=1, source_target_pairs={{0,1},{1,0},{2,3},{3,2},{4,5},{5,4},{6,7},{7,6},{8,9},{9,8},{10,11... | collective-permute-start | bytes 1179656 | tf_op jit(solution)/shard_map/ppermute | solution.py:530
  91.4 2.1 %collective-permute-start.23 = (f32[768,128]{1,0:T(8,128)S(1)}, f32[768,128]{1,0:T(8,128)S(1)}, u32[]{:S(2)}, u32[]{:S(2)}) collective-permute-start(f32[768,128]{1,0:T(8,128)S(1)} %collective-permute-done.22.refs_0_), channel_id=1, source_target_pairs={{0,1},{1,0},{2,3},{3,2},{4,5},{5,4},{6,7},{7,6},{8,9},{9,8},{10,11... | collective-permute-start | bytes 1179656 | tf_op jit(solution)/shard_map/ppermute | solution.py:530
  91.4 2.1 %collective-permute-start.27 = (f32[512,128]{1,0:T(8,128)S(1)}, f32[512,128]{1,0:T(8,128)S(1)}, u32[]{:S(2)}, u32[]{:S(2)}) collective-permute-start(f32[512,128]{1,0:T(8,128)S(1)} %collective-permute-done.26.refs_2_), channel_id=1, source_target_pairs={{0,1},{1,0},{2,3},{3,2},{4,5},{5,4},{6,7},{7,6},{8,9},{9,8},{10,11... | collective-permute-start | bytes 786440 | tf_op jit(solution)/shard_map/ppermute | solution.py:530
  94.8 3.3 %collective-permute-start.28 = (f32[8,128]{1,0:T(8,128)S(1)}, f32[8,128]{1,0:T(8,128)S(1)}, u32[]{:S(2)}, u32[]{:S(2)}) collective-permute-start(f32[8,128]{1,0:T(8,128)S(1)} %get-tuple-element.89), channel_id=1, source_target_pairs={{0,1},{1,0},{2,3},{3,2},{4,5},{5,4},{6,7},{7,6},{8,9},{9,8},{10,11... | collective-permute-start | bytes 12296 | tf_op jit(solution)/shard_map/ppermute | solution.py:530
  98.0 4.8 %collective-permute-start.29 = (f32[8,128]{1,0:T(8,128)S(1)}, f32[8,128]{1,0:T(8,128)S(1)}, u32[]{:S(2)}, u32[]{:S(2)}) collective-permute-start(f32[8,128]{1,0:T(8,128)S(1)} %add.36), channel_id=1, source_target_pairs={{0,2},{2,0},{4,6},{6,4},{8,10},{10,8},{12,14},{14,12},{1,3},{3,1},... | collective-permute-start | bytes 12296 | tf_op jit(solution)/shard_map/ppermute | solution.py:539
  102.8 4.9 %collective-permute-start.30 = (f32[8,128]{1,0:T(8,128)S(1)}, f32[8,128]{1,0:T(8,128)S(1)}, u32[]{:S(2)}, u32[]{:S(2)}) collective-permute-start(f32[8,128]{1,0:T(8,128)S(1)} %add.37), channel_id=1, source_target_pairs={{0,4},{2,6},{4,0},{6,2},{8,12},{10,14},{12,8},{14,10},{1,5},{3,7},... | collective-permute-start | bytes 12296 | tf_op jit(solution)/shard_map/ppermute | solution.py:539
  107.7 4.6 %collective-permute-start.31 = (f32[8,128]{1,0:T(8,128)S(1)}, f32[8,128]{1,0:T(8,128)S(1)}, u32[]{:S(2)}, u32[]{:S(2)}) collective-permute-start(f32[8,128]{1,0:T(8,128)S(1)} %add.38), channel_id=1, source_target_pairs={{0,8},{2,10},{4,12},{6,14},{8,0},{10,2},{12,4},{14,6},{1,9},{3,11}... | collective-permute-start | bytes 12296 | tf_op jit(solution)/shard_map/ppermute | solution.py:539
  (1 other events, 18.9 us)

commit v6 on v5

--- a/solution.py
+++ b/solution.py
@@ -572,8 +572,7 @@
     far.append(pair_swap(after(turned, near[2], near[1])))
     near_mates = [core_swap(c) for c in near]
     image, near_eval = eval_product(points, given[0], rows, (near,), image)
-    far = [after(c, image[0]) for c in far]
-    far_mates = [core_swap(c) for c in far]
+    far_mates = [core_swap(far[0]), *(core_swap(after(c, image[0])) for c in far[1:])]
     image, far_eval = eval_product(points, given[0], rows, (far,), image)
     (*once, whole), rest_eval = eval_product(points, given[0], rows, (near_mates, far_mates), image, True)
 

time: 115 us -> 114 us (level)
  transfers between devices with their start and end apart: 32 -> 32, of which waited for: 9 -> 8; matrix products, arithmetic and copies ran while one was open for 0% -> 0% of each run, Pallas kernels for 31% -> 31%
where the time goes in v6:
time: 114 us
  starting transfers between devices  56.4 us (49%)
  Pallas kernels  46.6 us (41%)
  waiting for transfers between devices  8.43 us (7%)
  other arithmetic  1.85 us (2%)
    pallas_call x5, Pallas kernels, eval_product(): pl.pallas_call(functools.partial(both_kernel, points, halves, counts), ou...  22.2 us
    ppermute x8, starting transfers between devices, pair_swap(): return lax.ppermute(block, 'tm', [(i, i ^ 1) for i in range(count)])  19.8 us
    ppermute x6, starting transfers between devices, pair_shift(): return lax.ppermute(block, 'tm', route)  17.8 us
    pallas_call x5, Pallas kernels, product(): pl.pallas_call(functools.partial(product_kernel, points, len(values), hea...  11.2 us
    ppermute x15, starting transfers between devices, core_swap(): return lax.ppermute(block, 'tile', [(i, i ^ 1) for i in range(count)])  10.1 us
    ppermute x3, starting transfers between devices, stride_sum(): lax.ppermute(value, 'tm', [(i, i ^ step) for i in range(count)])  8.65 us
    pallas_call x1, Pallas kernels, sort_points(): pl.pallas_call(functools.partial(sort_kernel, points), out_shape=tuple((j...  8.37 us
    pallas_call x2, Pallas kernels, unsort(): pl.pallas_call(functools.partial(unsort_kernel, points), out_shape=jax.Sh...  4.94 us
  transfers between devices with their start and end apart: 32, of which 8 were waited for; matrix products, arithmetic and copies ran while one was open for 0% of the time, Pallas kernels for 31%

profile of v6, /device:TPU:0, one launch (start us, length us, event | category | flops | bytes accessed | tf_op | source)
XLA Modules:
  0.0 114.2 jit_solution(4133336007929070787)
XLA Ops:
  0.6 8.4 %sort_points.1 = (f32[824,128]{1,0:T(8,128)S(1)}, f32[768,128]{1,0:T(8,128)S(1)}, f32[512,128]{1,0:T(8,128)S(1)}, f32[2104,128]{1,0:T(8,128)S(1)}, f32[4,2272,128]{2,1,0:T(8,128)S(1)}, /*index=5*/s32[1,2048]{1,0:T(1,128)S(1)}) custom-call(f32[3,2048]{1,0:T(4,128)} %coords_hbm.1, f32[1,2048]{1,0:T(1,128)} %bitcast.5, f32[2048,128]{1,0:T(8,128)} %values_hbm.1), custom_call_target="tpu_custom_call" | custom-call | tf_op jit(solution)/shard_map/sort_points/pallas_call | solution.py:163
  9.5 2.6 %collective-permute-start = (f32[824,128]{1,0:T(8,128)S(1)}, f32[824,128]{1,0:T(8,128)S(1)}, u32[]{:S(2)}, u32[]{:S(2)}) collective-permute-start(f32[824,128]{1,0:T(8,128)S(1)} %get-tuple-element.46.own.refs_0_.refs_7_), channel_id=1, source_target_pairs={{0,2},{2,0},{4,6},{6,4},{8,10},{10,8},{12,14},{14,12},{1,3},{3,1},... | collective-permute-start | bytes 1265672 | tf_op jit(solution)/shard_map/ppermute | solution.py:515
  12.2 1.3 %collective-permute-start.1 = (f32[512,128]{1,0:T(8,128)S(1)}, f32[512,128]{1,0:T(8,128)S(1)}, u32[]{:S(2)}, u32[]{:S(2)}) collective-permute-start(f32[512,128]{1,0:T(8,128)S(1)} %get-tuple-element.49.refs_2_.refs_9_), channel_id=1, source_target_pairs={{4,0},{8,4},{2,6},{12,8},{6,10},{10,14},{5,1},{9,5},{3,7},{13,9},{... | collective-permute-start | bytes 786440 | tf_op jit(solution)/shard_map/ppermute | solution.py:525
  13.5 4.2 %collective-permute-start.6 = (f32[512,128]{1,0:T(8,128)S(1)}, f32[512,128]{1,0:T(8,128)S(1)}, u32[]{:S(2)}, u32[]{:S(2)}) collective-permute-start(f32[512,128]{1,0:T(8,128)S(1)} %get-tuple-element.49.refs_2_.refs_9_), channel_id=1, source_target_pairs={{0,2},{2,0},{4,6},{6,4},{8,10},{10,8},{12,14},{14,12},{1,3},{3,1},... | collective-permute-start | bytes 786440 | tf_op jit(solution)/shard_map/ppermute | solution.py:515
  17.7 6.1 %eval_product.5 = (f32[2048,128]{1,0:T(8,128)S(1)}, bf16[40,224,256]{2,1,0:T(8,128)(2,1)S(1)}, s32[3,168]{1,0:T(4,128)S(1)}, f32[48,128]{1,0:T(8,128)S(1)}) custom-call(f32[824,128]{1,0:T(8,128)S(1)} %get-tuple-element.46.own.refs_0_.refs_7_, f32[4,2272,128]{2,1,0:T(8,128)S(1)} %get-tuple-element.47.rows, ...), custom_call_target="tpu_custom_call" | custom-call | flops 1000000 | bytes 100000 | tf_op jit(solution)/shard_map/eval_product/pallas_call | solution.py:476
  23.8 3.5 %collective-permute-start.8 = (f32[824,128]{1,0:T(8,128)S(1)}, f32[824,128]{1,0:T(8,128)S(1)}, u32[]{:S(2)}, u32[]{:S(2)}) collective-permute-start(f32[824,128]{1,0:T(8,128)S(1)} %collective-permute-done.refs_0_), channel_id=1, source_target_pairs={{6,2},{0,4},{10,6},{4,8},{14,10},{8,12},{7,3},{1,5},{11,7},{5,9},{... | collective-permute-start | bytes 1265672 | tf_op jit(solution)/shard_map/ppermute | solution.py:525
  27.3 6.1 %eval_product.6 = (f32[2048,128]{1,0:T(8,128)S(1)}, bf16[40,224,256]{2,1,0:T(8,128)(2,1)S(1)}, s32[3,168]{1,0:T(4,128)S(1)}, f32[48,128]{1,0:T(8,128)S(1)}) custom-call(f32[824,128]{1,0:T(8,128)S(1)} %get-tuple-element.46.own.refs_0_.refs_7_, f32[4,2272,128]{2,1,0:T(8,128)S(1)} %get-tuple-element.47.rows, f32[2104,128]{1,0:T(8,128)S(1)} %collective-permute-done.4.refs_0_, ...), custom_call_target="tpu_custom_call" | custom-call | flops 1000000 | bytes 100000 | tf_op jit(solution)/shard_map/eval_product/pallas_call | solution.py:476
  33.4 3.5 %collective-permute-start.10 = (f32[768,128]{1,0:T(8,128)S(1)}, f32[768,128]{1,0:T(8,128)S(1)}, u32[]{:S(2)}, u32[]{:S(2)}) collective-permute-start(f32[768,128]{1,0:T(8,128)S(1)} %collective-permute-done.3.refs_1_), channel_id=1, source_target_pairs={{6,2},{0,4},{10,6},{4,8},{14,10},{8,12},{7,3},{1,5},{11,7},{5,9},{... | collective-permute-start | bytes 1179656 | tf_op jit(solution)/shard_map/ppermute | solution.py:525
  36.9 1.3 %collective-permute-start.12 = (f32[512,128]{1,0:T(8,128)S(1)}, f32[512,128]{1,0:T(8,128)S(1)}, u32[]{:S(2)}, u32[]{:S(2)}) collective-permute-start(f32[512,128]{1,0:T(8,128)S(1)} %collective-permute-done.1), channel_id=1, source_target_pairs={{0,2},{2,0},{4,6},{6,4},{8,10},{10,8},{12,14},{14,12},{1,3},{3,1},... | collective-permute-start | bytes 786440 | tf_op jit(solution)/shard_map/ppermute | solution.py:515
  38.8 6.1 %eval_product.7 = (f32[2048,128]{1,0:T(8,128)S(1)}, bf16[40,224,256]{2,1,0:T(8,128)(2,1)S(1)}, s32[3,168]{1,0:T(4,128)S(1)}, f32[48,128]{1,0:T(8,128)S(1)}) custom-call(f32[824,128]{1,0:T(8,128)S(1)} %get-tuple-element.46.own.refs_0_.refs_7_, f32[4,2272,128]{2,1,0:T(8,128)S(1)} %get-tuple-element.47.rows, f32[824,128]{1,0:T(8,128)S(1)} %collective-permute-done.refs_0_, ...), custom_call_target="tpu_custom_call" | custom-call | flops 1000000 | bytes 100000 | tf_op jit(solution)/shard_map/eval_product/pallas_call | solution.py:476
  46.0 1.9 %eval_product.8 = (f32[2048,128]{1,0:T(8,128)S(1)}, bf16[40,224,256]{2,1,0:T(8,128)(2,1)S(1)}, s32[3,168]{1,0:T(4,128)S(1)}, f32[48,128]{1,0:T(8,128)S(1)}) custom-call(f32[824,128]{1,0:T(8,128)S(1)} %get-tuple-element.46.own.refs_0_.refs_7_, f32[4,2272,128]{2,1,0:T(8,128)S(1)} %get-tuple-element.47.rows, f32[824,128]{1,0:T(8,128)S(1)} %collective-permute-done.8.refs_0_, ...), custom_call_target="tpu_custom_call" | custom-call | flops 1000000 | bytes 100000 | tf_op jit(solution)/shard_map/eval_product/pallas_call | solution.py:476
  47.9 2.0 %eval_product.9 = (f32[768,128]{1,0:T(8,128)S(1)}, f32[768,128]{1,0:T(8,128)S(1)}, f32[512,128]{1,0:T(8,128)S(1)}, f32[2048,128]{1,0:T(8,128)S(1)}, bf16[40,224,...) custom-call(f32[824,128]{1,0:T(8,128)S(1)} %get-tuple-element.46.own.refs_0_.refs_7_, ...), custom_call_target="tpu_custom_call" | custom-call | flops 1000000 | bytes 100000 | tf_op jit(solution)/shard_map/eval_product/pallas_call | solution.py:476
  49.9 4.6 %collective-permute-start.15 = (f32[2048,128]{1,0:T(8,128)S(1)}, f32[2048,128]{1,0:T(8,128)S(1)}, u32[]{:S(2)}, u32[]{:S(2)}) collective-permute-start(f32[2048,128]{1,0:T(8,128)S(1)} %get-tuple-element.70.source), channel_id=1, source_target_pairs={{0,1},{1,0},{2,3},{3,2},{4,5},{5,4},{6,7},{7,6},{8,9},{9,8},{10,11... | collective-permute-start | bytes 3145736 | tf_op jit(solution)/shard_map/ppermute | solution.py:530
  54.5 5.1 %collective-permute-start.18 = (f32[768,128]{1,0:T(8,128)S(1)}, f32[768,128]{1,0:T(8,128)S(1)}, u32[]{:S(2)}, u32[]{:S(2)}) collective-permute-start(f32[768,128]{1,0:T(8,128)S(1)} %get-tuple-element.75.refs_1_.refs_11_), channel_id=1, source_target_pairs={{0,2},{2,0},{4,6},{6,4},{8,10},{10,8},{12,14},{14,12},{1,3},{3,1},... | collective-permute-start | bytes 1179656 | tf_op jit(solution)/shard_map/ppermute | solution.py:515
  61.0 4.7 %collective-permute-start.20 = (f32[512,128]{1,0:T(8,128)S(1)}, f32[512,128]{1,0:T(8,128)S(1)}, u32[]{:S(2)}, u32[]{:S(2)}) collective-permute-start(f32[512,128]{1,0:T(8,128)S(1)} %get-tuple-element.76.refs_2_.refs_12_), channel_id=1, source_target_pairs={{0,2},{2,0},{4,6},{6,4},{8,10},{10,8},{12,14},{14,12},{1,3},{3,1},... | collective-permute-start | bytes 786440 | tf_op jit(solution)/shard_map/ppermute | solution.py:515
  65.7 3.1 %product.5.refs_1_ = f32[2048,128]{1,0:T(8,128)S(1)} custom-call(s32[3,168]{1,0:T(4,128)S(1)} %get-tuple-element.72.work, f32[48,128]{1,0:T(8,128)S(1)} %get-tuple-element.73.facts, f32[4,2272,128]{2,1,0:T(8,128)S(1)} %get-tuple-element.47.rows, bf16[40,224,256]{2,1,0:T(8,128)(2,1)S(1)} %get-tuple-element.74.cache, ...), custom_call_target="tpu_custom_call" | custom-call | flops 1000000 | bytes 100000 | tf_op jit(solution)/shard_map/product/pallas_call | solution.py:457
  69.6 5.1 %collective-permute-start.24 = (f32[768,128]{1,0:T(8,128)S(1)}, f32[768,128]{1,0:T(8,128)S(1)}, u32[]{:S(2)}, u32[]{:S(2)}) collective-permute-start(f32[768,128]{1,0:T(8,128)S(1)} %collective-permute-done.18.refs_1_), channel_id=1, source_target_pairs={{6,2},{0,4},{10,6},{4,8},{14,10},{8,12},{7,3},{1,5},{11,7},{5,9},{... | collective-permute-start | bytes 1179656 | tf_op jit(solution)/shard_map/ppermute | solution.py:525
  74.6 2.5 %unsort.2 = f32[2048,128]{1,0:T(8,128)S(1)} custom-call(s32[1,2048]{1,0:T(1,128)S(1)} %get-tuple-element.69.ranks, f32[2048,128]{1,0:T(8,128)S(1)} %get-tuple-element.70.source), custom_call_target="tpu_custom_call" | custom-call | flops 1000000 | bytes 100000 | tf_op jit(solution)/shard_map/unsort/pallas_call | solution.py:502
  77.1 3.0 %product.6.refs_3_ = f32[2048,128]{1,0:T(8,128)S(1)} custom-call(s32[3,168]{1,0:T(4,128)S(1)} %get-tuple-element.65.work, f32[48,128]{1,0:T(8,128)S(1)} %get-tuple-element.66.facts, f32[4,2272,128]{2,1,0:T(8,128)S(1)} %get-tuple-element.47.rows, bf16[40,224,256]{2,1,0:T(8,128)(2,1)S(1)} %get-tuple-element.67.cache, ...), custom_call_target="tpu_custom_call" | custom-call | flops 1000000 | bytes 100000 | tf_op jit(solution)/shard_map/product/pallas_call | solution.py:457
  80.1 3.2 %collective-permute-start.22 = (f32[768,128]{1,0:T(8,128)S(1)}, f32[768,128]{1,0:T(8,128)S(1)}, u32[]{:S(2)}, u32[]{:S(2)}) collective-permute-start(f32[768,128]{1,0:T(8,128)S(1)} %collective-permute-done.14.refs_0_), channel_id=1, source_target_pairs={{6,2},{0,4},{10,6},{4,8},{14,10},{8,12},{7,3},{1,5},{11,7},{5,9},{... | collective-permute-start | bytes 1179656 | tf_op jit(solution)/shard_map/ppermute | solution.py:525
  83.3 1.8 %collective-permute-start.26 = (f32[512,128]{1,0:T(8,128)S(1)}, f32[512,128]{1,0:T(8,128)S(1)}, u32[]{:S(2)}, u32[]{:S(2)}) collective-permute-start(f32[512,128]{1,0:T(8,128)S(1)} %collective-permute-done.16), channel_id=1, source_target_pairs={{0,2},{2,0},{4,6},{6,4},{8,10},{10,8},{12,14},{14,12},{1,3},{3,1},... | collective-permute-start | bytes 786440 | tf_op jit(solution)/shard_map/ppermute | solution.py:515
  85.6 2.9 %product.7.refs_3_ = f32[2048,128]{1,0:T(8,128)S(1)} custom-call(s32[3,168]{1,0:T(4,128)S(1)} %get-tuple-element.78.work, f32[48,128]{1,0:T(8,128)S(1)} %get-tuple-element.79.facts, f32[4,2272,128]{2,1,0:T(8,128)S(1)} %get-tuple-element.47.rows, bf16[40,224,256]{2,1,0:T(8,128)(2,1)S(1)} %get-tuple-element.80.cache, ...), custom_call_target="tpu_custom_call" | custom-call | flops 1000000 | bytes 100000 | tf_op jit(solution)/shard_map/product/pallas_call | solution.py:457
  88.5 1.9 %collective-permute-done.22.refs_0_ = f32[768,128]{1,0:T(8,128)S(1)} collective-permute-done((f32[768,128]{1,0:T(8,128)S(1)}, f32[768,128]{1,0:T(8,128)S(1)}, u32[]{:S(2)}, u32[]{:S(2)}) %collective-permute-start.22) | collective-permute-done | bytes 393248 | tf_op jit(solution)/shard_map/ppermute | solution.py:525
  93.5 1.3 %product.9 = (f32[2048,128]{1,0:T(8,128)S(1)}, f32[8,128]{1,0:T(8,128)S(1)}) custom-call(s32[3,328]{1,0:T(4,128)S(1)} %get-tuple-element.61.work, f32[96,128]{1,0:T(8,128)S(1)} %get-tuple-element.62.facts, f32[4,2272,128]{2,1,0:T(8,128)S(1)} %get-tuple-element.47.rows, bf16[40,224,256]{2,1,0:T(8,128)(2,1)S(1)} %get-tuple-element.63.cache, ...), custom_call_target="tpu_custom_call" | custom-call | flops 1000000 | bytes 100000 | tf_op jit(solution)/shard_map/product/pallas_call | solution.py:457
  94.8 2.4 %collective-permute-start.28 = (f32[8,128]{1,0:T(8,128)S(1)}, f32[8,128]{1,0:T(8,128)S(1)}, u32[]{:S(2)}, u32[]{:S(2)}) collective-permute-start(f32[8,128]{1,0:T(8,128)S(1)} %get-tuple-element.87), channel_id=1, source_target_pairs={{0,1},{1,0},{2,3},{3,2},{4,5},{5,4},{6,7},{7,6},{8,9},{9,8},{10,11... | collective-permute-start | bytes 12296 | tf_op jit(solution)/shard_map/ppermute | solution.py:530
  98.1 3.2 %collective-permute-start.29 = (f32[8,128]{1,0:T(8,128)S(1)}, f32[8,128]{1,0:T(8,128)S(1)}, u32[]{:S(2)}, u32[]{:S(2)}) collective-permute-start(f32[8,128]{1,0:T(8,128)S(1)} %add.36), channel_id=1, source_target_pairs={{0,2},{2,0},{4,6},{6,4},{8,10},{10,8},{12,14},{14,12},{1,3},{3,1},... | collective-permute-start | bytes 12296 | tf_op jit(solution)/shard_map/ppermute | solution.py:539
  101.3 1.6 %collective-permute-done.29 = f32[8,128]{1,0:T(8,128)S(1)} collective-permute-done((f32[8,128]{1,0:T(8,128)S(1)}, f32[8,128]{1,0:T(8,128)S(1)}, u32[]{:S(2)}, u32[]{:S(2)}) %collective-permute-start.29) | collective-permute-done | bytes 4128 | tf_op jit(solution)/shard_map/ppermute | solution.py:539
  102.9 2.4 %collective-permute-start.30 = (f32[8,128]{1,0:T(8,128)S(1)}, f32[8,128]{1,0:T(8,128)S(1)}, u32[]{:S(2)}, u32[]{:S(2)}) collective-permute-start(f32[8,128]{1,0:T(8,128)S(1)} %add.37), channel_id=1, source_target_pairs={{0,4},{2,6},{4,0},{6,2},{8,12},{10,14},{12,8},{14,10},{1,5},{3,7},... | collective-permute-start | bytes 12296 | tf_op jit(solution)/shard_map/ppermute | solution.py:539
  105.3 2.5 %unsort.3 = f32[2048,128]{1,0:T(8,128)S(1)} custom-call(s32[1,2048]{1,0:T(1,128)S(1)} %get-tuple-element.69.ranks, f32[2048,128]{1,0:T(8,128)S(1)} %get-tuple-element.88.source), custom_call_target="tpu_custom_call" | custom-call | flops 1000000 | bytes 100000 | tf_op jit(solution)/shard_map/unsort/pallas_call | solution.py:502
  107.8 3.1 %collective-permute-start.31 = (f32[8,128]{1,0:T(8,128)S(1)}, f32[8,128]{1,0:T(8,128)S(1)}, u32[]{:S(2)}, u32[]{:S(2)}) collective-permute-start(f32[8,128]{1,0:T(8,128)S(1)} %add.38), channel_id=1, source_target_pairs={{0,8},{2,10},{4,12},{6,14},{8,0},{10,2},{12,4},{14,6},{1,9},{3,11}... | collective-permute-start | bytes 12296 | tf_op jit(solution)/shard_map/ppermute | solution.py:539
  110.8 1.6 %collective-permute-done.31 = f32[8,128]{1,0:T(8,128)S(1)} collective-permute-done((f32[8,128]{1,0:T(8,128)S(1)}, f32[8,128]{1,0:T(8,128)S(1)}, u32[]{:S(2)}, u32[]{:S(2)}) %collective-permute-start.31) | collective-permute-done | bytes 4128 | tf_op jit(solution)/shard_map/ppermute | solution.py:539
  112.4 1.8 %multiply_subtract_fusion = (f32[2048,128]{1,0:T(8,128)}, f32[2048,128]{1,0:T(8,128)}) fusion(f32[2048,128]{1,0:T(8,128)S(1)} %unsort.2, f32[2048,128]{1,0:T(8,128)S(1)} %unsort.3, f32[2048,128]{1,0:T(8,128)S(1)} %copy-done, f32[128]{0:T(128)S(1)} %bitcast.7, f32[128]{0:T(128)S(1)} %get-tuple-element.90, f32[128]{0:T(128)S(1)} %bitcast.6), kind=kLoop, calls=%fused_computation | loop fusion | flops 3407872 | bytes 5244416 | tf_op jit(solution)/shard_map/sub | solution.py:606
  (54 shorter events, 8.9 us)
Async XLA Ops:
  9.0 18.3 %collective-permute-start.4 = (f32[2104,128]{1,0:T(8,128)S(1)}, f32[2104,128]{1,0:T(8,128)S(1)}, u32[]{:S(2)}, u32[]{:S(2)}) collective-permute-start(f32[2104,128]{1,0:T(8,128)S(1)} %get-tuple-element.52), channel_id=1, source_target_pairs={{0,1},{1,0},{2,3},{3,2},{4,5},{5,4},{6,7},{7,6},{8,9},{9,8},{10,11... | collective-permute-start | bytes 3231752 | tf_op jit(solution)/shard_map/ppermute | solution.py:530
  9.5 14.3 %collective-permute-start = (f32[824,128]{1,0:T(8,128)S(1)}, f32[824,128]{1,0:T(8,128)S(1)}, u32[]{:S(2)}, u32[]{:S(2)}) collective-permute-start(f32[824,128]{1,0:T(8,128)S(1)} %get-tuple-element.46.own.refs_0_.refs_7_), channel_id=1, source_target_pairs={{0,2},{2,0},{4,6},{6,4},{8,10},{10,8},{12,14},{14,12},{1,3},{3,1},... | collective-permute-start | bytes 1265672 | tf_op jit(solution)/shard_map/ppermute | solution.py:515
  12.1 21.3 %collective-permute-start.3 = (f32[768,128]{1,0:T(8,128)S(1)}, f32[768,128]{1,0:T(8,128)S(1)}, u32[]{:S(2)}, u32[]{:S(2)}) collective-permute-start(f32[768,128]{1,0:T(8,128)S(1)} %get-tuple-element.48.refs_1_.refs_8_), channel_id=1, source_target_pairs={{0,2},{2,0},{4,6},{6,4},{8,10},{10,8},{12,14},{14,12},{1,3},{3,1},... | collective-permute-start | bytes 1179656 | tf_op jit(solution)/shard_map/ppermute | solution.py:515
  12.2 11.6 %collective-permute-start.1 = (f32[512,128]{1,0:T(8,128)S(1)}, f32[512,128]{1,0:T(8,128)S(1)}, u32[]{:S(2)}, u32[]{:S(2)}) collective-permute-start(f32[512,128]{1,0:T(8,128)S(1)} %get-tuple-element.49.refs_2_.refs_9_), channel_id=1, source_target_pairs={{4,0},{8,4},{2,6},{12,8},{6,10},{10,14},{5,1},{9,5},{3,7},{13,9},{... | collective-permute-start | bytes 786440 | tf_op jit(solution)/shard_map/ppermute | solution.py:525
  13.5 23.4 %collective-permute-start.6 = (f32[512,128]{1,0:T(8,128)S(1)}, f32[512,128]{1,0:T(8,128)S(1)}, u32[]{:S(2)}, u32[]{:S(2)}) collective-permute-start(f32[512,128]{1,0:T(8,128)S(1)} %get-tuple-element.49.refs_2_.refs_9_), channel_id=1, source_target_pairs={{0,2},{2,0},{4,6},{6,4},{8,10},{10,8},{12,14},{14,12},{1,3},{3,1},... | collective-permute-start | bytes 786440 | tf_op jit(solution)/shard_map/ppermute | solution.py:515
  23.8 14.9 %collective-permute-start.8 = (f32[824,128]{1,0:T(8,128)S(1)}, f32[824,128]{1,0:T(8,128)S(1)}, u32[]{:S(2)}, u32[]{:S(2)}) collective-permute-start(f32[824,128]{1,0:T(8,128)S(1)} %collective-permute-done.refs_0_), channel_id=1, source_target_pairs={{6,2},{0,4},{10,6},{4,8},{14,10},{8,12},{7,3},{1,5},{11,7},{5,9},{... | collective-permute-start | bytes 1265672 | tf_op jit(solution)/shard_map/ppermute | solution.py:525
  33.4 11.4 %collective-permute-start.10 = (f32[768,128]{1,0:T(8,128)S(1)}, f32[768,128]{1,0:T(8,128)S(1)}, u32[]{:S(2)}, u32[]{:S(2)}) collective-permute-start(f32[768,128]{1,0:T(8,128)S(1)} %collective-permute-done.3.refs_1_), channel_id=1, source_target_pairs={{6,2},{0,4},{10,6},{4,8},{14,10},{8,12},{7,3},{1,5},{11,7},{5,9},{... | collective-permute-start | bytes 1179656 | tf_op jit(solution)/shard_map/ppermute | solution.py:525
  36.9 8.5 %collective-permute-start.12 = (f32[512,128]{1,0:T(8,128)S(1)}, f32[512,128]{1,0:T(8,128)S(1)}, u32[]{:S(2)}, u32[]{:S(2)}) collective-permute-start(f32[512,128]{1,0:T(8,128)S(1)} %collective-permute-done.1), channel_id=1, source_target_pairs={{0,2},{2,0},{4,6},{6,4},{8,10},{10,8},{12,14},{14,12},{1,3},{3,1},... | collective-permute-start | bytes 786440 | tf_op jit(solution)/shard_map/ppermute | solution.py:515
  38.2 7.3 %collective-permute-start.7 = (f32[512,128]{1,0:T(8,128)S(1)}, f32[512,128]{1,0:T(8,128)S(1)}, u32[]{:S(2)}, u32[]{:S(2)}) collective-permute-start(f32[512,128]{1,0:T(8,128)S(1)} %collective-permute-done.6.refs_2_), channel_id=1, source_target_pairs={{0,1},{1,0},{2,3},{3,2},{4,5},{5,4},{6,7},{7,6},{8,9},{9,8},{10,11... | collective-permute-start | bytes 786440 | tf_op jit(solution)/shard_map/ppermute | solution.py:530
  38.2 9.6 %collective-permute-start.2 = (f32[824,128]{1,0:T(8,128)S(1)}, f32[824,128]{1,0:T(8,128)S(1)}, u32[]{:S(2)}, u32[]{:S(2)}) collective-permute-start(f32[824,128]{1,0:T(8,128)S(1)} %collective-permute-done.refs_0_), channel_id=1, source_target_pairs={{0,1},{1,0},{2,3},{3,2},{4,5},{5,4},{6,7},{7,6},{8,9},{9,8},{10,11... | collective-permute-start | bytes 1265672 | tf_op jit(solution)/shard_map/ppermute | solution.py:530
  38.8 9.1 %collective-permute-start.9 = (f32[824,128]{1,0:T(8,128)S(1)}, f32[824,128]{1,0:T(8,128)S(1)}, u32[]{:S(2)}, u32[]{:S(2)}) collective-permute-start(f32[824,128]{1,0:T(8,128)S(1)} %collective-permute-done.8.refs_0_), channel_id=1, source_target_pairs={{0,1},{1,0},{2,3},{3,2},{4,5},{5,4},{6,7},{7,6},{8,9},{9,8},{10,11... | collective-permute-start | bytes 1265672 | tf_op jit(solution)/shard_map/ppermute | solution.py:530
  44.9 3.0 %collective-permute-start.5 = (f32[768,128]{1,0:T(8,128)S(1)}, f32[768,128]{1,0:T(8,128)S(1)}, u32[]{:S(2)}, u32[]{:S(2)}) collective-permute-start(f32[768,128]{1,0:T(8,128)S(1)} %collective-permute-done.3.refs_1_), channel_id=1, source_target_pairs={{0,1},{1,0},{2,3},{3,2},{4,5},{5,4},{6,7},{7,6},{8,9},{9,8},{10,11... | collective-permute-start | bytes 1179656 | tf_op jit(solution)/shard_map/ppermute | solution.py:530
  45.4 2.5 %collective-permute-start.11 = (f32[768,128]{1,0:T(8,128)S(1)}, f32[768,128]{1,0:T(8,128)S(1)}, u32[]{:S(2)}, u32[]{:S(2)}) collective-permute-start(f32[768,128]{1,0:T(8,128)S(1)} %collective-permute-done.10.refs_1_), channel_id=1, source_target_pairs={{0,1},{1,0},{2,3},{3,2},{4,5},{5,4},{6,7},{7,6},{8,9},{9,8},{10,11... | collective-permute-start | bytes 1179656 | tf_op jit(solution)/shard_map/ppermute | solution.py:530
  45.5 2.4 %collective-permute-start.13 = (f32[512,128]{1,0:T(8,128)S(1)}, f32[512,128]{1,0:T(8,128)S(1)}, u32[]{:S(2)}, u32[]{:S(2)}) collective-permute-start(f32[512,128]{1,0:T(8,128)S(1)} %collective-permute-done.12.refs_2_), channel_id=1, source_target_pairs={{0,1},{1,0},{2,3},{3,2},{4,5},{5,4},{6,7},{7,6},{8,9},{9,8},{10,11... | collective-permute-start | bytes 786440 | tf_op jit(solution)/shard_map/ppermute | solution.py:530
  49.9 24.7 %collective-permute-start.15 = (f32[2048,128]{1,0:T(8,128)S(1)}, f32[2048,128]{1,0:T(8,128)S(1)}, u32[]{:S(2)}, u32[]{:S(2)}) collective-permute-start(f32[2048,128]{1,0:T(8,128)S(1)} %get-tuple-element.70.source), channel_id=1, source_target_pairs={{0,1},{1,0},{2,3},{3,2},{4,5},{5,4},{6,7},{7,6},{8,9},{9,8},{10,11... | collective-permute-start | bytes 3145736 | tf_op jit(solution)/shard_map/ppermute | solution.py:530
  54.5 15.0 %collective-permute-start.18 = (f32[768,128]{1,0:T(8,128)S(1)}, f32[768,128]{1,0:T(8,128)S(1)}, u32[]{:S(2)}, u32[]{:S(2)}) collective-permute-start(f32[768,128]{1,0:T(8,128)S(1)} %get-tuple-element.75.refs_1_.refs_11_), channel_id=1, source_target_pairs={{0,2},{2,0},{4,6},{6,4},{8,10},{10,8},{12,14},{14,12},{1,3},{3,1},... | collective-permute-start | bytes 1179656 | tf_op jit(solution)/shard_map/ppermute | solution.py:515
  59.6 20.5 %collective-permute-start.14 = (f32[768,128]{1,0:T(8,128)S(1)}, f32[768,128]{1,0:T(8,128)S(1)}, u32[]{:S(2)}, u32[]{:S(2)}) collective-permute-start(f32[768,128]{1,0:T(8,128)S(1)} %get-tuple-element.64.refs_0_.refs_10_), channel_id=1, source_target_pairs={{0,2},{2,0},{4,6},{6,4},{8,10},{10,8},{12,14},{14,12},{1,3},{3,1},... | collective-permute-start | bytes 1179656 | tf_op jit(solution)/shard_map/ppermute | solution.py:515
  59.7 20.4 %collective-permute-start.16 = (f32[512,128]{1,0:T(8,128)S(1)}, f32[512,128]{1,0:T(8,128)S(1)}, u32[]{:S(2)}, u32[]{:S(2)}) collective-permute-start(f32[512,128]{1,0:T(8,128)S(1)} %get-tuple-element.76.refs_2_.refs_12_), channel_id=1, source_target_pairs={{4,0},{8,4},{2,6},{12,8},{6,10},{10,14},{5,1},{9,5},{3,7},{13,9},{... | collective-permute-start | bytes 786440 | tf_op jit(solution)/shard_map/ppermute | solution.py:525
  61.0 22.4 %collective-permute-start.20 = (f32[512,128]{1,0:T(8,128)S(1)}, f32[512,128]{1,0:T(8,128)S(1)}, u32[]{:S(2)}, u32[]{:S(2)}) collective-permute-start(f32[512,128]{1,0:T(8,128)S(1)} %get-tuple-element.76.refs_2_.refs_12_), channel_id=1, source_target_pairs={{0,2},{2,0},{4,6},{6,4},{8,10},{10,8},{12,14},{14,12},{1,3},{3,1},... | collective-permute-start | bytes 786440 | tf_op jit(solution)/shard_map/ppermute | solution.py:515
  69.6 16.1 %collective-permute-start.24 = (f32[768,128]{1,0:T(8,128)S(1)}, f32[768,128]{1,0:T(8,128)S(1)}, u32[]{:S(2)}, u32[]{:S(2)}) collective-permute-start(f32[768,128]{1,0:T(8,128)S(1)} %collective-permute-done.18.refs_1_), channel_id=1, source_target_pairs={{6,2},{0,4},{10,6},{4,8},{14,10},{8,12},{7,3},{1,5},{11,7},{5,9},{... | collective-permute-start | bytes 1179656 | tf_op jit(solution)/shard_map/ppermute | solution.py:525
  80.1 10.4 %collective-permute-start.22 = (f32[768,128]{1,0:T(8,128)S(1)}, f32[768,128]{1,0:T(8,128)S(1)}, u32[]{:S(2)}, u32[]{:S(2)}) collective-permute-start(f32[768,128]{1,0:T(8,128)S(1)} %collective-permute-done.14.refs_0_), channel_id=1, source_target_pairs={{6,2},{0,4},{10,6},{4,8},{14,10},{8,12},{7,3},{1,5},{11,7},{5,9},{... | collective-permute-start | bytes 1179656 | tf_op jit(solution)/shard_map/ppermute | solution.py:525
  83.3 8.1 %collective-permute-start.26 = (f32[512,128]{1,0:T(8,128)S(1)}, f32[512,128]{1,0:T(8,128)S(1)}, u32[]{:S(2)}, u32[]{:S(2)}) collective-permute-start(f32[512,128]{1,0:T(8,128)S(1)} %collective-permute-done.16), channel_id=1, source_target_pairs={{0,2},{2,0},{4,6},{6,4},{8,10},{10,8},{12,14},{14,12},{1,3},{3,1},... | collective-permute-start | bytes 786440 | tf_op jit(solution)/shard_map/ppermute | solution.py:515
  85.1 6.3 %collective-permute-start.21 = (f32[512,128]{1,0:T(8,128)S(1)}, f32[512,128]{1,0:T(8,128)S(1)}, u32[]{:S(2)}, u32[]{:S(2)}) collective-permute-start(f32[512,128]{1,0:T(8,128)S(1)} %collective-permute-done.20.refs_2_), channel_id=1, source_target_pairs={{0,1},{1,0},{2,3},{3,2},{4,5},{5,4},{6,7},{7,6},{8,9},{9,8},{10,11... | collective-permute-start | bytes 786440 | tf_op jit(solution)/shard_map/ppermute | solution.py:530
  85.1 7.7 %collective-permute-start.19 = (f32[768,128]{1,0:T(8,128)S(1)}, f32[768,128]{1,0:T(8,128)S(1)}, u32[]{:S(2)}, u32[]{:S(2)}) collective-permute-start(f32[768,128]{1,0:T(8,128)S(1)} %collective-permute-done.18.refs_1_), channel_id=1, source_target_pairs={{0,1},{1,0},{2,3},{3,2},{4,5},{5,4},{6,7},{7,6},{8,9},{9,8},{10,11... | collective-permute-start | bytes 1179656 | tf_op jit(solution)/shard_map/ppermute | solution.py:530
  85.6 7.2 %collective-permute-start.25 = (f32[768,128]{1,0:T(8,128)S(1)}, f32[768,128]{1,0:T(8,128)S(1)}, u32[]{:S(2)}, u32[]{:S(2)}) collective-permute-start(f32[768,128]{1,0:T(8,128)S(1)} %collective-permute-done.24.refs_1_), channel_id=1, source_target_pairs={{0,1},{1,0},{2,3},{3,2},{4,5},{5,4},{6,7},{7,6},{8,9},{9,8},{10,11... | collective-permute-start | bytes 1179656 | tf_op jit(solution)/shard_map/ppermute | solution.py:530
  90.5 2.4 %collective-permute-start.17 = (f32[768,128]{1,0:T(8,128)S(1)}, f32[768,128]{1,0:T(8,128)S(1)}, u32[]{:S(2)}, u32[]{:S(2)}) collective-permute-start(f32[768,128]{1,0:T(8,128)S(1)} %collective-permute-done.14.refs_0_), channel_id=1, source_target_pairs={{0,1},{1,0},{2,3},{3,2},{4,5},{5,4},{6,7},{7,6},{8,9},{9,8},{10,11... | collective-permute-start | bytes 1179656 | tf_op jit(solution)/shard_map/ppermute | solution.py:530
  91.4 2.1 %collective-permute-start.23 = (f32[768,128]{1,0:T(8,128)S(1)}, f32[768,128]{1,0:T(8,128)S(1)}, u32[]{:S(2)}, u32[]{:S(2)}) collective-permute-start(f32[768,128]{1,0:T(8,128)S(1)} %collective-permute-done.22.refs_0_), channel_id=1, source_target_pairs={{0,1},{1,0},{2,3},{3,2},{4,5},{5,4},{6,7},{7,6},{8,9},{9,8},{10,11... | collective-permute-start | bytes 1179656 | tf_op jit(solution)/shard_map/ppermute | solution.py:530
  91.4 2.1 %collective-permute-start.27 = (f32[512,128]{1,0:T(8,128)S(1)}, f32[512,128]{1,0:T(8,128)S(1)}, u32[]{:S(2)}, u32[]{:S(2)}) collective-permute-start(f32[512,128]{1,0:T(8,128)S(1)} %collective-permute-done.26.refs_2_), channel_id=1, source_target_pairs={{0,1},{1,0},{2,3},{3,2},{4,5},{5,4},{6,7},{7,6},{8,9},{9,8},{10,11... | collective-permute-start | bytes 786440 | tf_op jit(solution)/shard_map/ppermute | solution.py:530
  94.8 3.2 %collective-permute-start.28 = (f32[8,128]{1,0:T(8,128)S(1)}, f32[8,128]{1,0:T(8,128)S(1)}, u32[]{:S(2)}, u32[]{:S(2)}) collective-permute-start(f32[8,128]{1,0:T(8,128)S(1)} %get-tuple-element.87), channel_id=1, source_target_pairs={{0,1},{1,0},{2,3},{3,2},{4,5},{5,4},{6,7},{7,6},{8,9},{9,8},{10,11... | collective-permute-start | bytes 12296 | tf_op jit(solution)/shard_map/ppermute | solution.py:530
  98.1 4.8 %collective-permute-start.29 = (f32[8,128]{1,0:T(8,128)S(1)}, f32[8,128]{1,0:T(8,128)S(1)}, u32[]{:S(2)}, u32[]{:S(2)}) collective-permute-start(f32[8,128]{1,0:T(8,128)S(1)} %add.36), channel_id=1, source_target_pairs={{0,2},{2,0},{4,6},{6,4},{8,10},{10,8},{12,14},{14,12},{1,3},{3,1},... | collective-permute-start | bytes 12296 | tf_op jit(solution)/shard_map/ppermute | solution.py:539
  102.9 4.9 %collective-permute-start.30 = (f32[8,128]{1,0:T(8,128)S(1)}, f32[8,128]{1,0:T(8,128)S(1)}, u32[]{:S(2)}, u32[]{:S(2)}) collective-permute-start(f32[8,128]{1,0:T(8,128)S(1)} %add.37), channel_id=1, source_target_pairs={{0,4},{2,6},{4,0},{6,2},{8,12},{10,14},{12,8},{14,10},{1,5},{3,7},... | collective-permute-start | bytes 12296 | tf_op jit(solution)/shard_map/ppermute | solution.py:539
  107.8 4.6 %collective-permute-start.31 = (f32[8,128]{1,0:T(8,128)S(1)}, f32[8,128]{1,0:T(8,128)S(1)}, u32[]{:S(2)}, u32[]{:S(2)}) collective-permute-start(f32[8,128]{1,0:T(8,128)S(1)} %add.38), channel_id=1, source_target_pairs={{0,8},{2,10},{4,12},{6,14},{8,0},{10,2},{12,4},{14,6},{1,9},{3,11}... | collective-permute-start | bytes 12296 | tf_op jit(solution)/shard_map/ppermute | solution.py:539
  (1 other events, 18.9 us)
